TPU v7x, 128 devices: a whole 4x4x4 slice. The times are simulated.
128 devices in a mesh: lon: 8 (over y, x_hi), lat: 16 (over x_lo, z, core).
Axes of the slice: x: 4 (x_hi: 2, x_lo: 2; x = x_hi * 2 + x_lo), y: 4, z: 4, core: 2. Of those that a mesh axis runs over, the one named last changes fastest.
Arguments:
- tokens: bfloat16 [4, 192, 384, 192], P(None, 'lat', 'lon'), may hold values from -6 to 6
- cotangent: bfloat16 [4, 192, 384, 192], P(None, 'lat', 'lon'), may hold values from -6 to 6
- region_ids: int32 [192], P('lat'), may hold values from 0 to 47, never falling along the last dimension, each value on 1 to 12 neighbouring positions
- norm_gains: float32 [2, 192], replicated, may hold values from 0.5 to 1.5
- w_qkv: bfloat16 [192, 576], replicated, may hold values from -0.4375 to 0.4375
- w_proj: bfloat16 [192, 192], replicated, may hold values from -0.4375 to 0.4375
- w_up: bfloat16 [192, 768], replicated, may hold values from -0.4375 to 0.4375
- w_down: bfloat16 [768, 192], replicated, may hold values from -0.21875 to 0.21875
- earth_bias: float32 [2, 32, 6, 144, 144], P(None, 'lat'), may hold values from -2 to 250
Outputs:
- grad_tokens: bfloat16 [4, 192, 384, 192], P(None, 'lat', 'lon')
- grad_qkv: float32 [192, 576], replicated
- grad_proj: float32 [192, 192], replicated
- grad_up: float32 [192, 768], replicated
- grad_down: float32 [768, 192], replicated
- grad_gains: float32 [2, 192], replicated
- grad_bias: float32 [2, 32, 6, 144, 144], P(None, 'lat', None, 'lon')
Inputs may be any that keep to these rules, and one draw needn't show every extreme that they name: `region_ids`: never falls from one latitude row to the next; a run of equal ids spans 1 to 12 rows.
All inputs are finite; a program needn't handle non-finite values.
Results may differ from a plain program's by a relative error of at most 0.015.
Values may be sent and summed in bfloat16 or wider, within the bound.
No kernel may reach another device: no remote copies, remote signals or barrier semaphores. Data moves between devices by JAX's collectives and lax.ppermute only.
A program may use at most 192 MiB of HBM per device.

v0:
```python
import math

import jax
import jax.numpy as jnp
import numpy as np
from jax import lax
from jax.sharding import PartitionSpec as P

HEADS = 6
WLEV = 2
WLAT = 6
WLON = 12


epsilon = 1e-05
inv_root_two = 0.7071067811865476
inv_root_tau = 0.3989422804014327


def from_behind(value, axis, steps):
    count = lax.axis_size(axis)
    pairs = [(source, (source + steps) % count) for source in range(count)]
    return lax.ppermute(value, axis, pairs)


def mult(form, left, right):
    return jnp.einsum(form, left, right, preferred_element_type=jnp.float32)


def contract_rows(left, right):
    return lax.dot_general(
        left, right, (((0,), (0,)), ((), ())), preferred_element_type=jnp.float32
    )


def contract_cols(left, right):
    return lax.dot_general(
        left, right, (((1,), (1,)), ((), ())), preferred_element_type=jnp.float32
    )


def normalize(values):
    centred = values - jnp.mean(values, axis=-1, keepdims=True)
    inverse = lax.rsqrt(jnp.mean(centred * centred, axis=-1, keepdims=True) + epsilon)
    return (centred * inverse, inverse)


def norm_back(normed, inverse, gain_row, upstream):
    scaled = upstream * gain_row
    return inverse * (
        scaled
        - jnp.mean(scaled, axis=-1, keepdims=True)
        - normed * jnp.mean(scaled * normed, axis=-1, keepdims=True)
    )


def to_windows(layer_in):
    levels, row_count, col_count, channels = layer_in.shape
    grouped = layer_in.reshape(
        levels // WLEV, WLEV, row_count // WLAT, WLAT, col_count // WLON, WLON, channels
    )
    return grouped.transpose(0, 2, 4, 1, 3, 5, 6).reshape(
        levels // WLEV, row_count // WLAT, col_count // WLON, WLEV * WLAT * WLON, channels
    )


def from_windows(windows, levels, row_count, col_count):
    channels = windows.shape[-1]
    grouped = windows.reshape(
        levels // WLEV, row_count // WLAT, col_count // WLON, WLEV, WLAT, WLON, channels
    )
    return grouped.transpose(0, 3, 1, 4, 2, 5, 6).reshape(levels, row_count, col_count, channels)


def region_mask(row_ids):
    lookup = np.arange(WLEV * WLAT * WLON) // WLON % WLAT
    per_token = row_ids.reshape(-1, WLAT)[:, lookup]
    return per_token[:, :, None] == per_token[:, None, :]


def shift_ahead(layer_in, row_ids):
    half_lat = WLAT // 2
    half_lon = WLON // 2
    incoming_rows, incoming_ids = from_behind(
        (layer_in[:, :half_lat], row_ids[:half_lat]), "lat", -1
    )
    layer_in = jnp.concatenate([layer_in[:, half_lat:], incoming_rows], axis=1)
    row_ids = jnp.concatenate([row_ids[half_lat:], incoming_ids], axis=0)
    incoming_cols = from_behind(layer_in[:, :, :half_lon], "lon", -1)
    return (jnp.concatenate([layer_in[:, :, half_lon:], incoming_cols], axis=2), row_ids)


def shift_behind(layer_in):
    half_lat = WLAT // 2
    half_lon = WLON // 2
    incoming_rows = from_behind(layer_in[:, -half_lat:], "lat", 1)
    layer_in = jnp.concatenate([incoming_rows, layer_in[:, :-half_lat]], axis=1)
    incoming_cols = from_behind(layer_in[:, :, -half_lon:], "lon", 1)
    return jnp.concatenate([incoming_cols, layer_in[:, :, :-half_lon]], axis=2)


def attend_forward(shifted, allowed, bias, w_qkv, w_proj, scaling):
    levels, row_count, col_count, channels = shifted.shape
    head_size = channels // HEADS
    windows = to_windows(shifted)
    mixed = mult("abnmc,cd->abnmd", windows, w_qkv)
    mixed = mixed.reshape(mixed.shape[:4] + (3, HEADS, head_size))
    queries = (mixed[..., 0, :, :] * scaling).astype(jnp.bfloat16)
    keys_low = mixed[..., 1, :, :].astype(jnp.bfloat16)
    values = mixed[..., 2, :, :].astype(jnp.bfloat16)
    scores = mult("abnmhd,abnkhd->abnhmk", queries, keys_low) + bias[:, :, None]
    scores = jnp.where(allowed[None, :, None, None], scores, -1e30)
    largest = jnp.max(scores, axis=-1, keepdims=True)
    powers = jnp.exp(scores - largest)
    weights = powers / jnp.sum(powers, axis=-1, keepdims=True)
    rounded = weights.astype(jnp.bfloat16)
    merged = (
        mult("abnhmk,abnkhd->abnmhd", rounded, values).astype(jnp.bfloat16).reshape(windows.shape)
    )
    projected = mult("abnmc,ce->abnme", merged, w_proj).astype(jnp.bfloat16)
    attended = from_windows(projected, levels, row_count, col_count)
    return (attended, (windows, queries, keys_low, values, weights, rounded, merged))


def attend_backward(saved, upstream, w_qkv, w_proj, scaling):
    windows, queries, keys_low, values, weights, rounded, merged = saved
    levels, row_count, col_count, channels = upstream.shape
    grad_windows = to_windows(upstream)
    grad_proj = mult("abnmc,abnme->ce", merged, grad_windows)
    grad_merged = (
        mult("abnme,ce->abnmc", grad_windows, w_proj).astype(jnp.bfloat16).reshape(queries.shape)
    )
    grad_values = mult("abnhmk,abnmhd->abnkhd", rounded, grad_merged)
    grad_weights = mult("abnmhd,abnkhd->abnhmk", grad_merged, values)
    grad_scores = weights * (grad_weights - jnp.sum(weights * grad_weights, axis=-1, keepdims=True))
    grad_bias = jnp.sum(grad_scores, axis=2)
    scores_low = grad_scores.astype(jnp.bfloat16)
    grad_queries = mult("abnhmk,abnkhd->abnmhd", scores_low, keys_low) * scaling
    grad_keys = mult("abnhmk,abnmhd->abnkhd", scores_low, queries)
    grad_mixed = jnp.stack([grad_queries, grad_keys, grad_values], axis=4).astype(jnp.bfloat16)
    grad_mixed = grad_mixed.reshape(windows.shape[:4] + (3 * channels,))
    grad_qkv = mult("abnmc,abnmd->cd", windows, grad_mixed)
    grad_shifted = mult("abnmd,cd->abnmc", grad_mixed, w_qkv).astype(jnp.bfloat16)
    return (
        from_windows(grad_shifted, levels, row_count, col_count),
        grad_qkv,
        grad_proj,
        grad_bias,
    )


def feed_forward(tokens, attended, upstream, gain_row, w_up, w_down):
    shape_in = tokens.shape
    channels = shape_in[-1]
    residual = tokens.astype(jnp.float32).reshape(-1, channels) + attended.astype(
        jnp.float32
    ).reshape(-1, channels)
    normed, inverse = normalize(residual)
    inner_in = (normed * gain_row).astype(jnp.bfloat16)
    hidden = jnp.dot(inner_in, w_up, preferred_element_type=jnp.float32)
    normal_cdf = 0.5 * (1.0 + jax.scipy.special.erf(hidden * inv_root_two))
    activated = (hidden * normal_cdf).astype(jnp.bfloat16)
    grad_out = upstream.reshape(-1, channels)
    grad_down = contract_rows(activated, grad_out)
    grad_act = contract_cols(grad_out, w_down)
    derivative = normal_cdf + hidden * jnp.exp(-0.5 * hidden * hidden) * inv_root_tau
    grad_hidden = (grad_act * derivative).astype(jnp.bfloat16)
    grad_up = contract_rows(inner_in, grad_hidden)
    grad_inner = contract_cols(grad_hidden, w_up)
    second_gain = jnp.sum(grad_inner * normed, axis=0)
    grad_resid = grad_out.astype(jnp.float32) + norm_back(normed, inverse, gain_row, grad_inner)
    return (grad_resid.reshape(shape_in), grad_up, grad_down, second_gain)


def local(tokens, cotangent, region_ids, norm_gains, w_qkv, w_proj, w_up, w_down, earth_bias):
    channels = tokens.shape[-1]
    scaling = float(channels // HEADS) ** (-0.5)
    tokens_here, upstream_here, rows_here = (tokens, cotangent, region_ids)
    normed, inverse = normalize(tokens_here.astype(jnp.float32))
    lowered = (normed * norm_gains[0]).astype(jnp.bfloat16)
    shifted, rows_shifted = shift_ahead(lowered, rows_here)
    attended_shifted, saved = attend_forward(
        shifted, region_mask(rows_shifted), earth_bias, w_qkv, w_proj, scaling
    )
    attended = shift_behind(attended_shifted)
    attended = lax.optimization_barrier(attended)
    grad_resid, grad_up, grad_down, second_gain = feed_forward(
        tokens_here, attended, upstream_here, norm_gains[1], w_up, w_down
    )
    grad_lowered = grad_resid.astype(jnp.bfloat16)
    grad_shifted, unused_rows = shift_ahead(grad_lowered, rows_here)
    grad_back, grad_qkv, grad_proj, grad_bias = attend_backward(
        saved, grad_shifted, w_qkv, w_proj, scaling
    )
    bias_total = lax.psum_scatter(
        grad_bias.astype(jnp.bfloat16), "lon", scatter_dimension=3, tiled=True
    ).astype(jnp.float32)
    grad_normed = shift_behind(grad_back)
    grad_normed = lax.optimization_barrier(grad_normed)
    back_float = grad_normed.astype(jnp.float32)
    grad_here = (grad_resid + norm_back(normed, inverse, norm_gains[0], back_float)).astype(
        jnp.bfloat16
    )
    first_gain = jnp.sum(back_float * normed, axis=(0, 1, 2))
    grad_qkv, grad_proj, grad_up, grad_down, first_gain, second_gain = lax.psum(
        (grad_qkv, grad_proj, grad_up, grad_down, first_gain, second_gain), ("lon", "lat")
    )
    cell_count = (
        tokens.shape[0]
        * tokens.shape[1]
        * tokens.shape[2]
        * lax.axis_size("lon")
        * lax.axis_size("lat")
    )
    rescale = 1.0 / math.sqrt(cell_count)
    grad_gains = jnp.stack([first_gain, second_gain]) * rescale
    return (
        grad_here,
        grad_qkv * rescale,
        grad_proj * rescale,
        grad_up * rescale,
        grad_down * rescale,
        grad_gains,
        bias_total,
    )


def solution(mesh):
    placed = (
        P(None, "lat", "lon", None),
        P(None, "lat", "lon", None),
        P("lat"),
        P(),
        P(),
        P(),
        P(),
        P(),
        P(None, "lat", None, None, None),
    )
    return jax.shard_map(
        local,
        mesh=mesh,
        in_specs=placed,
        out_specs=(
            P(None, "lat", "lon", None),
            P(),
            P(),
            P(),
            P(),
            P(),
            P(None, "lat", None, "lon", None),
        ),
        check_vma=False,
    )
```

profile of v0, /device:TPU:1, one launch (start us, length us, event | category | flops | bytes accessed | tf_op | source)
XLA Modules:
  0.0 375.3 jit_solution(16942103583544769517)
XLA Ops:
  8.1 1.5 collective-permute-start.2
  10.3 2.3 convert_reduce_fusion
  12.7 1.8 fusion.31
  14.6 1.6 fusion.26
  17.0 4.5 %collective-permute-start = (bf16[4,3,48,192]{3,0,2,1:T(4,128)(2,1)}, bf16[4,3,48,192]{3,0,2,1:T(4,128)(2,1)S(1)}, u32[]{:S(2)}, u32[]{:S(2)}) collective-permute-start(bf16[4,3,48,192]{3,0,2,1:T(4,128)(2,1)} %slice.98), channel_id=1, source_target_pairs={{0,15},{1,0},{2,1},{3,2},{4,3},{5,4},{6,5},{7,6},{8,7},{9,8},{10,9... | collective-permute-start | bytes 663560 | tf_op jit(solution)/shard_map/ppermute | solution.py:23
  22.1 5.6 %copy.117 = f32[2,2,6,144,144]{3,4,2,1,0:T(8,128)} copy(f32[2,2,6,144,144]{4,3,2,1,0:T(8,128)} %param.19) | data formatting | bytes 3981312 | tf_op args[8]
  29.0 5.0 %collective-permute-start.1 = (bf16[4,12,6,192]{3,0,2,1:T(4,128)(2,1)S(1)}, bf16[4,12,6,192]{3,0,2,1:T(4,128)(2,1)S(1)}, u32[]{:S(2)}, u32[]{:S(2)}) collective-permute-start(bf16[4,12,6,192]{3,0,2,1:T(4,128)(2,1)S(1)} %pad_maximum_fusion.8), channel_id=1, source_target_pairs={{0,112},{16,0},{32,16},{48,32},{64,48},{80,64},{96,80},{112,96},{1... | collective-permute-start | bytes 331784 | tf_op jit(solution)/shard_map/ppermute | solution.py:23
  34.7 1.8 collective-permute-done.1
  37.3 1.9 reshape.135
  39.2 1.9 copy.111
  41.1 1.4 fusion.68
  42.5 3.7 copy-done.3
  46.2 1.3 copy-done.6
  47.5 7.2 %fusion.47 = f32[2,2,4,6,144,144]{4,5,3,2,1,0:T(8,128)} fusion(bf16[2,2,4,144,3,6,32]{3,6,5,4,2,1,0:T(8,128)(2,1)S(1)} %get-tuple-element.46, f32[2,2,4,144,3,6,32]{3,6,5,4,2,1,0:T(8,128)S(1)} %get-tuple-element.47), kind=kOutput, calls=%fused_computation.71 | convolution fusion | flops 128286720 | bytes 12681216 | tf_op jit(solution)/shard_map/abnmhd,abnkhd->abnhmk/dot_general | solution.py:27
  54.6 19.2 %fusion.69 = (f32[2,2,4,6,144]{4,3,2,1,0:T(8,128)S(1)}, f32[2,2,4,6,144,144]{4,5,3,2,1,0:T(8,128)}) fusion(f32[2,2,4,6,144,144]{4,5,3,2,1,0:T(8,128)} %fusion.47, f32[2,2,6,144,144]{3,4,2,1,0:T(8,128)} %copy.117, pred[2,144,144]{1,2,0:T(8,128)(4,1)S(1)} %broadcast_compare_fusion), kind=kOutput, calls=%fused_computation.120 | output fusion | flops 11944079 | bytes 18012672 | tf_op jit(solution)/shard_map/sub | solution.py:114
  73.8 6.6 %fusion.34 = bf16[2,2,4,6,32,144]{5,4,3,2,1,0:T(8,128)(2,1)S(1)} fusion(bf16[2,2,4,144,3,6,32]{3,6,5,4,2,1,0:T(8,128)(2,1)} %copy-done.6, f32[2,2,4,6,144,144]{4,5,3,2,1,0:T(8,128)} %get-tuple-element.49, f32[2,2,4,6,144]{4,3,2,1,0:T(8,128)S(1)} %get-tuple-element.48), kind=kOutput, calls=%fused_computation.57 | convolution fusion | flops 131825664 | bytes 16668672 | tf_op jit(solution)/shard_map/abnhmk,abnkhd->abnmhd/dot_general | solution.py:27
  81.8 2.2 copy.121
  84.0 3.6 reshape.140
  88.1 3.3 collective-permute-done.3
  92.2 2.2 collective-permute-start.4
  94.5 2.3 copy.109
  96.7 4.0 %collective-permute-done.4 = bf16[4,12,6,192]{3,0,2,1:T(4,128)(2,1)} collective-permute-done((bf16[4,12,6,192]{3,0,2,1:T(4,128)(2,1)S(1)}, bf16[4,12,6,192]{3,0,2,1:T(4,128)(2,1)}, u32[]{:S(2)}, u32[]{:S(2)}) %collective-permute-start.4) | collective-permute-done | bytes 110624 | tf_op jit(solution)/shard_map/ppermute | solution.py:23
  100.8 1.9 fusion.49
  104.1 2.9 multiply_reduce_fusion.1
  107.4 3.5 copy.123
  110.9 2.0 copy.125
  113.0 1.2 fusion.65
  114.2 3.0 fusion.13
  117.3 3.5 fusion.7
  120.8 1.7 multiply_reduce_fusion.2
  122.6 1.8 multiply_add_fusion
  124.4 3.0 copy.126
  127.4 1.9 convert_element_type.91
  129.4 7.1 %collective-permute-start.5 = (bf16[4,3,48,192]{3,2,1,0:T(8,128)(2,1)S(1)}, bf16[4,3,48,192]{3,2,1,0:T(8,128)(2,1)S(1)}, u32[]{:S(2)}, u32[]{:S(2)}) collective-permute-start(bf16[4,3,48,192]{3,2,1,0:T(8,128)(2,1)S(1)} %slice.107), channel_id=1, source_target_pairs={{0,15},{1,0},{2,1},{3,2},{4,3},{5,4},{6,5},{7,6},{8,7},{9,8},{10,9... | collective-permute-start | bytes 663560 | tf_op jit(solution)/shard_map/ppermute | solution.py:23
  136.5 1.8 fusion.64
  138.3 3.5 collective-permute-start.6
  142.1 2.4 collective-permute-done.6
  145.8 1.8 reshape.142
  147.6 2.0 copy.128
  149.6 1.2 convolution_bitcast_fusion.1
  150.9 1.5 convolution_convert_fusion.2
  152.4 2.8 copy.130
  155.2 9.2 %fusion.43 = bf16[2,2,4,144,1,6,32]{3,6,5,2,1,0,4:T(8,128)(2,1)} fusion(bf16[2,2,4,144,6,32]{3,5,4,2,1,0:T(8,128)(2,1)} %bitcast.118, f32[2,2,4,6,144,144]{4,5,3,2,1,0:T(8,128)} %get-tuple-element.49, f32[2,2,4,6,144]{4,3,2,1,0:T(8,128)S(1)} %copy-done.25), kind=kOutput, calls=%fused_computation.69 | convolution fusion | flops 131825664 | bytes 9787392 | tf_op jit(solution)/shard_map/abnhmk,abnmhd->abnkhd/dot_general | solution.py:27
  164.7 9.5 %multiply_reduce_fusion = (f32[2,2,4,6,144]{4,3,2,1,0:T(8,128)S(1)}, f32[2,2,4,6,144,144]{4,5,3,2,1,0:T(8,128)}) fusion(f32[2,2,4,6,144,144]{4,5,3,2,1,0:T(8,128)S(1)} %bitcast.104, f32[2,2,4,6,144]{4,3,2,1,0:T(8,128)S(1)} %copy-done.25, bf16[2,2,4,144,6,32]{3,5,4,2,1,0:T(8,128)(2,1)} %bitcast.119, bf16[2,2,4,144,3,6,32]{3,6,5,4,2,1,0:T(8,128)(2,1)} %copy-done.6), kind=kOutput, calls=%fused_computation.3 | convolution fusion | flops 133360128 | bytes 19181568 | tf_op jit(solution)/shard_map/abnmhd,abnkhd->abnhmk/dot_general | solution.py:27
  174.2 11.9 %fusion.11 = (bf16[2,2,6,144,144]{3,4,2,1,0:T(8,128)(2,1)}, bf16[2,2,4,6,144,144]{4,5,3,2,1,0:T(8,128)(2,1)S(1)}) fusion(f32[2,2,4,6,144,144]{4,5,3,2,1,0:T(8,128)} %get-tuple-element.52, f32[2,2,4,6,144]{4,3,2,1,0:T(8,128)S(1)} %get-tuple-element.51, f32[2,2,4,6,144,144]{4,5,3,2,1,0:T(8,128)} %get-tuple-element.49, f32[2,2,4,6,144]{4,3,2,1,0:T(8,128)S(1)} %copy-done.25), kind=kLoop, calls=%fused_computation.20 | loop fusion | flops 9455616 | bytes 21012480 | tf_op jit(solution)/shard_map/reduce_sum | solution.py:136
  186.1 4.2 %fusion.41 = bf16[2,2,4,144,1,6,32]{3,6,5,2,1,0,4:T(8,128)(2,1)S(1)} fusion(bf16[2,2,4,6,144,144]{4,5,3,2,1,0:T(8,128)(2,1)S(1)} %get-tuple-element.41, f32[2,2,4,144,3,6,32]{3,6,5,4,2,1,0:T(8,128)} %copy-done.3), kind=kOutput, calls=%fused_computation.67 | convolution fusion | flops 128729088 | bytes 8011776 | tf_op jit(solution)/shard_map/abnhmk,abnmhd->abnkhd/dot_general | solution.py:27
  190.3 2.6 fusion.42
  193.0 1.5 pad_maximum_fusion
  195.4 2.1 copy-done.5
  197.5 2.7 convolution_bitcast_fusion
  200.3 3.8 %convolution_convert_fusion.1 = bf16[2,2,4,144,192]{4,3,2,1,0:T(8,128)(2,1)S(1)} fusion(bf16[2,2,4,144,576]{3,4,2,1,0:T(8,128)(2,1)} %bitcast.108, bf16[192,576]{1,0:T(8,128)(2,1)S(1)} %copy-done.22), kind=kOutput, calls=%fused_computation.64 | convolution fusion | flops 510050304 | bytes 3760128 | tf_op jit(solution)/shard_map/abnmd,cd->abnmc/dot_general | solution.py:27
  204.8 2.2 copy.137
  207.0 3.2 reshape.146
  211.6 4.2 %collective-permute-done.7 = bf16[4,3,48,192]{3,0,2,1:T(4,128)(2,1)S(1)} collective-permute-done((bf16[4,3,48,192]{3,0,2,1:T(4,128)(2,1)S(1)}, bf16[4,3,48,192]{3,0,2,1:T(4,128)(2,1)S(1)}, u32[]{:S(2)}, u32[]{:S(2)}) %collective-permute-start.7) | collective-permute-done | bytes 221216 | tf_op jit(solution)/shard_map/ppermute | solution.py:23
  216.0 4.9 %copy.143 = bf16[2,2,6,144,144]{4,2,1,0,3:T(8,128)(2,1)} copy(bf16[2,2,6,144,144]{3,4,2,1,0:T(8,128)(2,1)} %get-tuple-element.40) | data formatting | bytes 1990656 | tf_op jit(solution)/shard_map/convert_element_type | solution.py:196
  220.9 3.7 collective-permute-done.8
  225.6 3.9 %fusion.33 = (f32[192]{0:T(256)S(1)}, f32[4,12,48]{0,2,1:T(8,128)S(1)}, f32[4,12,48]{0,2,1:T(8,128)S(1)}) fusion(bf16[4,12,48,192]{3,0,2,1:T(4,128)(2,1)S(1)} %fusion.48, f32[4,12,48]{0,2,1:T(8,128)S(1)} %copy-done.12, f32[4,12,48]{0,2,1:T(8,128)S(1)} %copy-done.10, bf16[4,12,48,192]{3,2,1,0:T(8,128)(2,1)S(1)} %copy-done.2, f32[192]{0:T(256)S(1)} %bitcast.130), kind=kLoop, calls=%fused_computation.50 | loop fusion | flops 4418880 | bytes 1807872 | tf_op jit(solution)/shard_map/reduce_sum | solution.py:204
  229.5 3.9 %fusion.30 = bf16[4,12,48,192]{3,0,2,1:T(4,128)(2,1)S(1)} fusion(bf16[4,12,48,192]{3,0,2,1:T(4,128)(2,1)S(1)} %fusion.48, f32[4,12,48,192]{3,2,1,0:T(8,128)S(1)} %bitcast.106, f32[4,12,48]{0,2,1:T(8,128)S(1)} %broadcast_multiply_fusion.3, f32[4,12,48]{0,2,1:T(8,128)S(1)} %broadcast_multiply_fusion.4, f32[192]{0:T(256)S(1)} %bitcast.131, ...), kind=kLoop, calls=%fused_computation.47 | loop fusion | flops 4866048 | bytes 4461312 | tf_op jit(solution)/shard_map/convert_element_type | solution.py:201
  234.6 74.5 %all-reduce = (f32[1,192]{1,0:T(1,128)S(1)}, f32[1,192]{1,0:T(1,128)S(1)}) all-reduce(f32[1,192]{1,0:T(1,128)S(1)} %bitcast.133, f32[1,192]{1,0:T(1,128)S(1)} %bitcast.132), channel_id=1, replica_groups=mesh['lon'=8,'lat'=16] {'lon','lat'}, use_global_device_ids=true, to_apply=%region_18.19 | all-reduce | flops 384 | bytes 3072 | tf_op jit(solution)/shard_map/psum | solution.py:205
  309.7 49.7 %all-reduce.4.cloned.1.call-done = (f32[192,576]{1,0:T(8,128)}, f32[192,192]{1,0:T(8,128)}, f32[192,768]{1,0:T(8,128)}, f32[768,192]{0,1:T(8,128)}) async-done(((f32[192,576]{1,0:T(8,128)}, f32[192,192]{1,0:T(8,128)}, f32[192,768]{1,0:T(8,128)}, f32[768,192]{0,1:T(8,128)}), (f32[192,576]{1,0:T(8,128)}, f32[192,192]{1,0:T(8,128)}, f32[192,768]{1,0:T(8,128)}, ...) | async-done | bytes 1769488 | tf_op jit(solution)/shard_map/psum | solution.py:205
  359.4 1.7 broadcast_multiply_fusion.7
  361.1 1.9 broadcast_multiply_fusion.2
  362.9 1.9 broadcast_multiply_fusion.1
  365.7 1.9 copy.145
  (134 shorter events, 18.6 us)
Async XLA Ops:
  8.0 104.9 %copy-start = (bf16[192,768]{1,0:T(8,128)(2,1)S(1)}, bf16[192,768]{1,0:T(8,128)(2,1)}, u32[]{:S(2)}) copy-start(bf16[192,768]{1,0:T(8,128)(2,1)} %param.17) | copy-start | bytes 884740
  8.0 4.6 %copy-start.2 = (bf16[4,12,48,192]{3,2,1,0:T(8,128)(2,1)S(1)}, bf16[4,12,48,192]{3,2,1,0:T(8,128)(2,1)}, u32[]{:S(2)}) copy-start(bf16[4,12,48,192]{3,2,1,0:T(8,128)(2,1)} %param.11) | copy-start | bytes 2654212
  8.0 351.3 %all-reduce.4.cloned.1.call-start = ((), (), s32[]{:S(2)}) async-start(), calls=%async_computation.2 | async-start | bytes 3735552 | tf_op jit(solution)/shard_map/psum | solution.py:205
  8.1 19.6 %collective-permute-start.2 = (s32[3]{0:T(128)}, s32[3]{0:T(128)S(1)}, u32[]{:S(2)}, u32[]{:S(2)}) collective-permute-start(s32[3]{0:T(128)} %bitcast.134), channel_id=1, source_target_pairs={{0,15},{1,0},{2,1},{3,2},{4,3},{5,4},{6,5},{7,6},{8,7},{9,8},{10,9... | collective-permute-start | bytes 44 | tf_op jit(solution)/shard_map/ppermute | solution.py:23
  10.3 5.9 %copy-start.28 = (f32[1,192]{1,0:T(1,128)}, f32[1,192]{1,0:T(1,128)S(1)}, u32[]{:S(2)}) copy-start(f32[1,192]{1,0:T(1,128)S(1)} %get-tuple-element.45) | copy-start | bytes 2308
  12.7 3.5 copy-start.9
  14.5 7.0 %copy-start.32 = (s32[12]{0:T(128)S(1)}, s32[12]{0:T(128)}, u32[]{:S(2)}) copy-start(s32[12]{0:T(128)} %param.13) | copy-start | bytes 148
  14.6 6.9 %copy-start.11 = (f32[4,12,48]{0,2,1:T(8,128)}, f32[4,12,48]{0,2,1:T(8,128)S(1)}, u32[]{:S(2)}) copy-start(f32[4,12,48]{0,2,1:T(8,128)S(1)} %add_rsqrt_fusion.1) | copy-start | bytes 27652
  14.6 7.3 %copy-start.30 = (s32[144]{0:T(256)S(1)}, s32[144]{0:T(256)}, u32[]{:S(2)}) copy-start(s32[144]{0:T(256)} %constant.51) | copy-start | bytes 1732
  14.6 7.3 %copy-start.21 = (bf16[192,576]{1,0:T(8,128)(2,1)S(1)}, bf16[192,576]{1,0:T(8,128)(2,1)}, u32[]{:S(2)}) copy-start(bf16[192,576]{1,0:T(8,128)(2,1)} %param.15) | copy-start | bytes 663556
  17.0 11.8 %collective-permute-start = (bf16[4,3,48,192]{3,0,2,1:T(4,128)(2,1)}, bf16[4,3,48,192]{3,0,2,1:T(4,128)(2,1)S(1)}, u32[]{:S(2)}, u32[]{:S(2)}) collective-permute-start(bf16[4,3,48,192]{3,0,2,1:T(4,128)(2,1)} %slice.98), channel_id=1, source_target_pairs={{0,15},{1,0},{2,1},{3,2},{4,3},{5,4},{6,5},{7,6},{8,7},{9,8},{10,9... | collective-permute-start | bytes 663560 | tf_op jit(solution)/shard_map/ppermute | solution.py:23
  29.0 7.5 %collective-permute-start.1 = (bf16[4,12,6,192]{3,0,2,1:T(4,128)(2,1)S(1)}, bf16[4,12,6,192]{3,0,2,1:T(4,128)(2,1)S(1)}, u32[]{:S(2)}, u32[]{:S(2)}) collective-permute-start(bf16[4,12,6,192]{3,0,2,1:T(4,128)(2,1)S(1)} %pad_maximum_fusion.8), channel_id=1, source_target_pairs={{0,112},{16,0},{32,16},{48,32},{64,48},{80,64},{96,80},{112,96},{1... | collective-permute-start | bytes 331784 | tf_op jit(solution)/shard_map/ppermute | solution.py:23
  41.1 1.4 copy-start.7
  42.5 3.7 copy-start.3
  42.5 4.9 %copy-start.6 = (bf16[2,2,4,144,3,6,32]{3,6,5,4,2,1,0:T(8,128)(2,1)}, bf16[2,2,4,144,3,6,32]{3,6,5,4,2,1,0:T(8,128)(2,1)S(1)}, u32[]{:S(2)}) copy-start(bf16[2,2,4,144,3,6,32]{3,6,5,4,2,1,0:T(8,128)(2,1)S(1)} %get-tuple-element.46) | copy-start | bytes 7962628
  73.8 6.6 %copy-start.24 = (f32[2,2,4,6,144]{4,3,2,1,0:T(8,128)}, f32[2,2,4,6,144]{4,3,2,1,0:T(8,128)S(1)}, u32[]{:S(2)}) copy-start(f32[2,2,4,6,144]{4,3,2,1,0:T(8,128)S(1)} %get-tuple-element.48) | copy-start | bytes 165892
  73.8 6.7 %copy-start.26 = (bf16[192,192]{1,0:T(8,128)(2,1)S(1)}, bf16[192,192]{1,0:T(8,128)(2,1)}, u32[]{:S(2)}) copy-start(bf16[192,192]{1,0:T(8,128)(2,1)} %param.16) | copy-start | bytes 221188
  80.5 1.3 copy-start.33
  87.7 3.7 collective-permute-start.3
  91.4 0.7 copy-start.19
  92.2 8.5 %collective-permute-start.4 = (bf16[4,12,6,192]{3,0,2,1:T(4,128)(2,1)S(1)}, bf16[4,12,6,192]{3,0,2,1:T(4,128)(2,1)}, u32[]{:S(2)}, u32[]{:S(2)}) collective-permute-start(bf16[4,12,6,192]{3,0,2,1:T(4,128)(2,1)S(1)} %pad_maximum_fusion.7), channel_id=1, source_target_pairs={{0,16},{16,32},{32,48},{48,64},{64,80},{80,96},{96,112},{112,0},{1... | collective-permute-start | bytes 331784 | tf_op jit(solution)/shard_map/ppermute | solution.py:23
  113.0 1.3 copy-start.20
  114.2 3.0 copy-start.31
  120.8 1.7 copy-start.13
  120.8 1.8 copy-start.15
  127.4 9.1 %copy-start.14 = (bf16[2304,768]{1,0:T(8,128)(2,1)S(1)}, bf16[2304,768]{1,0:T(8,128)(2,1)}, u32[]{:S(2)}) copy-start(bf16[2304,768]{1,0:T(8,128)(2,1)} %copy-done.13) | copy-start | bytes 10616836
  129.4 8.8 %collective-permute-start.5 = (bf16[4,3,48,192]{3,2,1,0:T(8,128)(2,1)S(1)}, bf16[4,3,48,192]{3,2,1,0:T(8,128)(2,1)S(1)}, u32[]{:S(2)}, u32[]{:S(2)}) collective-permute-start(bf16[4,3,48,192]{3,2,1,0:T(8,128)(2,1)S(1)} %slice.107), channel_id=1, source_target_pairs={{0,15},{1,0},{2,1},{3,2},{4,3},{5,4},{6,5},{7,6},{8,7},{9,8},{10,9... | collective-permute-start | bytes 663560 | tf_op jit(solution)/shard_map/ppermute | solution.py:23
  138.3 6.3 %collective-permute-start.6 = (bf16[4,12,6,192]{3,2,1,0:T(8,128)(2,1)S(1)}, bf16[4,12,6,192]{3,2,1,0:T(8,128)(2,1)S(1)}, u32[]{:S(2)}, u32[]{:S(2)}) collective-permute-start(bf16[4,12,6,192]{3,2,1,0:T(8,128)(2,1)S(1)} %pad_maximum_fusion.5), channel_id=1, source_target_pairs={{0,112},{16,0},{32,16},{48,32},{64,48},{80,64},{96,80},{112,96},{1... | collective-permute-start | bytes 331784 | tf_op jit(solution)/shard_map/ppermute | solution.py:23
  147.6 2.0 copy-start.34
  149.6 1.3 copy-start.27
  150.9 4.3 %copy-start.25 = (f32[2,2,4,6,144]{4,3,2,1,0:T(8,128)S(1)}, f32[2,2,4,6,144]{4,3,2,1,0:T(8,128)}, u32[]{:S(2)}) copy-start(f32[2,2,4,6,144]{4,3,2,1,0:T(8,128)} %copy-done.24) | copy-start | bytes 165892
  152.4 12.0 %slice-start = ((s8[14155776]{0:T(1024)(128)(4,1)}), s8[1572864]{0:T(1024)(128)(4,1)S(1)}, s32[]{:S(2)}) async-start(s8[14155776]{0:T(1024)(128)(4,1)} %bitcast.103), calls=%async_computation.3 | async-start | bytes 3145728
  155.2 9.2 %slice-start.1 = ((s8[14155776]{0:T(1024)(128)(4,1)}), s8[4194304]{0:T(1024)(128)(4,1)S(1)}, s32[]{:S(2)}) async-start(s8[14155776]{0:T(1024)(128)(4,1)} %bitcast.103), calls=%async_computation.4 | async-start | bytes 8388608
  155.2 9.2 %slice-start.2 = ((s8[14155776]{0:T(1024)(128)(4,1)}), s8[4194304]{0:T(1024)(128)(4,1)S(1)}, s32[]{:S(2)}) async-start(s8[14155776]{0:T(1024)(128)(4,1)} %bitcast.103), calls=%async_computation.5 | async-start | bytes 8388608
  155.2 9.5 %slice-start.3 = ((s8[14155776]{0:T(1024)(128)(4,1)}), s8[4194304]{0:T(1024)(128)(4,1)S(1)}, s32[]{:S(2)}) async-start(s8[14155776]{0:T(1024)(128)(4,1)} %bitcast.103), calls=%async_computation.6 | async-start | bytes 8388608
  190.3 2.7 copy-start.16
  194.5 3.0 copy-start.8
  195.4 2.1 copy-start.5
  197.5 2.8 copy-start.22
  200.2 165.5 %reduce-scatter.2.cloned.1.call-start = ((), (), s32[]{:S(2)}) async-start(), calls=%async_computation.1 | async-start | bytes 2654208 | tf_op jit(solution)/shard_map/reduce_scatter | solution.py:195
  210.3 5.5 %collective-permute-start.7 = (bf16[4,3,48,192]{3,0,2,1:T(4,128)(2,1)S(1)}, bf16[4,3,48,192]{3,0,2,1:T(4,128)(2,1)S(1)}, u32[]{:S(2)}, u32[]{:S(2)}) collective-permute-start(bf16[4,3,48,192]{3,0,2,1:T(4,128)(2,1)S(1)} %slice.110), channel_id=1, source_target_pairs={{0,1},{1,2},{2,3},{3,4},{4,5},{5,6},{6,7},{7,8},{8,9},{9,10},{10,1... | collective-permute-start | bytes 663560 | tf_op jit(solution)/shard_map/ppermute | solution.py:23
  215.8 5.1 %copy-start.17 = (bf16[4,3,48,192]{3,0,2,1:T(4,128)(2,1)}, bf16[4,3,48,192]{3,0,2,1:T(4,128)(2,1)S(1)}, u32[]{:S(2)}) copy-start(bf16[4,3,48,192]{3,0,2,1:T(4,128)(2,1)S(1)} %collective-permute-done.7) | copy-start | bytes 663556
  215.9 8.7 %collective-permute-start.8 = (bf16[4,12,6,192]{3,0,2,1:T(4,128)(2,1)S(1)}, bf16[4,12,6,192]{3,0,2,1:T(4,128)(2,1)S(1)}, u32[]{:S(2)}, u32[]{:S(2)}) collective-permute-start(bf16[4,12,6,192]{3,0,2,1:T(4,128)(2,1)S(1)} %pad_maximum_fusion.6), channel_id=1, source_target_pairs={{0,16},{16,32},{32,48},{48,64},{64,80},{80,96},{96,112},{112,0},{1... | collective-permute-start | bytes 331784 | tf_op jit(solution)/shard_map/ppermute | solution.py:23
  220.9 3.7 copy-start.18
  220.9 4.7 %copy-start.10 = (f32[4,12,48]{0,2,1:T(8,128)S(1)}, f32[4,12,48]{0,2,1:T(8,128)}, u32[]{:S(2)}) copy-start(f32[4,12,48]{0,2,1:T(8,128)} %copy-done.9) | copy-start | bytes 27652
  220.9 4.7 %copy-start.12 = (f32[4,12,48]{0,2,1:T(8,128)S(1)}, f32[4,12,48]{0,2,1:T(8,128)}, u32[]{:S(2)}) copy-start(f32[4,12,48]{0,2,1:T(8,128)} %copy-done.11) | copy-start | bytes 27652
  220.9 4.7 %copy-start.29 = (f32[1,192]{1,0:T(1,128)S(1)}, f32[1,192]{1,0:T(1,128)}, u32[]{:S(2)}) copy-start(f32[1,192]{1,0:T(1,128)} %copy-done.28) | copy-start | bytes 2308
  225.6 4.0 %copy-start.4 = (f32[2304,192]{1,0:T(8,128)S(1)}, f32[2304,192]{1,0:T(8,128)}, u32[]{:S(2)}) copy-start(f32[2304,192]{1,0:T(8,128)} %copy.126) | copy-start | bytes 5308420
  233.4 134.2 %copy-start.1 = (bf16[192,768]{1,0:T(8,128)(2,1)S(1)}, bf16[192,768]{1,0:T(8,128)(2,1)}, u32[]{:S(2)}) copy-start(bf16[192,768]{1,0:T(8,128)(2,1)} %param.17) | copy-start | bytes 884740
  359.4 5.5 %copy-start.23 = (f32[768,192]{0,1:T(8,128)S(1)}, f32[768,192]{0,1:T(8,128)}, u32[]{:S(2)}) copy-start(f32[768,192]{0,1:T(8,128)} %get-tuple-element.39) | copy-start | bytes 1769476
Sparse Core Ops, SparseCore 0:
  200.4 158.9 all-reduce.3
Sparse Core Ops, SparseCore 1:
  221.0 83.2 reduce-scatter.1
where the time goes:
time: 381 us; the launch traced here: 375 us
  blocking collectives  74.5 us (20%)
  waiting for transfers between devices  69.1 us (18%)
  other arithmetic  66.7 us (18%)
  local copies, waits for them, and re-layouts  61.8 us (16%)
  matrix products  61.8 us (16%)
  starting transfers between devices  25 us (7%)
  between operations  16.4 us (4%)
    psum x1, blocking collectives, local(): lax.psum((grad_qkv, grad_proj, grad_up, grad_down, first_gain, second_gai...  74.5 us
    dot_general x12, matrix products, mult(): return jnp.einsum(form, left, right, preferred_element_type=jnp.float32)  50.6 us
    psum x1, waiting for transfers between devices, local(): lax.psum((grad_qkv, grad_proj, grad_up, grad_down, first_gain, second_gai...  49.7 us
    ppermute x9, starting transfers between devices, from_behind(): return lax.ppermute(value, axis, pairs)  24.9 us
    ppermute x9, waiting for transfers between devices, from_behind(): return lax.ppermute(value, axis, pairs)  19.4 us
    sub x1, other arithmetic, attend_forward(): powers = jnp.exp(scores - largest)  19.2 us
    unnamed x82, local copies, waits for them, and re-layouts  17.2 us
    reduce_sum x1, other arithmetic, attend_backward(): grad_bias = jnp.sum(grad_scores, axis=2)  11.9 us
  transfers between devices with their start and end apart: 11, of which 7 were waited for; matrix products, arithmetic and copies ran while one was open for 14% of the time, Pallas kernels for 0%

commit v1 on v0

v1 whole, which is shorter than its diff:
```python
import functools
import math

import jax
import jax.numpy as jnp
import numpy as np
from jax import lax
from jax.experimental import pallas as pl
from jax.experimental.pallas import tpu as pltpu
from jax.sharding import PartitionSpec as P

HEADS = 6
HEAD = 32
WLEV = 2
WLAT = 6
WLON = 12
C = HEADS * HEAD
FF = 4 * C
M = WLEV * WLAT * WLON
MAIN = 128
REST = M - MAIN
LANES = (HEADS + 1) * 128
SLABS = WLEV * WLAT

BF = jnp.bfloat16
F32 = jnp.float32
epsilon = 1e-05
inv_root_two = 0.7071067811865476
inv_root_tau = 0.3989422804014327


def perm(value, axis, steps):
    count = lax.axis_size(axis)
    pairs = [(source, (source + steps) % count) for source in range(count)]
    return lax.ppermute(value, axis, pairs)


def dot(left, right):
    return jnp.dot(left, right, preferred_element_type=F32)


def dot_nt(left, right):
    return lax.dot_general(left, right, (((1,), (1,)), ((), ())), preferred_element_type=F32)


def dot_tn(left, right):
    return lax.dot_general(left, right, (((0,), (0,)), ((), ())), preferred_element_type=F32)


def normalize(values):
    centred = values - jnp.mean(values, axis=-1, keepdims=True)
    inverse = lax.rsqrt(jnp.mean(centred * centred, axis=-1, keepdims=True) + epsilon)
    return centred * inverse, inverse


def norm_back(normed, inverse, gain_row, upstream):
    scaled = upstream * gain_row
    return inverse * (
        scaled
        - jnp.mean(scaled, axis=-1, keepdims=True)
        - normed * jnp.mean(scaled * normed, axis=-1, keepdims=True)
    )


def gelu_parts(u):
    bell = jnp.exp(u * u * -0.5)
    under = 1.0 + jnp.abs(u) * (0.3275911 * inv_root_two)
    t = pl.reciprocal(under, approx=True)
    t = t * (2.0 - under * t)
    tail = t * (
        0.5 * 0.254829592
        + t
        * (
            0.5 * -0.284496736
            + t * (0.5 * 1.421413741 + t * (0.5 * -1.453152027 + t * (0.5 * 1.061405429)))
        )
    )
    tail = tail * bell
    cdf = jnp.where(u >= 0.0, 1.0 - tail, tail)
    return cdf, cdf + u * (bell * inv_root_tau)


CHUNKS = ((0, 256), (256, 512), (512, 768), (768, 896))


def spread_heads(rows, mask):
    first, last = rows[:MAIN], rows[MAIN:]
    return jnp.concatenate([first] * HEADS + [last] * 8, axis=0) * mask


def per_query(weights_ref, right, right_t, rest_mask):
    parts = [
        dot(
            right_t[HEAD * e : HEAD * (e + 1), :],
            weights_ref[:, 128 * e : 128 * (e + 1)],
        )
        for e in range(HEADS)
    ]
    first = jnp.concatenate(parts, axis=0).T
    last = dot_tn(weights_ref[:, HEADS * 128 :], right) * rest_mask
    total = last[0:REST]
    for e in range(1, HEADS):
        total = total + last[REST * e : REST * (e + 1)]
    return jnp.concatenate([first, total], axis=0)


def block_kernel(
    tok_ref, cot_ref, bias_ref, kid_ref, qid_ref, gains_ref, mask_ref,
    wq_ref, wk_ref, wv_ref, wp_ref, wup_ref, wqt_ref, wkt_ref, wvt_ref, wpt_ref, wupt_ref, wdt_ref,
    gtok_ref, gbias_ref, pack_ref,
    grid_ref, grid2_ref, x_ref, c_ref, cb_ref, h_ref, n1_ref, r1_ref, biast_ref, gbt_ref,
    p_ref, pb_ref, ds_ref, qbd_ref, dobd_ref, o_ref, dys_ref, dq_ref, dk_ref, dv_ref,
    g_ref, act_ref, du_ref, gt_ref, acc_ref, gacc_ref,
):
    cols = tok_ref.shape[2]
    windows = cols // WLON
    rows = windows * M
    step = pl.program_id(0) * pl.num_programs(1) + pl.program_id(1)
    last_step = pl.num_programs(0) * pl.num_programs(1) - 1

    @pl.when(step == 0)
    def _():
        acc_ref[...] = jnp.zeros_like(acc_ref)
        gacc_ref[...] = jnp.zeros_like(gacc_ref)

    grid_ref[...] = tok_ref[...].reshape(rows, C).astype(F32)
    grid2_ref[...] = cot_ref[...].reshape(rows, C).astype(F32)
    for n in range(windows):
        for s in range(SLABS):
            to = n * M + s * WLON
            at = s * cols + n * WLON
            x_ref[to : to + WLON, :] = grid_ref[at : at + WLON, :]
            c_ref[to : to + WLON, :] = grid2_ref[at : at + WLON, :]

    gain0 = gains_ref[0:1, :]
    gain1 = gains_ref[1:2, :]

    rest_pad = jnp.zeros((128 - HEADS * REST, M), F32)
    rest = jnp.concatenate([bias_ref[0, 0, e, MAIN:, :] for e in range(HEADS)] + [rest_pad], axis=0)
    kid = kid_ref[0]
    for e in range(HEADS + 1):
        block = bias_ref[0, 0, e, :MAIN, :] if e < HEADS else rest
        lanes = slice(128 * e, 128 * (e + 1))
        biast_ref[:, lanes] = jnp.where(kid == qid_ref[0, :, lanes], block.T, -1e30)
    gbt_ref[...] = jnp.zeros_like(gbt_ref)

    scaling = float(HEAD) ** -0.5

    def window(n, carry):
        here = pl.ds(pl.multiple_of(n * M, M), M)
        x = x_ref[here, :]
        n1, r1 = normalize(x)
        n1_ref[here, :] = n1
        r1_ref[here, :] = r1
        h = (n1 * gain0).astype(BF)
        h_ref[here, :] = h
        q = (dot(h, wq_ref[...]) * scaling).astype(BF)
        k32 = dot(h, wk_ref[...])
        v32 = dot(h, wv_ref[...])
        k = k32.astype(BF)
        v = v32.astype(BF)
        kt = k32.T.astype(BF)
        vt = v32.T.astype(BF)
        qbd_ref[...] = spread_heads(q, mask_ref[...])
        for lo, hi in CHUNKS:
            scores = dot_nt(k, qbd_ref[lo:hi, :]) + biast_ref[:, lo:hi]
            powers = jnp.exp(scores - jnp.max(scores, axis=0, keepdims=True))
            weights = powers * (1.0 / jnp.sum(powers, axis=0, keepdims=True))
            p_ref[:, lo:hi] = weights
            pb_ref[:, lo:hi] = weights.astype(BF)
        rest_mask = mask_ref[HEADS * 128 :, :].astype(F32)
        o = per_query(pb_ref, v, vt, rest_mask).astype(BF)
        o_ref[here, :] = o
        attended = dot(o, wp_ref[...]).astype(BF).astype(F32)
        n2, r2 = normalize(x + attended)
        g = (n2 * gain1).astype(BF)
        g_ref[here, :] = g
        c32 = c_ref[here, :]
        cb = c32.astype(BF)
        cb_ref[here, :] = cb
        dg = jnp.zeros((M, C), F32)
        for lo in range(0, FF, 256):
            part = slice(lo, lo + 256)
            u = dot(g, wup_ref[:, part])
            cdf, slope = gelu_parts(u)
            act_ref[here, part] = (u * cdf).astype(BF)
            du = (dot(cb, wdt_ref[:, part]) * slope).astype(BF)
            du_ref[here, part] = du
            dg = dg + dot(du, wupt_ref[part, :])
        gacc_ref[8:16, :] += jnp.sum((dg * n2).reshape(M // 8, 8, C), axis=0)
        dy = c32 + norm_back(n2, r2, gain1, dg)
        gt_ref[here, :] = dy
        dys = dy.astype(BF)
        dys_ref[here, :] = dys
        do = dot(dys, wpt_ref[...]).astype(BF)
        dobd_ref[...] = spread_heads(do, mask_ref[...])
        for lo, hi in CHUNKS:
            weights = p_ref[:, lo:hi]
            dp = dot_nt(v, dobd_ref[lo:hi, :]) * weights
            ds = dp - weights * jnp.sum(dp, axis=0, keepdims=True)
            gbt_ref[:, lo:hi] += ds
            ds_ref[:, lo:hi] = ds.astype(BF)
        dv = dot(pb_ref[...], dobd_ref[...]).astype(BF)
        dk = dot(ds_ref[...], qbd_ref[...]).astype(BF)
        dq = (per_query(ds_ref, k, kt, rest_mask) * scaling).astype(BF)
        dq_ref[here, :] = dq
        dk_ref[here, :] = dk
        dv_ref[here, :] = dv
        dh = dot(dq, wqt_ref[...]) + dot(dk, wkt_ref[...]) + dot(dv, wvt_ref[...])
        dh = dh.astype(BF).astype(F32)
        n1 = n1_ref[here, :]
        gacc_ref[0:8, :] += jnp.sum((dh * n1).reshape(M // 8, 8, C), axis=0)
        gt_ref[here, :] += norm_back(n1, r1_ref[here, :], gain0, dh)
        return carry

    lax.fori_loop(0, windows, window, 0)

    for n in range(windows):
        for s in range(SLABS):
            at = n * M + s * WLON
            to = s * cols + n * WLON
            grid_ref[to : to + WLON, :] = gt_ref[at : at + WLON, :]
    gtok_ref[...] = grid_ref[...].astype(BF).reshape(gtok_ref.shape)

    for e in range(HEADS):
        gbias_ref[0, 0, e, :MAIN, :] = gbt_ref[:, 128 * e : 128 * (e + 1)].T.astype(BF)
    rest = gbt_ref[:, HEADS * 128 :].T.astype(BF)
    for e in range(HEADS):
        gbias_ref[0, 0, e, MAIN:, :] = rest[REST * e : REST * (e + 1), :]

    h = h_ref[...]
    small = [
        dot_tn(h, dq_ref[...]),
        dot_tn(h, dk_ref[...]),
        dot_tn(h, dv_ref[...]),
        dot_tn(o_ref[...], dys_ref[...]),
    ]
    for i in range(2):
        one, two = small[2 * i], small[2 * i + 1]
        acc_ref[3 * i] += one[:, :128]
        acc_ref[3 * i + 1] += two[:, :128]
        acc_ref[3 * i + 2] += jnp.concatenate([one[:, 128:], two[:, 128:]], axis=1)
    up = dot_tn(g_ref[...], du_ref[...])
    down = dot_tn(cb_ref[...], act_ref[...])
    for i in range(FF // 128):
        acc_ref[6 + i] += up[:, 128 * i : 128 * (i + 1)]
        acc_ref[12 + i] += down[:, 128 * i : 128 * (i + 1)]

    @pl.when(step == last_step)
    def _():
        for i in range(18):
            pack_ref[C * i : C * (i + 1), :] = acc_ref[i].astype(BF)
        gains = jnp.concatenate(
            [
                jnp.sum(gacc_ref[0:8, :], axis=0, keepdims=True),
                jnp.sum(gacc_ref[8:16, :], axis=0, keepdims=True),
                jnp.zeros((6, C), F32),
            ],
            axis=0,
        )
        wide = jnp.concatenate(
            [gains[:, :128], jnp.concatenate([gains[:, 128:], jnp.zeros((8, 64), F32)], axis=1)],
            axis=0,
        )
        pack_ref[18 * C : 18 * C + 16, :] = wide.astype(BF)


def run_block(tokens, cotangent, bias, row_ids, gains, w_qkv, w_proj, w_up, w_down):
    levels, nrows, cols, channels = tokens.shape
    blocks = levels // WLEV
    bands = nrows // WLAT
    rows = (cols // WLON) * M
    cell_row = np.arange(M) // WLON % WLAT
    rest = np.concatenate([np.tile(np.arange(MAIN, M), HEADS), np.zeros(128 - HEADS * REST, int)])
    lane_cell = np.concatenate([np.tile(np.arange(MAIN), HEADS), rest])
    band_ids = row_ids.reshape(bands, WLAT)
    kid = band_ids[:, cell_row][:, :, None]
    qid = band_ids[:, cell_row[lane_cell]][:, None, :]
    head_of_row = np.concatenate(
        [
            np.repeat(np.arange(HEADS), MAIN),
            np.repeat(np.arange(HEADS), REST),
            np.full(128 - HEADS * REST, -1),
        ]
    )
    mask = jnp.asarray(head_of_row[:, None] == np.arange(C)[None, :] // HEAD, BF)
    wq, wk, wv = (w_qkv[:, C * i : C * (i + 1)] for i in range(3))
    weights = (wq, wk, wv, w_proj, w_up, wq.T, wk.T, wv.T, w_proj.T, w_up.T, w_down.T)

    def whole(shape):
        zeros = (0,) * len(shape)
        return pl.BlockSpec(shape, lambda p, w: zeros)

    field = pl.BlockSpec((WLEV, WLAT, cols, C), lambda p, w: (p, w, 0, 0))
    biases = pl.BlockSpec((1, 1, HEADS, M, M), lambda p, w: (p, w, 0, 0, 0))
    v32 = lambda *shape: pltpu.VMEM(shape, F32)
    v16 = lambda *shape: pltpu.VMEM(shape, BF)
    return pl.pallas_call(
        block_kernel,
        grid=(blocks, bands),
        in_specs=[
            field,
            field,
            biases,
            pl.BlockSpec((1, M, 1), lambda p, w: (w, 0, 0)),
            pl.BlockSpec((1, 1, LANES), lambda p, w: (w, 0, 0)),
            whole(gains.shape),
            whole(mask.shape),
        ]
        + [whole(w.shape) for w in weights],
        out_specs=[field, biases, whole((4096, 128))],
        out_shape=[
            jax.ShapeDtypeStruct(tokens.shape, BF),
            jax.ShapeDtypeStruct(bias.shape, BF),
            jax.ShapeDtypeStruct((4096, 128), BF),
        ],
        scratch_shapes=[
            v32(rows, C), v32(rows, C), v32(rows, C), v32(rows, C), v16(rows, C), v16(rows, C),
            v32(rows, C), v32(rows, 1), v32(M, LANES), v32(M, LANES),
            v32(M, LANES), v16(M, LANES), v16(M, LANES), v16(LANES, C), v16(LANES, C),
            v16(rows, C), v16(rows, C), v16(rows, C), v16(rows, C), v16(rows, C),
            v16(rows, C), v16(rows, FF), v16(rows, FF), v32(rows, C), v32(18, C, 128), v32(16, C),
        ],
        compiler_params=pltpu.CompilerParams(
            vmem_limit_bytes=48 * 1024 * 1024,
            dimension_semantics=("arbitrary", "arbitrary"),
        ),
        cost_estimate=pl.CostEstimate(flops=14_000_000_000, bytes_accessed=10_000_000, transcendentals=5_000_000),
        name="window_block",
    )(tokens, cotangent, bias, kid, qid, gains, mask, *weights)


def unpack_kernel(scale, in_ref, qkv_ref, proj_ref, up_ref, down_ref, gains_ref):
    def tile(i):
        return in_ref[C * i : C * (i + 1), :].astype(F32) * scale

    half_qk, half_vp = tile(2), tile(5)
    qkv_ref[...] = jnp.concatenate(
        [tile(0), half_qk[:, :64], tile(1), half_qk[:, 64:], tile(3), half_vp[:, :64]], axis=1
    )
    proj_ref[...] = jnp.concatenate([tile(4), half_vp[:, 64:]], axis=1)
    for i in range(FF // 128):
        up_ref[:, 128 * i : 128 * (i + 1)] = tile(6 + i)
        down_ref[128 * i : 128 * (i + 1), :] = tile(12 + i).T
    wide = in_ref[18 * C : 18 * C + 16, :].astype(F32) * scale
    gains_ref[...] = jnp.concatenate([wide[0:2, :], wide[8:10, :64]], axis=1)


def unpack(packed, scale):
    shapes = ((C, 3 * C), (C, C), (C, FF), (FF, C), (2, C))
    return pl.pallas_call(
        functools.partial(unpack_kernel, scale),
        out_shape=[jax.ShapeDtypeStruct(s, F32) for s in shapes],
        compiler_params=pltpu.CompilerParams(vmem_limit_bytes=32 * 1024 * 1024),
        name="unpack_sums",
    )(packed)


def local(tokens, cotangent, region_ids, norm_gains, w_qkv, w_proj, w_up, w_down, earth_bias):
    levels, nrows, cols, channels = tokens.shape
    half_lat = WLAT // 2
    half_lon = WLON // 2
    both = ("lon", "lat")
    devices = lax.axis_size("lon") * lax.axis_size("lat")

    pair = jnp.stack([tokens, cotangent])
    ids_in = perm(region_ids[:half_lat], "lat", -1)
    row_ids = jnp.concatenate([region_ids[half_lat:], ids_in], axis=0)
    rows_in = perm(pair[:, :, :half_lat], "lat", -1)
    pair = jnp.concatenate([pair[:, :, half_lat:], rows_in], axis=2)
    cols_in = perm(pair[:, :, :, :half_lon], "lon", -1)
    pair = jnp.concatenate([pair[:, :, :, half_lon:], cols_in], axis=3)

    grad_rolled, grad_bias, packed = run_block(
        pair[0], pair[1], earth_bias, row_ids, norm_gains, w_qkv, w_proj, w_up, w_down
    )

    cols_back = perm(grad_rolled[:, :, -half_lon:], "lon", 1)
    grad_rolled = jnp.concatenate([cols_back, grad_rolled[:, :, :-half_lon]], axis=2)
    rows_back = perm(grad_rolled[:, -half_lat:], "lat", 1)
    grad_tokens = jnp.concatenate([rows_back, grad_rolled[:, :-half_lat]], axis=1)

    pieces = lax.all_to_all(packed.reshape(devices, -1, 128), both, 0, 0, tiled=True)
    summed = jnp.sum(pieces.astype(F32), axis=0).astype(BF)
    spread = jnp.broadcast_to(summed[None], (devices,) + summed.shape)
    packed = lax.all_to_all(spread, both, 0, 0, tiled=True).reshape(-1, 128)
    cell_count = levels * nrows * cols * devices
    grads = unpack(packed, 1.0 / math.sqrt(cell_count))

    lons = lax.axis_size("lon")
    blocks, bands = earth_bias.shape[:2]
    share = M // lons
    by_lon = grad_bias.reshape(blocks * bands * HEADS, lons, share, M).transpose(1, 0, 2, 3)
    shares = lax.all_to_all(by_lon.reshape(lons, -1, M), "lon", 0, 0, tiled=True)
    bias_total = jnp.sum(shares.astype(F32), axis=0).reshape(blocks, bands, HEADS, share, M)
    return (grad_tokens, *grads, bias_total)


def solution(mesh):
    placed = (
        P(None, "lat", "lon", None),
        P(None, "lat", "lon", None),
        P("lat"),
        P(),
        P(),
        P(),
        P(),
        P(),
        P(None, "lat", None, None, None),
    )
    return jax.shard_map(
        local,
        mesh=mesh,
        in_specs=placed,
        out_specs=(
            P(None, "lat", "lon", None),
            P(),
            P(),
            P(),
            P(),
            P(),
            P(None, "lat", None, "lon", None),
        ),
        check_vma=False,
    )
```

time: 381 us -> 181 us (0.48)
  blocking collectives: 74.5 us -> 0 us
  matrix products: 61.8 us -> 0 us
  Pallas kernels: 0 us -> 59.7 us
  other arithmetic: 66.7 us -> 11.5 us
  local copies, waits for them, and re-layouts: 61.8 us -> 21.2 us
  waiting for transfers between devices: 69.1 us -> 47.2 us
  between operations: 16.4 us -> 0.89 us
  starting transfers between devices: 25 us -> 38.3 us
    psum x1 -> x0, blocking collectives: 74.5 us -> none  [local(): lax.psum((grad_qkv, grad_proj, grad_up, grad_down, first_gain, second_gai...]
    dot_general x17 -> x0, matrix products: 61.8 us -> none  [the longest x12 50.6 us: mult(): return jnp.einsum(form, left, right, preferred_element_type=jnp.float32)]
    pallas_call x0 -> x2, Pallas kernels: none -> 59.7 us  [the longest x1 58.3 us: run_block(): pl.pallas_call(block_kernel, grid=(blocks, bands), in_specs=[field, field...]
    psum x1 -> x0, waiting for transfers between devices: 49.7 us -> none  [local(): lax.psum((grad_qkv, grad_proj, grad_up, grad_down, first_gain, second_gai...]
    all_to_all x0 -> x3, waiting for transfers between devices: none -> 23.2 us  [the longest x1 15.7 us: local(): lax.all_to_all(by_lon.reshape(lons, -1, M), 'lon', 0, 0, tiled=True)]
    reduce_sum x6 -> x2, other arithmetic: 24 us -> 1.61 us  [the longest x1 1.42 us: local(): summed = jnp.sum(pieces.astype(F32), axis=0).astype(BF)]
    all_to_all x0 -> x3, starting transfers between devices: none -> 21.8 us  [the longest x1 12.4 us: local(): lax.all_to_all(packed.reshape(devices, -1, 128), both, 0, 0, tiled=True)]
    sub x1 -> x0, other arithmetic: 19.2 us -> none  [attend_forward(): powers = jnp.exp(scores - largest)]
  transfers between devices with their start and end apart: 11 -> 8, of which waited for: 7 -> 5; matrix products, arithmetic and copies ran while one was open for 14% -> 15% of each run, Pallas kernels for 0% -> 0%
where the time goes in v1:
time: 181 us; the launch traced here: 179 us
  Pallas kernels  59.7 us (33%)
  waiting for transfers between devices  47.2 us (26%)
  starting transfers between devices  38.3 us (21%)
  local copies, waits for them, and re-layouts  21.2 us (12%)
  other arithmetic  11.5 us (6%)
    pallas_call x1, Pallas kernels, run_block(): pl.pallas_call(block_kernel, grid=(blocks, bands), in_specs=[field, field...  58.3 us
    ppermute x5, waiting for transfers between devices, perm(): return lax.ppermute(value, axis, pairs)  24.1 us
    ppermute x5, starting transfers between devices, perm(): return lax.ppermute(value, axis, pairs)  16.5 us
    all_to_all x1, waiting for transfers between devices, local(): lax.all_to_all(by_lon.reshape(lons, -1, M), 'lon', 0, 0, tiled=True)  15.7 us
    all_to_all x1, starting transfers between devices, local(): lax.all_to_all(packed.reshape(devices, -1, 128), both, 0, 0, tiled=True)  12.4 us
    all_to_all x1, waiting for transfers between devices, local(): lax.all_to_all(packed.reshape(devices, -1, 128), both, 0, 0, tiled=True)  7.52 us
    all_to_all x1, starting transfers between devices, local(): packed = lax.all_to_all(spread, both, 0, 0, tiled=True).reshape(-1, 128)  5.83 us
    reshape x1, local copies, waits for them, and re-layouts, local(): by_lon.reshape(lons, -1, M)  4.19 us
  transfers between devices with their start and end apart: 8, of which 5 were waited for; matrix products, arithmetic and copies ran while one was open for 15% of the time, Pallas kernels for 0%

profile of v1, /device:TPU:1, one launch (start us, length us, event | category | flops | bytes accessed | tf_op | source)
XLA Modules:
  0.0 178.7 jit_solution(13634730295011079660)
XLA Ops:
  0.6 0.0 copy-start.10
  0.6 1.5 collective-permute-start.2
  2.1 2.0 %pad_maximum_fusion.2 = bf16[2,4,3,48,192]{4,3,2,1,0:T(8,128)(2,1)} fusion(bf16[1,4,12,48,192]{4,3,2,1,0:T(8,128)(2,1)} %bitcast.35, bf16[1,4,12,48,192]{4,3,2,1,0:T(8,128)(2,1)} %bitcast.37), kind=kLoop, calls=%fused_computation.15 | loop fusion | flops 221184 | bytes 2211840 | tf_op jit(solution)/shard_map/stack | solution.py:366
  4.2 4.5 %collective-permute-start = (bf16[2,4,3,48,192]{4,3,2,1,0:T(8,128)(2,1)}, bf16[2,4,3,48,192]{4,3,2,1,0:T(8,128)(2,1)S(1)}, u32[]{:S(2)}, u32[]{:S(2)}) collective-permute-start(bf16[2,4,3,48,192]{4,3,2,1,0:T(8,128)(2,1)} %pad_maximum_fusion.2), channel_id=1, source_target_pairs={{0,15},{1,0},{2,1},{3,2},{4,3},{5,4},{6,5},{7,6},{8,7},{9,8},{10,9... | collective-permute-start | bytes 1327112 | tf_op jit(solution)/shard_map/ppermute | solution.py:35
  8.7 0.0 copy-done.10
  8.7 0.1 fusion.5
  8.8 0.0 copy-done.13
  8.8 0.1 slice.51
  8.9 0.0 copy-done.1
  8.9 0.1 copy.74
  9.0 0.1 copy.89
  9.1 0.1 copy.88
  9.2 0.1 copy.87
  9.3 0.0 copy-done
  9.3 0.2 copy.75
  9.5 0.0 copy-done.12
  9.5 0.0 copy-done.11
  9.5 0.0 copy-done.8
  9.5 1.5 fusion
  11.0 0.0 copy-start.5
  11.1 2.6 %collective-permute-done = bf16[2,4,3,48,192]{4,3,2,1,0:T(8,128)(2,1)S(1)} collective-permute-done((bf16[2,4,3,48,192]{4,3,2,1,0:T(8,128)(2,1)}, bf16[2,4,3,48,192]{4,3,2,1,0:T(8,128)(2,1)S(1)}, u32[]{:S(2)}, u32[]{:S(2)}) %collective-permute-start) | collective-permute-done | bytes 442400 | tf_op jit(solution)/shard_map/ppermute | solution.py:35
  13.7 0.8 pad_maximum_fusion.3
  14.5 5.3 %collective-permute-start.1 = (bf16[2,4,12,6,192]{4,3,2,1,0:T(8,128)(2,1)}, bf16[2,4,12,6,192]{4,3,2,1,0:T(8,128)(2,1)S(1)}, u32[]{:S(2)}, u32[]{:S(2)}) collective-permute-start(bf16[2,4,12,6,192]{4,3,2,1,0:T(8,128)(2,1)} %pad_maximum_fusion.3), channel_id=1, source_target_pairs={{0,112},{16,0},{32,16},{48,32},{64,48},{80,64},{96,80},{112,96},{1... | collective-permute-start | bytes 663560 | tf_op jit(solution)/shard_map/ppermute | solution.py:35
  19.8 0.0 collective-permute-done.2
  19.8 0.1 pad_add_fusion
  19.9 0.1 reshape.33
  19.9 0.1 copy.67
  20.0 0.7 gather_fusion
  20.7 1.0 copy.76.kid_ref
  21.7 1.9 %gather_fusion.1 = s32[896,2]{1,0:T(8,128)S(1)} fusion(s32[2,6]{0,1:T(8,128)S(1)} %copy.67, s32[1024]{0:T(1024)S(1)} %pad_clamp_fusion), kind=kCustom, calls=%fused_computation.1 | custom fusion | bytes 17920 | tf_op jit(solution)/shard_map/gather | solution.py:278
  23.6 0.2 copy.70
  23.8 2.2 %slice_maximum_fusion = bf16[2,4,12,42,192]{4,3,2,1,0:T(8,128)(2,1)S(1)} fusion(bf16[2,4,3,48,192]{4,3,2,1,0:T(8,128)(2,1)S(1)} %collective-permute-done, bf16[2,4,9,48,192]{4,3,2,1,0:T(8,128)(2,1)} %copy-done.5), kind=kLoop, calls=%fused_computation.2 | loop fusion | flops 774144 | bytes 3317760 | tf_op jit(solution)/shard_map/concatenate | solution.py:370
  25.9 0.0 copy-start.2
  26.0 0.0 copy-start.3
  26.0 0.0 copy-start.4
  26.0 0.0 collective-permute-done.1
  26.0 1.7 fusion.4
  27.7 0.0 copy-done.4
  27.7 58.3 %window_block.1 = (bf16[4,12,48,192]{3,2,1,0:T(8,128)(2,1)S(1)}, bf16[2,2,6,144,144]{4,3,2,1,0:T(8,128)(2,1)}, bf16[4096,128]{1,0:T(8,128)(2,1)}) custom-call(bf16[4,12,48,192]{3,2,1,0:T(8,128)(2,1)S(1)} %get-tuple-element.52.tok_ref, bf16[4,12,48,192]{3,2,1,0:T(8,128)(2,1)} %get-tuple-element.51.cot_ref, f32[2,2,6,144,144]{4,3,2,1,0:T(8,128)} %bias_ref.1, ...), custom_call_target="tpu_custom_call" | custom-call | flops 14000000000 | bytes 10000000 | tf_op jit(solution)/shard_map/window_block/pallas_call | solution.py:298
  86.0 12.4 %all-to-all-start = ((bf16[128,32,128]{2,1,0:T(8,128)(2,1)}), bf16[128,32,128]{2,1,0:T(8,128)(2,1)S(1)}, u32[]{:S(2)}, u32[]{:S(2)}) async-start(bf16[128,32,128]{2,1,0:T(8,128)(2,1)} %bitcast.13), calls=%async_computation | async-start | bytes 2097152 | tf_op jit(solution)/shard_map/all_to_all | solution.py:383
  98.4 4.1 %reshape.36 = bf16[24,8,18,144]{3,2,1,0:T(8,128)(2,1)} reshape(bf16[2,2,6,144,144]{4,3,2,1,0:T(8,128)(2,1)} %get-tuple-element.22) | data formatting | bytes 1990656 | tf_op jit(solution)/shard_map/reshape | solution.py:393
  102.5 3.3 %copy.80 = bf16[8,24,18,144]{3,0,2,1:T(8,128)(2,1)} copy(bf16[8,24,18,144]{3,2,0,1:T(8,128)(2,1)} %bitcast.33) | data formatting | bytes 1990656 | tf_op jit(solution)/shard_map/transpose | solution.py:393
  105.9 4.2 %copy.81 = bf16[8,432,144]{1,2,0:T(8,128)(2,1)} copy(bf16[8,432,144]{2,0,1:T(8,128)(2,1)} %bitcast.34) | data formatting | bytes 1990656 | tf_op jit(solution)/shard_map/reshape | solution.py:394
  110.1 7.5 %all-to-all-done = bf16[128,32,128]{2,1,0:T(8,128)(2,1)S(1)} async-done(((bf16[128,32,128]{2,1,0:T(8,128)(2,1)}), bf16[128,32,128]{2,1,0:T(8,128)(2,1)S(1)}, u32[]{:S(2)}, u32[]{:S(2)}) %all-to-all-start) | async-done | bytes 1048608 | tf_op jit(solution)/shard_map/all_to_all | solution.py:383
  117.6 1.0 copy-done.9
  118.6 3.6 %all-to-all-start.2 = ((bf16[8,432,144]{1,2,0:T(8,128)(2,1)}), bf16[8,432,144]{1,2,0:T(8,128)(2,1)S(1)}, u32[]{:S(2)}, u32[]{:S(2)}) async-start(bf16[8,432,144]{1,2,0:T(8,128)(2,1)} %copy.81), calls=%async_computation.2 | async-start | bytes 2359296 | tf_op jit(solution)/shard_map/all_to_all | solution.py:394
  122.1 1.4 reduce_sum.21
  123.6 15.7 %all-to-all-done.2 = bf16[8,432,144]{1,2,0:T(8,128)(2,1)S(1)} async-done(((bf16[8,432,144]{1,2,0:T(8,128)(2,1)}), bf16[8,432,144]{1,2,0:T(8,128)(2,1)S(1)}, u32[]{:S(2)}, u32[]{:S(2)}) %all-to-all-start.2) | async-done | bytes 995360 | tf_op jit(solution)/shard_map/all_to_all | solution.py:394
  139.2 1.2 broadcast_in_dim.22
  140.4 0.2 copy-done.6
  140.6 5.8 %all-to-all-start.1 = ((bf16[128,32,128]{2,1,0:T(8,128)(2,1)}), bf16[128,32,128]{2,1,0:T(8,128)(2,1)S(1)}, u32[]{:S(2)}, u32[]{:S(2)}) async-start(bf16[128,32,128]{2,1,0:T(8,128)(2,1)} %broadcast_in_dim.22), calls=%async_computation.1 | async-start | bytes 2097152 | tf_op jit(solution)/shard_map/all_to_all | solution.py:386
  146.5 3.0 %collective-permute-start.3 = (bf16[4,12,6,192]{3,2,1,0:T(8,128)(2,1)S(1)}, bf16[4,12,6,192]{3,2,1,0:T(8,128)(2,1)S(1)}, u32[]{:S(2)}, u32[]{:S(2)}) collective-permute-start(bf16[4,12,6,192]{3,2,1,0:T(8,128)(2,1)S(1)} %slice.56), channel_id=1, source_target_pairs={{0,16},{16,32},{32,48},{48,64},{64,80},{80,96},{96,112},{112,0},{1... | collective-permute-start | bytes 331784 | tf_op jit(solution)/shard_map/ppermute | solution.py:35
  149.5 17.7 %collective-permute-done.3 = bf16[4,12,6,192]{3,2,1,0:T(8,128)(2,1)S(1)} collective-permute-done((bf16[4,12,6,192]{3,2,1,0:T(8,128)(2,1)S(1)}, bf16[4,12,6,192]{3,2,1,0:T(8,128)(2,1)S(1)}, u32[]{:S(2)}, u32[]{:S(2)}) %collective-permute-start.3) | collective-permute-done | bytes 110624 | tf_op jit(solution)/shard_map/ppermute | solution.py:35
  167.2 0.1 pad_maximum_fusion.4
  167.4 2.3 %collective-permute-start.4 = (bf16[4,3,48,192]{3,2,1,0:T(8,128)(2,1)S(1)}, bf16[4,3,48,192]{3,2,1,0:T(8,128)(2,1)S(1)}, u32[]{:S(2)}, u32[]{:S(2)}) collective-permute-start(bf16[4,3,48,192]{3,2,1,0:T(8,128)(2,1)S(1)} %pad_maximum_fusion.4), channel_id=1, source_target_pairs={{0,1},{1,2},{2,3},{3,4},{4,5},{5,6},{6,7},{7,8},{8,9},{9,10},{10,1... | collective-permute-start | bytes 663560 | tf_op jit(solution)/shard_map/ppermute | solution.py:35
  169.6 3.7 %collective-permute-done.4 = bf16[4,3,48,192]{3,2,1,0:T(8,128)(2,1)S(1)} collective-permute-done((bf16[4,3,48,192]{3,2,1,0:T(8,128)(2,1)S(1)}, bf16[4,3,48,192]{3,2,1,0:T(8,128)(2,1)S(1)}, u32[]{:S(2)}, u32[]{:S(2)}) %collective-permute-start.4) | collective-permute-done | bytes 221216 | tf_op jit(solution)/shard_map/ppermute | solution.py:35
  173.3 1.5 fusion.3
  174.8 0.2 convert_reduce_fusion
  175.0 0.2 copy.82
  175.2 0.1 reshape.38
  175.2 1.1 copy.84
  176.3 0.0 all-to-all-done.1
  176.3 1.3 unpack_sums.1
  177.7 1.1 copy.83
  (17 shorter events, 0.1 us)
Async XLA Ops:
  0.6 8.0 %copy-start.10 = (bf16[192,576]{1,0:T(8,128)(2,1)S(1)}, bf16[192,576]{1,0:T(8,128)(2,1)}, u32[]{:S(2)}) copy-start(bf16[192,576]{1,0:T(8,128)(2,1)} %param.18) | copy-start | bytes 663556
  0.6 19.1 %collective-permute-start.2 = (s32[3]{0:T(128)}, s32[3]{0:T(128)S(1)}, u32[]{:S(2)}, u32[]{:S(2)}) collective-permute-start(s32[3]{0:T(128)} %bitcast.41), channel_id=1, source_target_pairs={{0,15},{1,0},{2,1},{3,2},{4,3},{5,4},{6,5},{7,6},{8,7},{9,8},{10,9... | collective-permute-start | bytes 44 | tf_op jit(solution)/shard_map/ppermute | solution.py:35
  2.1 6.6 %copy-start.13 = (s32[12]{0:T(128)S(1)}, s32[12]{0:T(128)}, u32[]{:S(2)}) copy-start(s32[12]{0:T(128)} %param.16) | copy-start | bytes 148
  2.1 6.7 %copy-start.1 = (bf16[192,192]{1,0:T(8,128)(2,1)S(1)}, bf16[192,192]{1,0:T(8,128)(2,1)}, u32[]{:S(2)}) copy-start(bf16[192,192]{1,0:T(8,128)(2,1)} %wp_ref.1) | copy-start | bytes 221188
  2.1 7.1 %copy-start = (bf16[192,768]{1,0:T(8,128)(2,1)S(1)}, bf16[192,768]{1,0:T(8,128)(2,1)}, u32[]{:S(2)}) copy-start(bf16[192,768]{1,0:T(8,128)(2,1)} %wup_ref.1) | copy-start | bytes 884740
  4.2 5.3 %copy-start.12 = (s32[144]{0:T(256)S(1)}, s32[144]{0:T(256)}, u32[]{:S(2)}) copy-start(s32[144]{0:T(256)} %constant.27) | copy-start | bytes 1732
  4.2 5.3 %copy-start.11 = (s32[896]{0:T(1024)S(1)}, s32[896]{0:T(1024)}, u32[]{:S(2)}) copy-start(s32[896]{0:T(1024)} %constant.28) | copy-start | bytes 10756
  4.2 5.3 %copy-start.8 = (bf16[4,12,48,192]{3,2,1,0:T(8,128)(2,1)S(1)}, bf16[4,12,48,192]{3,2,1,0:T(8,128)(2,1)}, u32[]{:S(2)}) copy-start(bf16[4,12,48,192]{3,2,1,0:T(8,128)(2,1)} %param.15) | copy-start | bytes 2654212
  4.2 9.5 %collective-permute-start = (bf16[2,4,3,48,192]{4,3,2,1,0:T(8,128)(2,1)}, bf16[2,4,3,48,192]{4,3,2,1,0:T(8,128)(2,1)S(1)}, u32[]{:S(2)}, u32[]{:S(2)}) collective-permute-start(bf16[2,4,3,48,192]{4,3,2,1,0:T(8,128)(2,1)} %pad_maximum_fusion.2), channel_id=1, source_target_pairs={{0,15},{1,0},{2,1},{3,2},{4,3},{5,4},{6,5},{7,6},{8,7},{9,8},{10,9... | collective-permute-start | bytes 1327112 | tf_op jit(solution)/shard_map/ppermute | solution.py:35
  11.0 2.7 %copy-start.5 = (bf16[2,4,9,48,192]{4,3,2,1,0:T(8,128)(2,1)}, bf16[2,4,9,48,192]{4,3,2,1,0:T(8,128)(2,1)S(1)}, u32[]{:S(2)}) copy-start(bf16[2,4,9,48,192]{4,3,2,1,0:T(8,128)(2,1)S(1)} %fusion) | copy-start | bytes 3981316
  14.5 11.5 %collective-permute-start.1 = (bf16[2,4,12,6,192]{4,3,2,1,0:T(8,128)(2,1)}, bf16[2,4,12,6,192]{4,3,2,1,0:T(8,128)(2,1)S(1)}, u32[]{:S(2)}, u32[]{:S(2)}) collective-permute-start(bf16[2,4,12,6,192]{4,3,2,1,0:T(8,128)(2,1)} %pad_maximum_fusion.3), channel_id=1, source_target_pairs={{0,112},{16,0},{32,16},{48,32},{64,48},{80,64},{96,80},{112,96},{1... | collective-permute-start | bytes 663560 | tf_op jit(solution)/shard_map/ppermute | solution.py:35
  25.9 1.7 copy-start.2
  26.0 1.7 copy-start.3
  26.0 1.7 copy-start.4
  86.0 31.5 %all-to-all-start = ((bf16[128,32,128]{2,1,0:T(8,128)(2,1)}), bf16[128,32,128]{2,1,0:T(8,128)(2,1)S(1)}, u32[]{:S(2)}, u32[]{:S(2)}) async-start(bf16[128,32,128]{2,1,0:T(8,128)(2,1)} %bitcast.13), calls=%async_computation | async-start | bytes 2097152 | tf_op jit(solution)/shard_map/all_to_all | solution.py:383
  117.6 1.0 copy-start.9
  118.6 20.7 %all-to-all-start.2 = ((bf16[8,432,144]{1,2,0:T(8,128)(2,1)}), bf16[8,432,144]{1,2,0:T(8,128)(2,1)S(1)}, u32[]{:S(2)}, u32[]{:S(2)}) async-start(bf16[8,432,144]{1,2,0:T(8,128)(2,1)} %copy.81), calls=%async_computation.2 | async-start | bytes 2359296 | tf_op jit(solution)/shard_map/all_to_all | solution.py:394
  139.2 1.4 copy-start.6
  140.6 35.7 %all-to-all-start.1 = ((bf16[128,32,128]{2,1,0:T(8,128)(2,1)}), bf16[128,32,128]{2,1,0:T(8,128)(2,1)S(1)}, u32[]{:S(2)}, u32[]{:S(2)}) async-start(bf16[128,32,128]{2,1,0:T(8,128)(2,1)} %broadcast_in_dim.22), calls=%async_computation.1 | async-start | bytes 2097152 | tf_op jit(solution)/shard_map/all_to_all | solution.py:386
  146.5 20.7 %collective-permute-start.3 = (bf16[4,12,6,192]{3,2,1,0:T(8,128)(2,1)S(1)}, bf16[4,12,6,192]{3,2,1,0:T(8,128)(2,1)S(1)}, u32[]{:S(2)}, u32[]{:S(2)}) collective-permute-start(bf16[4,12,6,192]{3,2,1,0:T(8,128)(2,1)S(1)} %slice.56), channel_id=1, source_target_pairs={{0,16},{16,32},{32,48},{48,64},{64,80},{80,96},{96,112},{112,0},{1... | collective-permute-start | bytes 331784 | tf_op jit(solution)/shard_map/ppermute | solution.py:35
  167.3 7.4 %copy-start.7 = (bf16[8,432,144]{1,2,0:T(8,128)(2,1)S(1)}, bf16[8,432,144]{1,2,0:T(8,128)(2,1)}, u32[]{:S(2)}) copy-start(bf16[8,432,144]{1,2,0:T(8,128)(2,1)} %copy-done.6) | copy-start | bytes 2985988
  167.4 5.9 %collective-permute-start.4 = (bf16[4,3,48,192]{3,2,1,0:T(8,128)(2,1)S(1)}, bf16[4,3,48,192]{3,2,1,0:T(8,128)(2,1)S(1)}, u32[]{:S(2)}, u32[]{:S(2)}) collective-permute-start(bf16[4,3,48,192]{3,2,1,0:T(8,128)(2,1)S(1)} %pad_maximum_fusion.4), channel_id=1, source_target_pairs={{0,1},{1,2},{2,3},{3,4},{4,5},{5,6},{6,7},{7,8},{8,9},{9,10},{10,1... | collective-permute-start | bytes 663560 | tf_op jit(solution)/shard_map/ppermute | solution.py:35

commit v2 on v1

v2 whole, which is shorter than its diff:
```python
import functools
import math

import jax
import jax.numpy as jnp
import numpy as np
from jax import lax
from jax.experimental import pallas as pl
from jax.experimental.pallas import tpu as pltpu
from jax.sharding import PartitionSpec as P

HEADS = 6
HEAD = 32
WLEV = 2
WLAT = 6
WLON = 12
C = HEADS * HEAD
FF = 4 * C
M = WLEV * WLAT * WLON
MAIN = 128
REST = M - MAIN
LANES = (HEADS + 1) * 128
SLABS = WLEV * WLAT

BF = jnp.bfloat16
F32 = jnp.float32
epsilon = 1e-05
inv_root_two = 0.7071067811865476
inv_root_tau = 0.3989422804014327


def perm(value, axis, steps):
    count = lax.axis_size(axis)
    pairs = [(source, (source + steps) % count) for source in range(count)]
    return lax.ppermute(value, axis, pairs)


def dot(left, right):
    return jnp.dot(left, right, preferred_element_type=F32)


def dot_nt(left, right):
    return lax.dot_general(left, right, (((1,), (1,)), ((), ())), preferred_element_type=F32)


def dot_tn(left, right):
    return lax.dot_general(left, right, (((0,), (0,)), ((), ())), preferred_element_type=F32)


def normalize(values):
    centred = values - jnp.mean(values, axis=-1, keepdims=True)
    inverse = lax.rsqrt(jnp.mean(centred * centred, axis=-1, keepdims=True) + epsilon)
    return centred * inverse, inverse


def norm_back(normed, inverse, gain_row, upstream):
    scaled = upstream * gain_row
    return inverse * (
        scaled
        - jnp.mean(scaled, axis=-1, keepdims=True)
        - normed * jnp.mean(scaled * normed, axis=-1, keepdims=True)
    )


def gelu_parts(u):
    bell = jnp.exp2(u * u * (-0.5 * math.log2(math.e)))
    under = 1.0 + jnp.abs(u) * (0.3275911 * inv_root_two)
    t = pl.reciprocal(under, approx=True)
    t = t * (2.0 - under * t)
    tail = t * (
        0.5 * 0.254829592
        + t
        * (
            0.5 * -0.284496736
            + t * (0.5 * 1.421413741 + t * (0.5 * -1.453152027 + t * (0.5 * 1.061405429)))
        )
    )
    tail = tail * bell
    cdf = jnp.where(u >= 0.0, 1.0 - tail, tail)
    return cdf, cdf + u * (bell * inv_root_tau)


CHUNKS = ((0, 256), (256, 512), (512, 768), (768, 896))


def spread_heads(rows, mask):
    first, last = rows[:MAIN], rows[MAIN:]
    return jnp.concatenate([first] * HEADS + [last] * 8, axis=0) * mask


def per_query(weights_ref, right, right_t, rest_mask):
    parts = []
    for e in range(HEADS):
        parts.append(
            dot(
                right_t[HEAD * e : HEAD * (e + 1), :],
                weights_ref[:, 128 * e : 128 * (e + 1)],
            )
        )
        if e % 2:
            yield None
    first = jnp.concatenate(parts, axis=0).T
    yield None
    last = dot_tn(weights_ref[:, HEADS * 128 :], right) * rest_mask
    total = last[0:REST]
    for e in range(1, HEADS):
        total = total + last[REST * e : REST * (e + 1)]
    yield jnp.concatenate([first, total], axis=0)


def in_turn(*streams):
    streams = [[0, count, pieces] for count, pieces in streams]
    while streams:
        stream = min(streams, key=lambda entry: entry[0] / entry[1])
        stream[0] += 1
        if next(stream[2], streams) is streams:
            streams.remove(stream)


INNER = ((0, 0), (0, 1), (0, 2))
EDGE = ((0, 3), (1, 0), (1, 1), (1, 2), (1, 3))
STATE = ("ds", "q", "k", "h", "dv", "xb", "dy")
HALF_LAT = WLAT // 2
HALF_LON = WLON // 2
HALO_COLS = 8


class Refs:
    pass


def named(names, refs):
    r = Refs()
    for name, ref in zip(names, refs):
        setattr(r, name, ref)
    return r


def window_pieces(w, n, local_rows, cols):
    for a in range(WLEV):
        for b in range(WLAT):
            slab = (a * WLAT + b) * WLON
            i = HALF_LAT + w * WLAT + b
            j = HALF_LON + n * WLON
            own = min(WLON, cols - j)
            if i < local_rows:
                yield "own", None, (a * local_rows + i) * cols + j, own, slab
                if own < WLON:
                    yield "lon", a * local_rows + i, 0, WLON - own, slab + own
            else:
                i = i - local_rows
                yield "lat", None, (a * HALF_LAT + i) * cols + j, own, slab
                if own < WLON:
                    yield "corner", a * HALF_LAT + i, 0, WLON - own, slab + own


def forward_kernel(names, places, cols, *refs):
    r = named(names, refs)
    edge = hasattr(r, "halo_lat")
    bands = sorted({w for w, n in places})
    step = pl.program_id(0)
    last_step = pl.num_programs(0) - 1

    @pl.when(step == 0)
    def _():
        if edge:
            r.acc[...] = r.acc_in[...]
            r.proj[...] = r.proj_in[...]
            r.share32[...] = jnp.zeros_like(r.share32)
        else:
            r.acc[...] = jnp.zeros_like(r.acc)
            r.proj[...] = jnp.zeros_like(r.proj)
        r.wq[...] = r.wqkv[:, 0:C]
        r.wk[...] = r.wqkv[:, C : 2 * C]
        r.wv[...] = r.wqkv[:, 2 * C : 3 * C]

    gain0 = r.gains[0:1, :]
    gain1 = r.gains[1:2, :]
    scaling = float(HEAD) ** -0.5

    local_rows = r.tok.shape[1]
    for at, ref in enumerate((r.tok, r.cot)):
        r.own32[at] = ref[...].reshape(WLEV * local_rows * cols, C).astype(F32)
        if edge:
            r.lat32[at] = r.halo_lat[at].reshape(WLEV * HALF_LAT * cols, C).astype(F32)
            for a in range(WLEV):
                for i in range(local_rows):
                    r.lon32[at, a * local_rows + i] = r.halo_lon[at, a, i].astype(F32)
                for i in range(HALF_LAT):
                    r.corner32[at, a * HALF_LAT + i] = r.halo_corner[at, a, i].astype(F32)

    def bias_rows(at, w):
        kid = jnp.zeros((M, 1), jnp.int32)
        qid = jnp.zeros((1, LANES), jnp.int32)
        for b in range(WLAT):
            kid = jnp.where(r.krow[...] == b, r.ids[w * WLAT + b], kid)
            qid = jnp.where(r.qrow[...] == b, r.ids[w * WLAT + b], qid)
        rest_pad = jnp.zeros((128 - HEADS * REST, M), F32)
        rest = jnp.concatenate([r.bias[0, at, e, MAIN:, :] for e in range(HEADS)] + [rest_pad], axis=0)
        for e in range(HEADS + 1):
            block = r.bias[0, at, e, :MAIN, :] if e < HEADS else rest
            lanes = slice(128 * e, 128 * (e + 1))
            r.biast[at, :, lanes] = jnp.where(kid == qid[:, lanes], block.T, -1e30)
            yield None
        if edge and w == 0:
            r.gbt[at] = r.gbt_in[0]
        else:
            r.gbt[at] = jnp.zeros((M, LANES), F32)
        yield None

    rest_mask = r.mask[HEADS * 128 :, :].astype(F32)

    def front(t):
        w, n = places[t]
        band = bands.index(w)
        here = slice(t * M, (t + 1) * M)
        for at, to in ((0, r.x), (1, r.c)):
            for name, lead, start, length, slab in window_pieces(w, n, local_rows, cols):
                source = getattr(r, name + "32")
                index = (at,) if lead is None else (at, lead)
                to[t * M + slab : t * M + slab + length, :] = source[index + (slice(start, start + length),)]
            yield None
        x = r.x[here, :]
        r.xb[0, t] = x.astype(BF)
        h = (normalize(x)[0] * gain0).astype(BF)
        r.h[0, t] = h
        yield None
        q = (dot(h, r.wq[...]) * scaling).astype(BF)
        r.q[0, t] = q
        r.qbd[t] = spread_heads(q, r.mask[...])
        yield None
        r.k[0, t] = dot(h, r.wk[...]).astype(BF)
        yield None
        v32 = dot(h, r.wv[...])
        r.v[here, :] = v32.astype(BF)
        vt = v32.T.astype(BF)
        yield None
        for lo, hi in CHUNKS:
            scores = dot_nt(r.k[0, t], r.qbd[t, lo:hi, :]) + r.biast[band, :, lo:hi]
            powers = jnp.exp(scores - jnp.max(scores, axis=0, keepdims=True))
            weights = powers * (1.0 / jnp.sum(powers, axis=0, keepdims=True))
            r.p[t, :, lo:hi] = weights
            r.pb[t, :, lo:hi] = weights.astype(BF)
            yield None
        for o in per_query(r.pb.at[t], r.v[here, :], vt, rest_mask):
            yield None
        o = o.astype(BF)
        r.o[here, :] = o
        y = r.x[here, :] + dot(o, r.wp[...]).astype(BF).astype(F32)
        yield None
        n2, r2 = normalize(y)
        r.n2[here, :] = n2
        r.r2[here, :] = r2
        r.g[here, :] = (n2 * gain1).astype(BF)
        r.cb[here, :] = r.c[here, :].astype(BF)
        yield None

    def middle(t):
        here = slice(t * M, (t + 1) * M)
        for lo in range(0, FF, 256):
            part = slice(lo, lo + 256)
            u = dot(r.g[here, :], r.wup[:, part])
            cdf, slope = gelu_parts(u)
            r.act[here, part] = (u * cdf).astype(BF)
            yield None
            r.du[here, part] = (dot_nt(r.cb[here, :], r.wdown[part, :]) * slope).astype(BF)
            yield None

    def back(t):
        w, n = places[t]
        band = bands.index(w)
        here = slice(t * M, (t + 1) * M)
        dg = dot_nt(r.du[here, :], r.wup[...])
        yield None
        dy = r.c[here, :] + norm_back(r.n2[here, :], r.r2[here, :], gain1, dg)
        r.dy[0, t] = dy
        dys = dy.astype(BF)
        r.dys[here, :] = dys
        yield None
        do = dot_nt(dys, r.wp[...]).astype(BF)
        r.dobd[t] = spread_heads(do, r.mask[...])
        yield None
        for lo, hi in CHUNKS:
            weights = r.p[t, :, lo:hi]
            dp = dot_nt(r.v[here, :], r.dobd[t, lo:hi, :]) * weights
            ds = dp - weights * jnp.sum(dp, axis=0, keepdims=True)
            r.gbt[band, :, lo:hi] += ds
            r.ds[0, t, :, lo:hi] = ds.astype(BF)
            yield None
        r.dv[0, t] = dot(r.pb[t], r.dobd[t]).astype(BF)
        yield None

    def dense_sums():
        for first, left, right in ((0, r.g, r.du), (6, r.cb, r.act)):
            left_t = left[...].T
            for lo in range(0, FF, 256):
                part = dot(left_t, right[:, lo : lo + 256])
                r.acc[first + lo // 128] += part[:, :128]
                r.acc[first + lo // 128 + 1] += part[:, 128:]
                yield None

    def proj_sum():
        r.proj[...] += dot_tn(r.o[...], r.dys[...])
        yield None

    def share_bias(at):
        share = M // r.share_out.shape[0]
        gbt = r.gbt.at[at]
        last = gbt[:, HEADS * 128 :].T
        for e in range(HEADS):
            r.bias32[at, M * e : M * e + MAIN, :] = gbt[:, 128 * e : 128 * (e + 1)].T[:, :MAIN]
            r.bias32[at, M * e + MAIN : M * (e + 1), :] = last[REST * e : REST * (e + 1), :MAIN]
            yield None
        far = jnp.concatenate(
            [gbt[MAIN:, 128 * e : 128 * (e + 1)] for e in range(HEADS)]
            + [jnp.zeros((128 - HEADS * REST, 128), F32)],
            axis=0,
        )
        r.bias32[at, M * HEADS : M * HEADS + MAIN, :] = far.T
        r.bias32[at, M * HEADS + MAIN : M * (HEADS + 1), :] = jnp.concatenate(
            [last[REST * e : REST * (e + 1), MAIN:] for e in range(HEADS)]
            + [jnp.zeros((REST, 128 - HEADS * REST), F32)],
            axis=1,
        )
        yield None
        for d in range(r.share_out.shape[0]):
            for e in range(HEADS + 1):
                r.share32[at, d, share * e : share * (e + 1), :] = r.bias32[
                    at, M * e + share * d : M * e + share * (d + 1), :
                ]
            r.share_out[d, 0, at] = r.share32[at, d].astype(BF)
            yield None

    count = len(places)
    for slot in range(count + 2):
        streams = []
        if slot == 0:
            in_turn((8, bias_rows(0, bands[0])))
            streams += [(8, bias_rows(at, bands[at])) for at in range(1, len(bands))]
        if slot < count:
            streams.append((16, front(slot)))
        if 0 <= slot - 1 < count:
            streams.append((6, middle(slot - 1)))
        if 0 <= slot - 2 < count:
            streams.append((9, back(slot - 2)))
        if slot == count + 1:
            streams.append((6, dense_sums()))
        in_turn(*streams)
    ends = [(1, proj_sum())]
    if edge:
        ends += [(15, share_bias(at)) for at in range(len(bands))]
    in_turn(*ends)

    if not edge:
        r.gbt_out[0] = r.gbt[0]

    @pl.when(step == last_step)
    def _():
        r.acc_out[...] = r.acc[...]
        r.proj_out[...] = r.proj[...]


def whole(shape):
    zeros = (0,) * len(shape)
    return pl.BlockSpec(tuple(shape), lambda p: zeros)


def by_level(shape, at, blocks=2):
    block = list(shape)
    block[at] = shape[at] // blocks
    return pl.BlockSpec(tuple(block), lambda p: tuple(p if i == at else 0 for i in range(len(shape))))


def call(kernel, blocks, ins, outs, scratch, name, share_of, limit, *fixed):
    names = [i[0] for i in ins] + [o[0] for o in outs] + [s[0] for s in scratch]
    return pl.pallas_call(
        functools.partial(kernel, names, *fixed),
        grid=(blocks,),
        in_specs=[i[2] for i in ins],
        out_specs=[o[3] for o in outs],
        out_shape=[jax.ShapeDtypeStruct(tuple(o[1]), o[2]) for o in outs],
        scratch_shapes=[pltpu.VMEM(tuple(s[1]), s[2]) for s in scratch],
        compiler_params=pltpu.CompilerParams(
            vmem_limit_bytes=limit * 1024 * 1024,
            dimension_semantics=("arbitrary",),
        ),
        cost_estimate=pl.CostEstimate(
            flops=int(14e9 * share_of), bytes_accessed=int(10e6 * share_of), transcendentals=int(5e6 * share_of)
        ),
        name=name,
    )(*[i[1] for i in ins])


def head_mask():
    head_of_row = np.concatenate(
        [
            np.repeat(np.arange(HEADS), MAIN),
            np.repeat(np.arange(HEADS), REST),
            np.full(128 - HEADS * REST, -1),
        ]
    )
    return jnp.asarray(head_of_row[:, None] == np.arange(C)[None, :] // HEAD, BF)


def run_forward(places, tokens, cotangent, bias, row_ids, weights, halos=None, before=None, lons=8):
    levels, local_rows, cols, channels = tokens.shape
    blocks = levels // WLEV
    count = len(places)
    rows = count * M
    bands = len({w for w, n in places})
    cell_row = (np.arange(M) // WLON % WLAT).astype(np.int32)
    rest = np.concatenate([np.tile(np.arange(MAIN, M), HEADS), np.zeros(128 - HEADS * REST, int)])
    lane_cell = np.concatenate([np.tile(np.arange(MAIN), HEADS), rest])
    edge = halos is not None
    ins = [
        ("tok", tokens, by_level(tokens.shape, 0)),
        ("cot", cotangent, by_level(tokens.shape, 0)),
        ("bias", bias, pl.BlockSpec((1, bands, HEADS, M, M), lambda p: (p, 0, 0, 0, 0))),
        ("ids", row_ids, pl.BlockSpec(memory_space=pltpu.SMEM)),
        ("krow", jnp.asarray(cell_row[:, None]), whole((M, 1))),
        ("qrow", jnp.asarray(cell_row[lane_cell][None, :]), whole((1, LANES))),
        ("mask", head_mask(), whole((LANES, C))),
    ] + [(name, w, whole(w.shape)) for name, w in weights.items()]
    flat = WLEV * local_rows * cols
    acc = (12, C, 128)
    scratch = [
        ("own32", (2, flat, C), F32),
        ("x", (rows, C), F32),
        ("c", (rows, C), F32),
        ("n2", (rows, C), F32),
        ("r2", (rows, 1), F32),
        ("biast", (bands, M, LANES), F32),
        ("gbt", (bands, M, LANES), F32),
        ("p", (count, M, LANES), F32),
        ("pb", (count, M, LANES), BF),
        ("qbd", (count, LANES, C), BF),
        ("dobd", (count, LANES, C), BF),
        ("acc", acc, F32),
        ("proj", (C, C), F32),
        ("act", (rows, FF), BF),
        ("du", (rows, FF), BF),
    ] + [(name, (rows, C), BF) for name in ("v", "o", "g", "cb", "dys")]
    scratch += [(name, (C, C), BF) for name in ("wq", "wk", "wv")]
    outs = []
    for name in STATE:
        shape = (blocks, count, M, LANES if name == "ds" else C)
        outs.append((name, shape, F32 if name == "dy" else BF, by_level(shape, 0)))
    outs += [("acc_out", acc, F32, whole(acc)), ("proj_out", (C, C), F32, whole((C, C)))]
    if edge:
        for name, value in zip(("halo_lat", "halo_lon", "halo_corner"), halos):
            ins.append((name, value, by_level(value.shape, 1)))
        for name, value in zip(("acc_in", "proj_in", "gbt_in"), before):
            ins.append((name, value, by_level(value.shape, 0) if name == "gbt_in" else whole(value.shape)))
        share = (lons, blocks, bands, 128, 128)
        outs.append(("share_out", share, BF, by_level(share, 1)))
        scratch += [
            ("lat32", (2, WLEV * HALF_LAT * cols, C), F32),
            ("lon32", (2, WLEV * local_rows, HALO_COLS, C), F32),
            ("corner32", (2, WLEV * HALF_LAT, HALO_COLS, C), F32),
            ("bias32", (bands, M * (HEADS + 1), 128), F32),
            ("share32", (bands, lons, 128, 128), F32),
        ]
    else:
        outs.append(("gbt_out", (blocks, M, LANES), F32, by_level((blocks, M, LANES), 0)))
    name = "edge_windows" if edge else "inner_windows"
    got = call(forward_kernel, blocks, ins, outs, scratch, name, count * blocks / 20, 60, places, cols)
    return got[: len(STATE)], got[len(STATE) :]


def attention_kernel(names, parts, *refs):
    r = named(names, refs)
    step = pl.program_id(0)
    last_step = pl.num_programs(0) - 1
    scaling = float(HEAD) ** -0.5
    rest_mask = r.mask[HEADS * 128 :, :].astype(F32)

    @pl.when(step == 0)
    def _():
        r.acc[...] = jnp.zeros_like(r.acc)

    def window(at, part, t):
        here = slice(at * M, (at + 1) * M)
        get = lambda name: getattr(r, name + str(part)).at[0, t]
        r.h[here, :] = get("h")[...]
        r.dv[here, :] = get("dv")[...]
        r.qbd[at % 4] = spread_heads(get("q")[...], r.mask[...])
        yield None
        k = get("k")[...]
        kt = k.astype(F32).T.astype(BF)
        yield None
        dk = dot(get("ds")[...], r.qbd[at % 4]).astype(BF)
        r.dk[here, :] = dk
        getattr(r, "dk_out" + str(part))[0, t] = dk
        yield None
        for dq in per_query(get("ds"), k, kt, rest_mask):
            yield None
        dq = (dq * scaling).astype(BF)
        r.dq[here, :] = dq
        getattr(r, "dq_out" + str(part))[0, t] = dq
        yield None

    order = [(part, t) for part, count in enumerate(parts) for t in range(count)]
    for at in range(0, len(order), 2):
        in_turn(*[(9, window(at + i, *order[at + i])) for i in range(2)])
    ht = r.h[...].T
    for i, right in enumerate((r.dq, r.dk, r.dv)):
        r.acc[i] += dot(ht, right[...])

    @pl.when(step == last_step)
    def _():
        per = r.pack_out.shape[1]

        def put(i, tile):
            r.pack_out[C // per * i : C // per * (i + 1)] = tile.astype(BF).reshape(C // per, per, 128)

        small = (r.acc[0], r.acc[1], r.acc[2], r.proj[...])
        for i in range(2):
            one, two = small[2 * i], small[2 * i + 1]
            put(3 * i, one[:, :128])
            put(3 * i + 1, two[:, :128])
            put(3 * i + 2, jnp.concatenate([one[:, 128:], two[:, 128:]], axis=1))
        for i in range(12):
            put(6 + i, r.dense[i])
        first = jnp.zeros((C, C), F32)
        for i in range(3):
            first = first + r.acc[i] * r.wqkv[:, C * i : C * (i + 1)].astype(F32)
        second = jnp.zeros((C, 128), F32)
        for i in range(6):
            second = second + r.dense[i] * r.wup[:, 128 * i : 128 * (i + 1)].astype(F32)
        sums = [jnp.sum(part.T, axis=0, keepdims=True) for part in (first, second)]
        gains = jnp.concatenate([sums[0] / r.gains[0:1, :], sums[1] / r.gains[1:2, :], jnp.zeros((6, C), F32)], axis=0)
        wide = jnp.concatenate(
            [gains[:, :128], jnp.concatenate([gains[:, 128:], jnp.zeros((8, 64), F32)], axis=1)],
            axis=0,
        )
        r.pack_out[18 * C // per, 0:16, :] = wide.astype(BF)


def run_attention(states, sums, weights, devices):
    ins, outs = [], []
    blocks = states[0][0].shape[0]
    parts = [state[0].shape[1] for state in states]
    for part, state in enumerate(states):
        for name, value in zip(STATE, state):
            if name not in ("xb", "dy"):
                ins.append((name + str(part), value, by_level(value.shape, 0)))
    mask = head_mask()
    ins += [
        ("dense", sums[0], whole(sums[0].shape)),
        ("proj", sums[1], whole(sums[1].shape)),
        ("mask", mask, whole(mask.shape)),
    ] + [(name, weights[name], whole(weights[name].shape)) for name in ("wqkv", "wup", "gains")]
    for part, count in enumerate(parts):
        shape = (blocks, count, M, C)
        for name in ("dq_out", "dk_out"):
            outs.append((name + str(part), shape, BF, by_level(shape, 0)))
    pack = (devices, 4096 // devices, 128)
    outs.append(("pack_out", pack, BF, whole(pack)))
    rows = sum(parts) * M
    scratch = [("acc", (3, C, C), F32), ("qbd", (4, LANES, C), BF)]
    scratch += [(name, (rows, C), BF) for name in ("h", "dq", "dk", "dv")]
    got = call(attention_kernel, blocks, ins, outs, scratch, "query_key_grads", 0.3, 60, parts)
    return [got[0:2], got[2:4]], got[-1]


def finish_kernel(names, parts, cols, *refs):
    r = named(names, refs)
    local_rows = r.gt_out.shape[1]
    gain0 = r.gains[0:1, :]

    @pl.when(pl.program_id(0) == 0)
    def _():
        for i in range(3):
            r.w[i] = r.wqkv[:, C * i : C * (i + 1)]
        for name in ("own32", "lat32", "lon32", "corner32"):
            ref = getattr(r, name)
            ref[...] = jnp.zeros_like(ref)

    def window(at, part, t, place):
        get = lambda name: getattr(r, name + str(part)).at[0, t]
        dh = dot_nt(get("dq")[...], r.w[0]) + dot_nt(get("dk")[...], r.w[1]) + dot_nt(get("dv")[...], r.w[2])
        dh = dh.astype(BF).astype(F32)
        yield None
        n1, r1 = normalize(get("xb")[...].astype(F32))
        yield None
        r.gt[at] = get("dy")[...] + norm_back(n1, r1, gain0, dh)
        yield None
        for name, lead, start, length, slab in window_pieces(*place, local_rows, cols):
            target = getattr(r, name + "32")
            index = () if lead is None else (lead,)
            target[index + (slice(start, start + length),)] = r.gt[at, slab : slab + length, :]
        yield None

    order = [(part, t, place) for part, places in enumerate(parts) for t, place in enumerate(places)]
    for at in range(0, len(order), 2):
        in_turn(*[(4, window(at + i, *order[at + i])) for i in range(2)])
    r.gt_out[...] = r.own32[...].astype(BF).reshape(r.gt_out.shape)
    r.lat_out[...] = r.lat32[...].astype(BF).reshape(r.lat_out.shape)
    for a in range(WLEV):
        for i in range(local_rows):
            r.lon_out[a, i] = r.lon32[a * local_rows + i].astype(BF)
        for i in range(HALF_LAT):
            r.corner_out[a, i] = r.corner32[a * HALF_LAT + i].astype(BF)


def run_finish(parts, states, grads, weights, shape):
    levels, local_rows, cols, channels = shape
    blocks = levels // WLEV
    ins = []
    for part, (state, grad) in enumerate(zip(states, grads)):
        for name in ("dv", "xb", "dy"):
            value = state[STATE.index(name)]
            ins.append((name + str(part), value, by_level(value.shape, 0)))
        for name, value in zip(("dq", "dk"), grad):
            ins.append((name + str(part), value, by_level(value.shape, 0)))
    ins += [(name, weights[name], whole(weights[name].shape)) for name in ("wqkv", "gains")]
    outs = []
    for name, out in (
        ("gt_out", shape),
        ("lat_out", (levels, HALF_LAT, cols, C)),
        ("lon_out", (levels, local_rows, HALO_COLS, C)),
        ("corner_out", (levels, HALF_LAT, HALO_COLS, C)),
    ):
        outs.append((name, out, BF, by_level(out, 0)))
    count = sum(len(places) for places in parts)
    scratch = [
        ("w", (3, C, C), BF),
        ("gt", (count, M, C), F32),
        ("own32", (WLEV * local_rows * cols, C), F32),
        ("lat32", (WLEV * HALF_LAT * cols, C), F32),
        ("lon32", (WLEV * local_rows, HALO_COLS, C), F32),
        ("corner32", (WLEV * HALF_LAT, HALO_COLS, C), F32),
    ]
    return call(finish_kernel, blocks, ins, outs, scratch, "token_grads", 0.1, 60, parts, cols)


def assemble_kernel(own_ref, lat_ref, lon_ref, corner_ref, out_ref):
    levels, local_rows, cols, channels = out_ref.shape
    keep = lax.broadcasted_iota(jnp.int32, (16, C), 0) >= HALF_LON
    pad = jnp.zeros((16 - HALO_COLS, C), F32)
    for a in range(levels):
        for i in range(local_rows):
            row = own_ref.at[a, i] if i >= HALF_LAT else lat_ref.at[a, i]
            left = lon_ref[a, i] if i >= HALF_LAT else corner_ref[a, i]
            left = jnp.concatenate([left.astype(F32), pad], axis=0)
            out_ref[a, i, 0:16, :] = jnp.where(keep, row[0:16, :].astype(F32), left).astype(BF)
            out_ref[a, i, 16:, :] = row[16:, :]


def assemble(own, *received):
    return pl.pallas_call(
        assemble_kernel,
        out_shape=jax.ShapeDtypeStruct(own.shape, BF),
        compiler_params=pltpu.CompilerParams(vmem_limit_bytes=32 * 1024 * 1024),
        name="assemble",
    )(own, *received)


def sum_kernel(in_ref, out_ref):
    total = jnp.sum(in_ref[...].astype(F32), axis=0, keepdims=True).astype(BF)
    out_ref[...] = jnp.broadcast_to(total, out_ref.shape)


def sum_pieces(pieces):
    return pl.pallas_call(
        sum_kernel,
        out_shape=jax.ShapeDtypeStruct(pieces.shape, BF),
        compiler_params=pltpu.CompilerParams(vmem_limit_bytes=32 * 1024 * 1024),
        name="sum_pieces",
    )(pieces)


def sum_bias_kernel(in_ref, out_ref):
    blocks, bands, heads, share, cells = out_ref.shape
    for p in range(blocks):
        for w in range(bands):
            total = jnp.sum(in_ref[:, p, w].astype(F32), axis=0)
            far = total[share * heads : share * (heads + 1)]
            for e in range(heads):
                near = total[share * e : share * (e + 1)]
                out_ref[p, w, e] = jnp.concatenate([near, far[:, REST * e : REST * (e + 1)]], axis=1)


def sum_bias(pieces, shape):
    return pl.pallas_call(
        sum_bias_kernel,
        out_shape=jax.ShapeDtypeStruct(shape, F32),
        compiler_params=pltpu.CompilerParams(vmem_limit_bytes=32 * 1024 * 1024),
        name="sum_bias",
    )(pieces)


def unpack_kernel(scale, in_ref, qkv_ref, proj_ref, up_ref, down_ref, gains_ref):
    def tile(i):
        return in_ref[C * i : C * (i + 1), :].astype(F32) * scale

    half_qk, half_vp = tile(2), tile(5)
    qkv_ref[...] = jnp.concatenate(
        [tile(0), half_qk[:, :64], tile(1), half_qk[:, 64:], tile(3), half_vp[:, :64]], axis=1
    )
    proj_ref[...] = jnp.concatenate([tile(4), half_vp[:, 64:]], axis=1)
    for i in range(FF // 128):
        up_ref[:, 128 * i : 128 * (i + 1)] = tile(6 + i)
        down_ref[128 * i : 128 * (i + 1), :] = tile(12 + i).T
    wide = in_ref[18 * C : 18 * C + 16, :].astype(F32) * scale
    gains_ref[...] = jnp.concatenate([wide[0:2, :], wide[8:10, :64]], axis=1)


def unpack(packed, scale):
    shapes = ((C, 3 * C), (C, C), (C, FF), (FF, C), (2, C))
    return pl.pallas_call(
        functools.partial(unpack_kernel, scale),
        out_shape=[jax.ShapeDtypeStruct(s, F32) for s in shapes],
        compiler_params=pltpu.CompilerParams(vmem_limit_bytes=60 * 1024 * 1024),
        name="unpack_sums",
    )(packed)


def local(tokens, cotangent, region_ids, norm_gains, w_qkv, w_proj, w_up, w_down, earth_bias):
    levels, nrows, cols, channels = tokens.shape
    both = ("lon", "lat")
    lons, lats = lax.axis_size("lon"), lax.axis_size("lat")
    devices = lons * lats

    def corner_perm(value, steps):
        pairs = [
            (a * lats + b, (a + steps) % lons * lats + (b + steps) % lats)
            for a in range(lons)
            for b in range(lats)
        ]
        return lax.ppermute(value, both, pairs)

    def both_fields(cut):
        return jnp.stack([cut(tokens), cut(cotangent)])

    halos = (
        perm(both_fields(lambda f: f[:, :HALF_LAT]), "lat", -1),
        perm(both_fields(lambda f: f[:, :, :HALO_COLS]), "lon", -1),
        corner_perm(both_fields(lambda f: f[:, :HALF_LAT, :HALO_COLS]), -1),
    )
    ids_in = perm(region_ids[:HALF_LAT], "lat", -1)
    row_ids = jnp.concatenate([region_ids[HALF_LAT:], ids_in], axis=0)

    weights = {"wqkv": w_qkv, "wp": w_proj, "wup": w_up, "wdown": w_down, "gains": norm_gains}
    inner, sums = run_forward(INNER, tokens, cotangent, earth_bias, region_ids[HALF_LAT:], weights)
    edge, sums = run_forward(EDGE, tokens, cotangent, earth_bias, row_ids, weights, halos, sums, lons)

    shares = lax.all_to_all(sums[2], "lon", 0, 0, tiled=True)
    states = (inner, edge)
    grads, packed = run_attention(states, sums, weights, devices)
    packed, shares = lax.optimization_barrier((packed, shares))
    pieces = lax.all_to_all(packed, both, 0, 0, tiled=True)
    own, *sent = run_finish((INNER, EDGE), states, grads, weights, tokens.shape)
    lat_in = perm(sent[0], "lat", 1)
    lon_in = perm(sent[1], "lon", 1)
    corner_in = corner_perm(sent[2], 1)
    summed, own = lax.optimization_barrier((sum_pieces(pieces), own))
    packed = lax.all_to_all(summed, both, 0, 0, tiled=True).reshape(-1, 128)
    cell_count = levels * nrows * cols * devices
    weight_grads = unpack(packed, 1.0 / math.sqrt(cell_count))
    bias_total = sum_bias(shares, earth_bias.shape[:3] + (M // lons, M))
    return (assemble(own, lat_in, lon_in, corner_in), *weight_grads, bias_total)


def solution(mesh):
    placed = (
        P(None, "lat", "lon", None),
        P(None, "lat", "lon", None),
        P("lat"),
        P(),
        P(),
        P(),
        P(),
        P(),
        P(None, "lat", None, None, None),
    )
    return jax.shard_map(
        local,
        mesh=mesh,
        in_specs=placed,
        out_specs=(
            P(None, "lat", "lon", None),
            P(),
            P(),
            P(),
            P(),
            P(),
            P(None, "lat", None, "lon", None),
        ),
        check_vma=False,
    )
```

time: 181 us -> 144 us (0.80)
  waiting for transfers between devices: 47.2 us -> 32.9 us
  local copies, waits for them, and re-layouts: 21.2 us -> 9.75 us
  other arithmetic: 11.5 us -> 0.8 us
  Pallas kernels: 59.7 us -> 66.2 us
  starting transfers between devices: 38.3 us -> 32 us
    ppermute x5, waiting for transfers between devices: 24.1 us -> 0.01 us  [perm(): return lax.ppermute(value, axis, pairs)]
    ppermute x0 -> x2, waiting for transfers between devices: none -> 14.6 us  [corner_perm(): return lax.ppermute(value, both, pairs)]
    ppermute x0 -> x2, starting transfers between devices: none -> 10.7 us  [corner_perm(): return lax.ppermute(value, both, pairs)]
    ppermute x5, starting transfers between devices: 16.5 us -> 6.84 us  [perm(): return lax.ppermute(value, axis, pairs)]
    reshape x5 -> x0, local copies, waits for them, and re-layouts: 8.55 us -> none  [the longest x1 4.19 us: local(): by_lon.reshape(lons, -1, M)]
    all_to_all x3, starting transfers between devices: 21.8 us -> 14.5 us  [the longest x1 5.8 us: local(): pieces = lax.all_to_all(packed, both, 0, 0, tiled=True)]
    pallas_call x1 -> x7, Pallas kernels: 58.3 us -> 63.4 us  [the longest x4 60.9 us: call(): pl.pallas_call(functools.partial(kernel, names, *fixed), grid=(blocks,),...]
    all_to_all x3, waiting for transfers between devices: 23.2 us -> 18.2 us  [the longest x1 12.4 us: local(): pieces = lax.all_to_all(packed, both, 0, 0, tiled=True)]
  transfers between devices with their start and end apart: 8 -> 10, of which waited for: 5 -> 3; matrix products, arithmetic and copies ran while one was open for 15% -> 4% of each run, Pallas kernels for 0% -> 25%
where the time goes in v2:
time: 144 us; the launch traced here: 142 us
  Pallas kernels  66.2 us (46%)
  waiting for transfers between devices  32.9 us (23%)
  starting transfers between devices  32 us (22%)
  local copies, waits for them, and re-layouts  9.75 us (7%)
    pallas_call x4, Pallas kernels, call(): pl.pallas_call(functools.partial(kernel, names, *fixed), grid=(blocks,),...  60.9 us
    ppermute x2, waiting for transfers between devices, corner_perm(): return lax.ppermute(value, both, pairs)  14.6 us
    all_to_all x1, waiting for transfers between devices, local(): pieces = lax.all_to_all(packed, both, 0, 0, tiled=True)  12.4 us
    ppermute x2, starting transfers between devices, corner_perm(): return lax.ppermute(value, both, pairs)  10.7 us
    ppermute x5, starting transfers between devices, perm(): return lax.ppermute(value, axis, pairs)  6.84 us
    unnamed x25, local copies, waits for them, and re-layouts  6.2 us
    all_to_all x1, waiting for transfers between devices, local(): shares = lax.all_to_all(sums[2], 'lon', 0, 0, tiled=True)  5.87 us
    all_to_all x1, starting transfers between devices, local(): pieces = lax.all_to_all(packed, both, 0, 0, tiled=True)  5.8 us
  transfers between devices with their start and end apart: 10, of which 3 were waited for; matrix products, arithmetic and copies ran while one was open for 4% of the time, Pallas kernels for 25%

profile of v2, /device:TPU:1, one launch (start us, length us, event | category | flops | bytes accessed | tf_op | source)
XLA Modules:
  0.0 142.4 jit_solution(18288189614968242704)
XLA Ops:
  0.6 1.5 %collective-permute-start = (s32[3]{0:T(128)}, s32[3]{0:T(128)S(1)}, u32[]{:S(2)}, u32[]{:S(2)}) collective-permute-start(s32[3]{0:T(128)} %bitcast.15), channel_id=1, source_target_pairs={{0,15},{1,0},{2,1},{3,2},{4,3},{5,4},{6,5},{7,6},{8,7},{9,8},{10,9... | collective-permute-start | bytes 44 | tf_op jit(solution)/shard_map/ppermute | solution.py:35
  2.1 0.8 slice_bitcast_fusion.4
  3.0 9.3 %collective-permute-start.3 = (bf16[2,4,3,8,192]{4,3,2,1,0:T(8,128)(2,1)S(1)}, bf16[2,4,3,8,192]{4,3,2,1,0:T(8,128)(2,1)S(1)}, u32[]{:S(2)}, u32[]{:S(2)}) collective-permute-start(bf16[2,4,3,8,192]{4,3,2,1,0:T(8,128)(2,1)S(1)} %pad_maximum_fusion.2), channel_id=1, source_target_pairs={{0,127},{1,112},{2,113},{3,114},{4,115},{5,116},{6,117},{7,118},{8... | collective-permute-start | bytes 221192 | tf_op jit(solution)/shard_map/ppermute | solution.py:731
  12.3 1.1 slice_bitcast_fusion.2
  13.4 0.1 pad_maximum_fusion.1
  13.5 0.0 copy-start.9
  13.5 0.0 copy-start.2
  13.5 0.6 collective-permute-start.2
  14.1 1.1 slice_bitcast_fusion
  15.2 0.1 pad_maximum_fusion
  15.3 0.1 collective-permute-start.1
  15.4 0.0 copy-done.9
  15.4 0.6 slice.25.refs_3_
  16.0 0.0 copy-done.2
  16.0 0.9 copy.23.refs_10_
  16.9 0.0 copy-start.10
  16.9 17.5 %inner_windows.1 = (bf16[2,3,144,896]{3,2,1,0:T(8,128)(2,1)}, bf16[2,3,144,192]{3,2,1,0:T(8,128)(2,1)}, bf16[2,3,144,192]{3,2,1,0:T(8,128)(2,1)}, bf16[2,3,144,1...) custom-call(bf16[4,12,48,192]{3,2,1,0:T(8,128)(2,1)} %refs_0_.3, ...), custom_call_target="tpu_custom_call" | custom-call | flops 4200000000 | bytes 3000000 | tf_op jit(solution)/shard_map/inner_windows/pallas_call | solution.py:376
  34.4 0.0 collective-permute-done
  34.4 0.0 copy-done.10
  34.5 0.6 pad_add_fusion.refs_3_
  35.0 0.0 collective-permute-done.3.refs_14_
  35.0 0.0 copy-start.7
  35.0 0.0 collective-permute-done.2.refs_13_
  35.1 0.0 copy-start.4
  35.1 0.0 collective-permute-done.1.refs_12_
  35.1 0.0 copy-start.3
  35.1 0.6 copy-done.7
  35.7 0.1 copy-done.4
  35.8 0.2 copy-done.3
  36.0 26.3 %edge_windows.1 = (bf16[2,5,144,896]{3,2,1,0:T(8,128)(2,1)}, bf16[2,5,144,192]{3,2,1,0:T(8,128)(2,1)}, bf16[2,5,144,192]{3,2,1,0:T(8,128)(2,1)}, bf16[2,5,144,19...) custom-call(bf16[4,12,48,192]{3,2,1,0:T(8,128)(2,1)} %refs_0_.3, ...), custom_call_target="tpu_custom_call" | custom-call | flops 7000000000 | bytes 5000000 | tf_op jit(solution)/shard_map/edge_windows/pallas_call | solution.py:376
  62.3 3.9 %all-to-all-start = ((bf16[8,2,2,128,128]{4,3,2,1,0:T(8,128)(2,1)}), bf16[8,2,2,128,128]{4,3,2,1,0:T(8,128)(2,1)S(1)}, u32[]{:S(2)}, u32[]{:S(2)}) async-start(bf16[8,2,2,128,128]{4,3,2,1,0:T(8,128)(2,1)} %get-tuple-element.61), calls=%async_computation | async-start | bytes 2097152 | tf_op jit(solution)/shard_map/all_to_all | solution.py:748
  66.2 10.1 %query_key_grads.1 = (bf16[2,3,144,192]{3,2,1,0:T(8,128)(2,1)}, bf16[2,3,144,192]{3,2,1,0:T(8,128)(2,1)}, bf16[2,5,144,192]{3,2,1,0:T(8,128)(2,1)}, bf16[2,5,144...) custom-call(bf16[2,3,144,896]{3,2,1,0:T(8,128)(2,1)} %get-tuple-element.45.refs_0_, ...), custom_call_target="tpu_custom_call" | custom-call | flops 4200000000 | bytes 3000000 | tf_op jit(solution)/shard_map/query_key_grads/pallas_call | solution.py:376
  76.3 5.9 %all-to-all-done.in_ref = bf16[8,2,2,128,128]{4,3,2,1,0:T(8,128)(2,1)S(1)} async-done(((bf16[8,2,2,128,128]{4,3,2,1,0:T(8,128)(2,1)}), bf16[8,2,2,128,128]{4,3,2,1,0:T(8,128)(2,1)S(1)}, u32[]{:S(2)}, u32[]{:S(2)}) %all-to-all-start) | async-done | bytes 1048608 | tf_op jit(solution)/shard_map/all_to_all | solution.py:748
  82.2 5.8 %all-to-all-start.1 = ((bf16[128,32,128]{2,1,0:T(8,128)(2,1)}), bf16[128,32,128]{2,1,0:T(8,128)(2,1)S(1)}, u32[]{:S(2)}, u32[]{:S(2)}) async-start(bf16[128,32,128]{2,1,0:T(8,128)(2,1)} %get-tuple-element.62), calls=%async_computation.1 | async-start | bytes 2097152 | tf_op jit(solution)/shard_map/all_to_all | solution.py:752
  88.0 6.9 %token_grads.1 = (bf16[4,12,48,192]{3,2,1,0:T(8,128)(2,1)}, bf16[4,3,48,192]{3,2,1,0:T(8,128)(2,1)}, bf16[4,12,8,192]{3,2,1,0:T(8,128)(2,1)}, bf16[4,3,8,192]{3,2,1,0:T(8,128)(2,1)}) custom-call(bf16[2,3,144,192]{3,2,1,0:T(8,128)(2,1)} %get-tuple-element.49.refs_4_.refs_0_, bf16[2,3,144,192]{3,2,1,0:T(8,128)(2,1)} %get-tuple-element.63.refs_1_, ...), custom_call_target="tpu_custom_call" | custom-call | flops 1400000000 | bytes 1000000 | tf_op jit(solution)/shard_map/token_grads/pallas_call | solution.py:376
  95.0 12.4 %all-to-all-done.1.in_ref = bf16[128,32,128]{2,1,0:T(8,128)(2,1)S(1)} async-done(((bf16[128,32,128]{2,1,0:T(8,128)(2,1)}), bf16[128,32,128]{2,1,0:T(8,128)(2,1)S(1)}, u32[]{:S(2)}, u32[]{:S(2)}) %all-to-all-start.1) | async-done | bytes 1048608 | tf_op jit(solution)/shard_map/all_to_all | solution.py:752
  107.3 1.2 sum_pieces.1
  108.5 0.0 copy-start.5
  108.5 0.0 copy-start.6
  108.5 0.0 copy-start.8
  108.5 4.7 %all-to-all-start.2 = ((bf16[128,32,128]{2,1,0:T(8,128)(2,1)}), bf16[128,32,128]{2,1,0:T(8,128)(2,1)S(1)}, u32[]{:S(2)}, u32[]{:S(2)}) async-start(bf16[128,32,128]{2,1,0:T(8,128)(2,1)} %sum_pieces.1), calls=%async_computation.2 | async-start | bytes 2097152 | tf_op jit(solution)/shard_map/all_to_all | solution.py:758
  113.3 0.0 copy-done.5
  113.3 2.0 %collective-permute-start.4 = (bf16[4,3,48,192]{3,2,1,0:T(8,128)(2,1)S(1)}, bf16[4,3,48,192]{3,2,1,0:T(8,128)(2,1)S(1)}, u32[]{:S(2)}, u32[]{:S(2)}) collective-permute-start(bf16[4,3,48,192]{3,2,1,0:T(8,128)(2,1)S(1)} %copy-done.5), channel_id=1, source_target_pairs={{0,1},{1,2},{2,3},{3,4},{4,5},{5,6},{6,7},{7,8},{8,9},{9,10},{10,1... | collective-permute-start | bytes 663560 | tf_op jit(solution)/shard_map/ppermute | solution.py:35
  115.2 0.0 copy-done.6
  115.3 2.7 %collective-permute-start.5 = (bf16[4,12,8,192]{3,2,1,0:T(8,128)(2,1)S(1)}, bf16[4,12,8,192]{3,2,1,0:T(8,128)(2,1)S(1)}, u32[]{:S(2)}, u32[]{:S(2)}) collective-permute-start(bf16[4,12,8,192]{3,2,1,0:T(8,128)(2,1)S(1)} %copy-done.6), channel_id=1, source_target_pairs={{0,16},{16,32},{32,48},{48,64},{64,80},{80,96},{96,112},{112,0},{1... | collective-permute-start | bytes 442376 | tf_op jit(solution)/shard_map/ppermute | solution.py:35
  118.0 0.0 copy-done.8
  118.0 0.0 copy-start
  118.0 1.4 collective-permute-start.6
  119.3 0.2 sum_bias.1
  119.6 1.1 copy.26
  120.7 14.6 %collective-permute-done.6.corner_ref = bf16[4,3,8,192]{3,2,1,0:T(8,128)(2,1)S(1)} collective-permute-done((bf16[4,3,8,192]{3,2,1,0:T(8,128)(2,1)S(1)}, bf16[4,3,8,192]{3,2,1,0:T(8,128)(2,1)S(1)}, u32[]{:S(2)}, u32[]{:S(2)}) %collective-permute-start.6) | collective-permute-done | bytes 36896 | tf_op jit(solution)/shard_map/ppermute | solution.py:731
  135.3 0.0 collective-permute-done.5.lon_ref
  135.3 0.0 collective-permute-done.4.lat_ref
  135.3 0.0 copy-done
  135.3 1.1 assemble.1
  136.4 0.0 all-to-all-done.2
  136.4 0.0 copy-start.1
  136.4 1.0 copy-done.1
  137.4 2.8 %unpack_sums.1 = (f32[192,576]{1,0:T(8,128)}, f32[192,192]{1,0:T(8,128)}, f32[192,768]{1,0:T(8,128)}, f32[768,192]{1,0:T(8,128)}, f32[2,192]{1,0:T(2,128)}) custom-call(bf16[4096,128]{1,0:T(8,128)(2,1)} %bitcast.14), custom_call_target="tpu_custom_call" | custom-call | tf_op jit(solution)/shard_map/unpack_sums/pallas_call | solution.py:711
  140.2 2.2 %copy.25 = f32[768,192]{0,1:T(8,128)} copy(f32[768,192]{1,0:T(8,128)} %get-tuple-element.87) | data formatting | bytes 1179648
  (1 shorter events, 0.0 us)
Async XLA Ops:
  0.6 33.8 %collective-permute-start = (s32[3]{0:T(128)}, s32[3]{0:T(128)S(1)}, u32[]{:S(2)}, u32[]{:S(2)}) collective-permute-start(s32[3]{0:T(128)} %bitcast.15), channel_id=1, source_target_pairs={{0,15},{1,0},{2,1},{3,2},{4,3},{5,4},{6,5},{7,6},{8,7},{9,8},{10,9... | collective-permute-start | bytes 44 | tf_op jit(solution)/shard_map/ppermute | solution.py:35
  3.0 32.1 %collective-permute-start.3 = (bf16[2,4,3,8,192]{4,3,2,1,0:T(8,128)(2,1)S(1)}, bf16[2,4,3,8,192]{4,3,2,1,0:T(8,128)(2,1)S(1)}, u32[]{:S(2)}, u32[]{:S(2)}) collective-permute-start(bf16[2,4,3,8,192]{4,3,2,1,0:T(8,128)(2,1)S(1)} %pad_maximum_fusion.2), channel_id=1, source_target_pairs={{0,127},{1,112},{2,113},{3,114},{4,115},{5,116},{6,117},{7,118},{8... | collective-permute-start | bytes 221192 | tf_op jit(solution)/shard_map/ppermute | solution.py:731
  13.5 1.9 %copy-start.9 = (s32[12]{0:T(128)S(1)}, s32[12]{0:T(128)}, u32[]{:S(2)}) copy-start(s32[12]{0:T(128)} %param.18) | copy-start | bytes 148
  13.5 2.5 %copy-start.2 = (bf16[768,192]{0,1:T(8,128)(2,1)S(1)}, bf16[768,192]{0,1:T(8,128)(2,1)}, u32[]{:S(2)}) copy-start(bf16[768,192]{0,1:T(8,128)(2,1)} %param.23) | copy-start | bytes 884740
  13.5 21.6 %collective-permute-start.2 = (bf16[2,4,12,8,192]{4,3,2,1,0:T(8,128)(2,1)S(1)}, bf16[2,4,12,8,192]{4,3,2,1,0:T(8,128)(2,1)S(1)}, u32[]{:S(2)}, u32[]{:S(2)}) collective-permute-start(bf16[2,4,12,8,192]{4,3,2,1,0:T(8,128)(2,1)S(1)} %pad_maximum_fusion.1), channel_id=1, source_target_pairs={{0,112},{16,0},{32,16},{48,32},{64,48},{80,64},{96,80},{112,96},{1... | collective-permute-start | bytes 884744 | tf_op jit(solution)/shard_map/ppermute | solution.py:35
  15.3 19.8 %collective-permute-start.1 = (bf16[2,4,3,48,192]{4,3,2,1,0:T(8,128)(2,1)S(1)}, bf16[2,4,3,48,192]{4,3,2,1,0:T(8,128)(2,1)S(1)}, u32[]{:S(2)}, u32[]{:S(2)}) collective-permute-start(bf16[2,4,3,48,192]{4,3,2,1,0:T(8,128)(2,1)S(1)} %pad_maximum_fusion), channel_id=1, source_target_pairs={{0,15},{1,0},{2,1},{3,2},{4,3},{5,4},{6,5},{7,6},{8,7},{9,8},{10,9... | collective-permute-start | bytes 1327112 | tf_op jit(solution)/shard_map/ppermute | solution.py:35
  16.9 17.5 %copy-start.10 = (s32[9]{0:T(128)S(1)}, s32[9]{0:T(128)}, u32[]{:S(2)}) copy-start(s32[9]{0:T(128)} %slice.25.refs_3_) | copy-start | bytes 112
  35.0 0.6 copy-start.7
  35.1 0.8 copy-start.4
  35.1 0.9 copy-start.3
  62.3 19.9 %all-to-all-start = ((bf16[8,2,2,128,128]{4,3,2,1,0:T(8,128)(2,1)}), bf16[8,2,2,128,128]{4,3,2,1,0:T(8,128)(2,1)S(1)}, u32[]{:S(2)}, u32[]{:S(2)}) async-start(bf16[8,2,2,128,128]{4,3,2,1,0:T(8,128)(2,1)} %get-tuple-element.61), calls=%async_computation | async-start | bytes 2097152 | tf_op jit(solution)/shard_map/all_to_all | solution.py:748
  82.2 25.1 %all-to-all-start.1 = ((bf16[128,32,128]{2,1,0:T(8,128)(2,1)}), bf16[128,32,128]{2,1,0:T(8,128)(2,1)S(1)}, u32[]{:S(2)}, u32[]{:S(2)}) async-start(bf16[128,32,128]{2,1,0:T(8,128)(2,1)} %get-tuple-element.62), calls=%async_computation.1 | async-start | bytes 2097152 | tf_op jit(solution)/shard_map/all_to_all | solution.py:752
  108.5 4.8 %copy-start.5 = (bf16[4,3,48,192]{3,2,1,0:T(8,128)(2,1)S(1)}, bf16[4,3,48,192]{3,2,1,0:T(8,128)(2,1)}, u32[]{:S(2)}) copy-start(bf16[4,3,48,192]{3,2,1,0:T(8,128)(2,1)} %get-tuple-element.73) | copy-start | bytes 663556
  108.5 6.7 %copy-start.6 = (bf16[4,12,8,192]{3,2,1,0:T(8,128)(2,1)S(1)}, bf16[4,12,8,192]{3,2,1,0:T(8,128)(2,1)}, u32[]{:S(2)}) copy-start(bf16[4,12,8,192]{3,2,1,0:T(8,128)(2,1)} %get-tuple-element.74) | copy-start | bytes 442372
  108.5 9.5 %copy-start.8 = (bf16[4,3,8,192]{3,2,1,0:T(8,128)(2,1)S(1)}, bf16[4,3,8,192]{3,2,1,0:T(8,128)(2,1)}, u32[]{:S(2)}) copy-start(bf16[4,3,8,192]{3,2,1,0:T(8,128)(2,1)} %get-tuple-element.75) | copy-start | bytes 110596
  108.5 27.9 %all-to-all-start.2 = ((bf16[128,32,128]{2,1,0:T(8,128)(2,1)}), bf16[128,32,128]{2,1,0:T(8,128)(2,1)S(1)}, u32[]{:S(2)}, u32[]{:S(2)}) async-start(bf16[128,32,128]{2,1,0:T(8,128)(2,1)} %sum_pieces.1), calls=%async_computation.2 | async-start | bytes 2097152 | tf_op jit(solution)/shard_map/all_to_all | solution.py:758
  113.3 22.0 %collective-permute-start.4 = (bf16[4,3,48,192]{3,2,1,0:T(8,128)(2,1)S(1)}, bf16[4,3,48,192]{3,2,1,0:T(8,128)(2,1)S(1)}, u32[]{:S(2)}, u32[]{:S(2)}) collective-permute-start(bf16[4,3,48,192]{3,2,1,0:T(8,128)(2,1)S(1)} %copy-done.5), channel_id=1, source_target_pairs={{0,1},{1,2},{2,3},{3,4},{4,5},{5,6},{6,7},{7,8},{8,9},{9,10},{10,1... | collective-permute-start | bytes 663560 | tf_op jit(solution)/shard_map/ppermute | solution.py:35
  115.3 20.0 %collective-permute-start.5 = (bf16[4,12,8,192]{3,2,1,0:T(8,128)(2,1)S(1)}, bf16[4,12,8,192]{3,2,1,0:T(8,128)(2,1)S(1)}, u32[]{:S(2)}, u32[]{:S(2)}) collective-permute-start(bf16[4,12,8,192]{3,2,1,0:T(8,128)(2,1)S(1)} %copy-done.6), channel_id=1, source_target_pairs={{0,16},{16,32},{32,48},{48,64},{64,80},{80,96},{96,112},{112,0},{1... | collective-permute-start | bytes 442376 | tf_op jit(solution)/shard_map/ppermute | solution.py:35
  118.0 17.3 %copy-start = (bf16[4,12,48,192]{3,2,1,0:T(8,128)(2,1)S(1)}, bf16[4,12,48,192]{3,2,1,0:T(8,128)(2,1)}, u32[]{:S(2)}) copy-start(bf16[4,12,48,192]{3,2,1,0:T(8,128)(2,1)} %get-tuple-element.72.own_ref) | copy-start | bytes 2654212
  118.0 17.3 %collective-permute-start.6 = (bf16[4,3,8,192]{3,2,1,0:T(8,128)(2,1)S(1)}, bf16[4,3,8,192]{3,2,1,0:T(8,128)(2,1)S(1)}, u32[]{:S(2)}, u32[]{:S(2)}) collective-permute-start(bf16[4,3,8,192]{3,2,1,0:T(8,128)(2,1)S(1)} %copy-done.8), channel_id=1, source_target_pairs={{0,17},{1,18},{2,19},{3,20},{4,21},{5,22},{6,23},{7,24},{8,25},{9,... | collective-permute-start | bytes 110600 | tf_op jit(solution)/shard_map/ppermute | solution.py:731
  136.4 1.0 copy-start.1

commit v3 on v2

--- a/solution.py
+++ b/solution.py
@@ -66,7 +66,6 @@
     bell = jnp.exp2(u * u * (-0.5 * math.log2(math.e)))
     under = 1.0 + jnp.abs(u) * (0.3275911 * inv_root_two)
     t = pl.reciprocal(under, approx=True)
-    t = t * (2.0 - under * t)
     tail = t * (
         0.5 * 0.254829592
         + t
@@ -117,6 +116,25 @@
             streams.remove(stream)
 
 
+def chain(*streams):
+    for stream in streams:
+        for piece in stream:
+            yield None
+
+
+def run_events(events):
+    tick = 0
+    while events:
+        for event in list(events):
+            start, pieces, stream = event
+            for i in range(pieces if start <= tick else 0):
+                if next(stream, events) is events:
+                    events.remove(event)
+                    break
+        tick += 1
+
+
+STAGGER = 3
 INNER = ((0, 0), (0, 1), (0, 2))
 EDGE = ((0, 3), (1, 0), (1, 1), (1, 2), (1, 3))
 STATE = ("ds", "q", "k", "h", "dv", "xb", "dy")
@@ -179,22 +197,37 @@
     scaling = float(HEAD) ** -0.5
 
     local_rows = r.tok.shape[1]
-    for at, ref in enumerate((r.tok, r.cot)):
-        r.own32[at] = ref[...].reshape(WLEV * local_rows * cols, C).astype(F32)
-        if edge:
-            r.lat32[at] = r.halo_lat[at].reshape(WLEV * HALF_LAT * cols, C).astype(F32)
+
+    def widen(w):
+        for at, ref in enumerate((r.tok, r.cot)):
+            first = HALF_LAT + w * WLAT
+            stop = min(first + WLAT, local_rows)
             for a in range(WLEV):
-                for i in range(local_rows):
-                    r.lon32[at, a * local_rows + i] = r.halo_lon[at, a, i].astype(F32)
-                for i in range(HALF_LAT):
-                    r.corner32[at, a * HALF_LAT + i] = r.halo_corner[at, a, i].astype(F32)
+                for i in range(first, stop):
+                    row = a * local_rows + i
+                    r.own32[at, row * cols : (row + 1) * cols, :] = ref[a, i].astype(F32)
+                    if edge:
+                        r.lon32[at, row] = r.halo_lon[at, a, i].astype(F32)
+                yield None
+            if stop < first + WLAT:
+                r.lat32[at] = r.halo_lat[at].reshape(WLEV * HALF_LAT * cols, C).astype(F32)
+                for a in range(WLEV):
+                    for i in range(HALF_LAT):
+                        r.corner32[at, a * HALF_LAT + i] = r.halo_corner[at, a, i].astype(F32)
+                yield None
+
+    def row_id(w, b):
+        i = HALF_LAT + w * WLAT + b
+        if i < local_rows:
+            return r.ids[i].astype(F32)
+        return r.halo_lat[0, 0, i - local_rows, 0:1, 0:1].astype(F32)
 
     def bias_rows(at, w):
-        kid = jnp.zeros((M, 1), jnp.int32)
-        qid = jnp.zeros((1, LANES), jnp.int32)
+        kid = jnp.zeros((M, 1), F32)
+        qid = jnp.zeros((1, LANES), F32)
         for b in range(WLAT):
-            kid = jnp.where(r.krow[...] == b, r.ids[w * WLAT + b], kid)
-            qid = jnp.where(r.qrow[...] == b, r.ids[w * WLAT + b], qid)
+            kid = jnp.where(r.krow[...] == b, row_id(w, b), kid)
+            qid = jnp.where(r.qrow[...] == b, row_id(w, b), qid)
         rest_pad = jnp.zeros((128 - HEADS * REST, M), F32)
         rest = jnp.concatenate([r.bias[0, at, e, MAIN:, :] for e in range(HEADS)] + [rest_pad], axis=0)
         for e in range(HEADS + 1):
@@ -238,7 +271,7 @@
         for lo, hi in CHUNKS:
             scores = dot_nt(r.k[0, t], r.qbd[t, lo:hi, :]) + r.biast[band, :, lo:hi]
             powers = jnp.exp(scores - jnp.max(scores, axis=0, keepdims=True))
-            weights = powers * (1.0 / jnp.sum(powers, axis=0, keepdims=True))
+            weights = powers * pl.reciprocal(jnp.sum(powers, axis=0, keepdims=True), approx=True)
             r.p[t, :, lo:hi] = weights
             r.pb[t, :, lo:hi] = weights.astype(BF)
             yield None
@@ -263,7 +296,7 @@
             cdf, slope = gelu_parts(u)
             r.act[here, part] = (u * cdf).astype(BF)
             yield None
-            r.du[here, part] = (dot_nt(r.cb[here, :], r.wdown[part, :]) * slope).astype(BF)
+            r.du[here, part] = (dot(r.cb[here, :], r.wdt[:, part]) * slope).astype(BF)
             yield None
 
     def back(t):
@@ -290,11 +323,12 @@
         r.dv[0, t] = dot(r.pb[t], r.dobd[t]).astype(BF)
         yield None
 
-    def dense_sums():
+    def sums(t):
+        here = slice(t * M, (t + 1) * M)
         for first, left, right in ((0, r.g, r.du), (6, r.cb, r.act)):
-            left_t = left[...].T
+            left_t = left[here, :].T
             for lo in range(0, FF, 256):
-                part = dot(left_t, right[:, lo : lo + 256])
+                part = dot(left_t, right[here, lo : lo + 256])
                 r.acc[first + lo // 128] += part[:, :128]
                 r.acc[first + lo // 128 + 1] += part[:, 128:]
                 yield None
@@ -332,24 +366,20 @@
             yield None
 
     count = len(places)
-    for slot in range(count + 2):
-        streams = []
-        if slot == 0:
-            in_turn((8, bias_rows(0, bands[0])))
-            streams += [(8, bias_rows(at, bands[at])) for at in range(1, len(bands))]
-        if slot < count:
-            streams.append((16, front(slot)))
-        if 0 <= slot - 1 < count:
-            streams.append((6, middle(slot - 1)))
-        if 0 <= slot - 2 < count:
-            streams.append((9, back(slot - 2)))
-        if slot == count + 1:
-            streams.append((6, dense_sums()))
-        in_turn(*streams)
-    ends = [(1, proj_sum())]
-    if edge:
-        ends += [(15, share_bias(at)) for at in range(len(bands))]
-    in_turn(*ends)
+    length = 31
+    events = [(0, 2, widen(bands[0])), (0, 3, bias_rows(0, bands[0]))]
+    events += [(1, 2, widen(w)) for w in bands[1:]]
+    events += [(2, 2, bias_rows(at, bands[at])) for at in range(1, len(bands))]
+    start = [3 + STAGGER * t for t in range(count)]
+    for t in range(count):
+        events.append((start[t], 1, chain(front(t), middle(t), back(t))))
+        events.append((start[t] + 22, 1, sums(t)))
+    for at in range(len(bands)):
+        last = max(t for t, place in enumerate(places) if place[0] == bands[at])
+        if edge:
+            events.append((start[last] + length + 1, 2, share_bias(at)))
+    events.append((start[-1] + length + 1, 1, proj_sum()))
+    run_events(events)
 
     if not edge:
         r.gbt_out[0] = r.gbt[0]
@@ -402,7 +432,7 @@
     return jnp.asarray(head_of_row[:, None] == np.arange(C)[None, :] // HEAD, BF)
 
 
-def run_forward(places, tokens, cotangent, bias, row_ids, weights, halos=None, before=None, lons=8):
+def run_forward(places, tokens, cotangent, bias, region_ids, weights, halos=None, before=None, lons=8):
     levels, local_rows, cols, channels = tokens.shape
     blocks = levels // WLEV
     count = len(places)
@@ -416,7 +446,7 @@
         ("tok", tokens, by_level(tokens.shape, 0)),
         ("cot", cotangent, by_level(tokens.shape, 0)),
         ("bias", bias, pl.BlockSpec((1, bands, HEADS, M, M), lambda p: (p, 0, 0, 0, 0))),
-        ("ids", row_ids, pl.BlockSpec(memory_space=pltpu.SMEM)),
+        ("ids", region_ids, pl.BlockSpec(memory_space=pltpu.SMEM)),
         ("krow", jnp.asarray(cell_row[:, None]), whole((M, 1))),
         ("qrow", jnp.asarray(cell_row[lane_cell][None, :]), whole((1, LANES))),
         ("mask", head_mask(), whole((LANES, C))),
@@ -634,6 +664,34 @@
     return call(finish_kernel, blocks, ins, outs, scratch, "token_grads", 0.1, 60, parts, cols)
 
 
+def cut_kernel(ids_ref, tok_rows, cot_rows, tok_cols, cot_cols, lat_ref, lon_ref, corner_ref):
+    cell = lax.broadcasted_iota(jnp.int32, (16, C), 0)
+    for at, (rows, cols) in enumerate(((tok_rows, tok_cols), (cot_rows, cot_cols))):
+        lat_ref[at] = rows[...]
+        lon_ref[at] = cols[:, :, :HALO_COLS, :]
+        corner_ref[at] = cols[:, :HALF_LAT, :HALO_COLS, :]
+    for a in range(lat_ref.shape[1]):
+        for i in range(HALF_LAT):
+            first = tok_rows[a, i, 0:16, :].astype(F32)
+            lat_ref[0, a, i, 0:16, :] = jnp.where(cell == 0, ids_ref[i].astype(F32), first).astype(BF)
+
+
+def cut_halos(tokens, cotangent, region_ids):
+    levels, local_rows, cols, channels = tokens.shape
+    row_spec = pl.BlockSpec((levels, HALF_LAT, cols, C), lambda i: (0, 0, 0, 0))
+    col_spec = pl.BlockSpec((levels, local_rows, 16, C), lambda i: (0, 0, 0, 0))
+    shapes = ((2, levels, HALF_LAT, cols, C), (2, levels, local_rows, HALO_COLS, C), (2, levels, HALF_LAT, HALO_COLS, C))
+    return pl.pallas_call(
+        cut_kernel,
+        grid=(1,),
+        in_specs=[pl.BlockSpec(memory_space=pltpu.SMEM), row_spec, row_spec, col_spec, col_spec],
+        out_specs=[whole(shape) for shape in shapes],
+        out_shape=[jax.ShapeDtypeStruct(shape, BF) for shape in shapes],
+        compiler_params=pltpu.CompilerParams(vmem_limit_bytes=60 * 1024 * 1024),
+        name="cut_halos",
+    )(region_ids, tokens, cotangent, tokens, cotangent)
+
+
 def assemble_kernel(own_ref, lat_ref, lon_ref, corner_ref, out_ref):
     levels, local_rows, cols, channels = out_ref.shape
     keep = lax.broadcasted_iota(jnp.int32, (16, C), 0) >= HALF_LON
@@ -701,17 +759,17 @@
     proj_ref[...] = jnp.concatenate([tile(4), half_vp[:, 64:]], axis=1)
     for i in range(FF // 128):
         up_ref[:, 128 * i : 128 * (i + 1)] = tile(6 + i)
-        down_ref[128 * i : 128 * (i + 1), :] = tile(12 + i).T
+        down_ref[:, 128 * i : 128 * (i + 1)] = tile(12 + i)
     wide = in_ref[18 * C : 18 * C + 16, :].astype(F32) * scale
     gains_ref[...] = jnp.concatenate([wide[0:2, :], wide[8:10, :64]], axis=1)
 
 
 def unpack(packed, scale):
-    shapes = ((C, 3 * C), (C, C), (C, FF), (FF, C), (2, C))
+    shapes = ((C, 3 * C), (C, C), (C, FF), (C, FF), (2, C))
     return pl.pallas_call(
         functools.partial(unpack_kernel, scale),
         out_shape=[jax.ShapeDtypeStruct(s, F32) for s in shapes],
-        compiler_params=pltpu.CompilerParams(vmem_limit_bytes=60 * 1024 * 1024),
+        compiler_params=pltpu.CompilerParams(vmem_limit_bytes=32 * 1024 * 1024),
         name="unpack_sums",
     )(packed)
 
@@ -730,20 +788,12 @@
         ]
         return lax.ppermute(value, both, pairs)
 
-    def both_fields(cut):
-        return jnp.stack([cut(tokens), cut(cotangent)])
-
-    halos = (
-        perm(both_fields(lambda f: f[:, :HALF_LAT]), "lat", -1),
-        perm(both_fields(lambda f: f[:, :, :HALO_COLS]), "lon", -1),
-        corner_perm(both_fields(lambda f: f[:, :HALF_LAT, :HALO_COLS]), -1),
-    )
-    ids_in = perm(region_ids[:HALF_LAT], "lat", -1)
-    row_ids = jnp.concatenate([region_ids[HALF_LAT:], ids_in], axis=0)
-
-    weights = {"wqkv": w_qkv, "wp": w_proj, "wup": w_up, "wdown": w_down, "gains": norm_gains}
-    inner, sums = run_forward(INNER, tokens, cotangent, earth_bias, region_ids[HALF_LAT:], weights)
-    edge, sums = run_forward(EDGE, tokens, cotangent, earth_bias, row_ids, weights, halos, sums, lons)
+    lat_cut, lon_cut, corner_cut = cut_halos(tokens, cotangent, region_ids)
+    halos = (perm(lat_cut, "lat", -1), perm(lon_cut, "lon", -1), corner_perm(corner_cut, -1))
+
+    weights = {"wqkv": w_qkv, "wp": w_proj, "wup": w_up, "wdt": w_down.T, "gains": norm_gains}
+    inner, sums = run_forward(INNER, tokens, cotangent, earth_bias, region_ids, weights)
+    edge, sums = run_forward(EDGE, tokens, cotangent, earth_bias, region_ids, weights, halos, sums, lons)
 
     shares = lax.all_to_all(sums[2], "lon", 0, 0, tiled=True)
     states = (inner, edge)
@@ -754,12 +804,13 @@
     lat_in = perm(sent[0], "lat", 1)
     lon_in = perm(sent[1], "lon", 1)
     corner_in = corner_perm(sent[2], 1)
-    summed, own = lax.optimization_barrier((sum_pieces(pieces), own))
+    summed, lat_in, lon_in, corner_in = lax.optimization_barrier((sum_pieces(pieces), lat_in, lon_in, corner_in))
     packed = lax.all_to_all(summed, both, 0, 0, tiled=True).reshape(-1, 128)
     cell_count = levels * nrows * cols * devices
     weight_grads = unpack(packed, 1.0 / math.sqrt(cell_count))
     bias_total = sum_bias(shares, earth_bias.shape[:3] + (M // lons, M))
-    return (assemble(own, lat_in, lon_in, corner_in), *weight_grads, bias_total)
+    qkv, proj, up, down, gains = weight_grads
+    return (assemble(own, lat_in, lon_in, corner_in), qkv, proj, up, down.T, gains, bias_total)
 
 
 def solution(mesh):

time: 144 us -> 128 us (0.89)
  local copies, waits for them, and re-layouts: 9.75 us -> 2.04 us
  Pallas kernels: 66.2 us -> 59.4 us
  starting transfers between devices: 32 us -> 35.8 us
  waiting for transfers between devices: 32.9 us -> 29.2 us
    all_to_all x1, waiting for transfers between devices: 0.01 us -> 16.7 us  [local(): packed = lax.all_to_all(summed, both, 0, 0, tiled=True).reshape(-1, 128)]
    ppermute x2, waiting for transfers between devices: 14.6 us -> 1.28 us  [corner_perm(): return lax.ppermute(value, both, pairs)]
    pallas_call x4, Pallas kernels: 60.9 us -> 53.2 us  [call(): pl.pallas_call(functools.partial(kernel, names, *fixed), grid=(blocks,),...]
    all_to_all x1, waiting for transfers between devices: 12.4 us -> 6.53 us  [local(): pieces = lax.all_to_all(packed, both, 0, 0, tiled=True)]
    unnamed x25 -> x9, local copies, waits for them, and re-layouts: 6.2 us -> 2.04 us
    all_to_all x1, starting transfers between devices: 4.74 us -> 7.91 us  [local(): packed = lax.all_to_all(summed, both, 0, 0, tiled=True).reshape(-1, 128)]
    another operation x3 -> x0, local copies, waits for them, and re-layouts: 2.97 us -> none  [both_fields(): return jnp.stack([cut(tokens), cut(cotangent)])]
    pallas_call x0 -> x1, Pallas kernels: none -> 2.35 us  [cut_halos(): pl.pallas_call(cut_kernel, grid=(1,), in_specs=[pl.BlockSpec(memory_space...]
  transfers between devices with their start and end apart: 10 -> 9, of which waited for: 3 -> 4; matrix products, arithmetic and copies ran while one was open for 4% -> 1% of each run, Pallas kernels for 25% -> 27%
where the time goes in v3:
time: 128 us; the launch traced here: 127 us
  Pallas kernels  59.4 us (46%)
  starting transfers between devices  35.8 us (28%)
  waiting for transfers between devices  29.2 us (23%)
  local copies, waits for them, and re-layouts  2.04 us (2%)
    pallas_call x4, Pallas kernels, call(): pl.pallas_call(functools.partial(kernel, names, *fixed), grid=(blocks,),...  53.2 us
    all_to_all x1, waiting for transfers between devices, local(): packed = lax.all_to_all(summed, both, 0, 0, tiled=True).reshape(-1, 128)  16.7 us
    ppermute x2, starting transfers between devices, corner_perm(): return lax.ppermute(value, both, pairs)  10.6 us
    all_to_all x1, starting transfers between devices, local(): packed = lax.all_to_all(summed, both, 0, 0, tiled=True).reshape(-1, 128)  7.91 us
    all_to_all x1, starting transfers between devices, local(): pieces = lax.all_to_all(packed, both, 0, 0, tiled=True)  6.76 us
    ppermute x4, starting transfers between devices, perm(): return lax.ppermute(value, axis, pairs)  6.62 us
    all_to_all x1, waiting for transfers between devices, local(): pieces = lax.all_to_all(packed, both, 0, 0, tiled=True)  6.53 us
    all_to_all x1, waiting for transfers between devices, local(): shares = lax.all_to_all(sums[2], 'lon', 0, 0, tiled=True)  4.7 us
  transfers between devices with their start and end apart: 9, of which 4 were waited for; matrix products, arithmetic and copies ran while one was open for 1% of the time, Pallas kernels for 27%

profile of v3, /device:TPU:1, one launch (start us, length us, event | category | flops | bytes accessed | tf_op | source)
XLA Modules:
  0.0 127.3 jit_solution(14053002321561336385)
XLA Ops:
  0.6 2.3 %cut_halos.1 = (bf16[2,4,3,48,192]{4,3,2,1,0:T(8,128)(2,1)}, bf16[2,4,12,8,192]{4,3,2,1,0:T(8,128)(2,1)}, bf16[2,4,3,8,192]{4,3,2,1,0:T(8,128)(2,1)}) custom-call(s32[12]{0:T(128)} %refs_3_.3, bf16[4,12,48,192]{3,2,1,0:T(8,128)(2,1)} %refs_0_.3, bf16[4,12,48,192]{3,2,1,0:T(8,128)(2,1)} %refs_1_.3, bf16[4,12,48,192]{3,2,1,0:T(8,128)(2,1)} %refs_0_.3, ...), custom_call_target="tpu_custom_call" | custom-call | tf_op jit(solution)/shard_map/cut_halos/pallas_call | solution.py:684
  3.0 1.4 %collective-permute-start = (bf16[2,4,3,48,192]{4,3,2,1,0:T(8,128)(2,1)}, bf16[2,4,3,48,192]{4,3,2,1,0:T(8,128)(2,1)S(1)}, u32[]{:S(2)}, u32[]{:S(2)}) collective-permute-start(bf16[2,4,3,48,192]{4,3,2,1,0:T(8,128)(2,1)} %get-tuple-element.57), channel_id=1, source_target_pairs={{0,15},{1,0},{2,1},{3,2},{4,3},{5,4},{6,5},{7,6},{8,7},{9,8},{10,9... | collective-permute-start | bytes 1327112 | tf_op jit(solution)/shard_map/ppermute | solution.py:35
  4.4 9.3 %collective-permute-start.2 = (bf16[2,4,3,8,192]{4,3,2,1,0:T(8,128)(2,1)}, bf16[2,4,3,8,192]{4,3,2,1,0:T(8,128)(2,1)S(1)}, u32[]{:S(2)}, u32[]{:S(2)}) collective-permute-start(bf16[2,4,3,8,192]{4,3,2,1,0:T(8,128)(2,1)} %get-tuple-element.59), channel_id=1, source_target_pairs={{0,127},{1,112},{2,113},{3,114},{4,115},{5,116},{6,117},{7,118},{8... | collective-permute-start | bytes 221192 | tf_op jit(solution)/shard_map/ppermute | solution.py:789
  13.7 0.5 collective-permute-start.1
  14.2 14.4 %inner_windows.1 = (bf16[2,3,144,896]{3,2,1,0:T(8,128)(2,1)}, bf16[2,3,144,192]{3,2,1,0:T(8,128)(2,1)}, bf16[2,3,144,192]{3,2,1,0:T(8,128)(2,1)}, bf16[2,3,144,1...) custom-call(bf16[4,12,48,192]{3,2,1,0:T(8,128)(2,1)} %refs_0_.3, ...), custom_call_target="tpu_custom_call" | custom-call | flops 4200000000 | bytes 3000000 | tf_op jit(solution)/shard_map/inner_windows/pallas_call | solution.py:406
  28.6 0.0 collective-permute-done.2.refs_14_
  28.6 0.0 copy-start.3
  28.7 0.0 collective-permute-done.1.refs_13_
  28.7 0.0 copy-start.2
  28.7 0.0 collective-permute-done.refs_12_
  28.7 0.0 copy-start.1
  28.7 0.6 copy-done.3
  29.3 0.1 copy-done.2
  29.4 0.2 copy-done.1
  29.6 21.7 %edge_windows.1 = (bf16[2,5,144,896]{3,2,1,0:T(8,128)(2,1)}, bf16[2,5,144,192]{3,2,1,0:T(8,128)(2,1)}, bf16[2,5,144,192]{3,2,1,0:T(8,128)(2,1)}, bf16[2,5,144,19...) custom-call(bf16[4,12,48,192]{3,2,1,0:T(8,128)(2,1)} %refs_0_.3, ...), custom_call_target="tpu_custom_call" | custom-call | flops 7000000000 | bytes 5000000 | tf_op jit(solution)/shard_map/edge_windows/pallas_call | solution.py:406
  51.3 3.9 %all-to-all-start = ((bf16[8,2,2,128,128]{4,3,2,1,0:T(8,128)(2,1)}), bf16[8,2,2,128,128]{4,3,2,1,0:T(8,128)(2,1)S(1)}, u32[]{:S(2)}, u32[]{:S(2)}) async-start(bf16[8,2,2,128,128]{4,3,2,1,0:T(8,128)(2,1)} %get-tuple-element.78), calls=%async_computation | async-start | bytes 2097152 | tf_op jit(solution)/shard_map/all_to_all | solution.py:798
  55.2 10.1 %query_key_grads.1 = (bf16[2,3,144,192]{3,2,1,0:T(8,128)(2,1)}, bf16[2,3,144,192]{3,2,1,0:T(8,128)(2,1)}, bf16[2,5,144,192]{3,2,1,0:T(8,128)(2,1)}, bf16[2,5,144...) custom-call(bf16[2,3,144,896]{3,2,1,0:T(8,128)(2,1)} %get-tuple-element.53.refs_0_, ...), custom_call_target="tpu_custom_call" | custom-call | flops 4200000000 | bytes 3000000 | tf_op jit(solution)/shard_map/query_key_grads/pallas_call | solution.py:406
  65.4 4.7 %all-to-all-done.in_ref = bf16[8,2,2,128,128]{4,3,2,1,0:T(8,128)(2,1)S(1)} async-done(((bf16[8,2,2,128,128]{4,3,2,1,0:T(8,128)(2,1)}), bf16[8,2,2,128,128]{4,3,2,1,0:T(8,128)(2,1)S(1)}, u32[]{:S(2)}, u32[]{:S(2)}) %all-to-all-start) | async-done | bytes 1048608 | tf_op jit(solution)/shard_map/all_to_all | solution.py:798
  70.1 6.8 %all-to-all-start.1 = ((bf16[128,32,128]{2,1,0:T(8,128)(2,1)}), bf16[128,32,128]{2,1,0:T(8,128)(2,1)S(1)}, u32[]{:S(2)}, u32[]{:S(2)}) async-start(bf16[128,32,128]{2,1,0:T(8,128)(2,1)} %get-tuple-element.79), calls=%async_computation.1 | async-start | bytes 2097152 | tf_op jit(solution)/shard_map/all_to_all | solution.py:802
  76.8 6.9 %token_grads.1 = (bf16[4,12,48,192]{3,2,1,0:T(8,128)(2,1)}, bf16[4,3,48,192]{3,2,1,0:T(8,128)(2,1)}, bf16[4,12,8,192]{3,2,1,0:T(8,128)(2,1)}, bf16[4,3,8,192]{3,2,1,0:T(8,128)(2,1)}) custom-call(bf16[2,3,144,192]{3,2,1,0:T(8,128)(2,1)} %get-tuple-element.50.refs_4_.refs_0_, bf16[2,3,144,192]{3,2,1,0:T(8,128)(2,1)} %get-tuple-element.51.refs_1_, ...), custom_call_target="tpu_custom_call" | custom-call | flops 1400000000 | bytes 1000000 | tf_op jit(solution)/shard_map/token_grads/pallas_call | solution.py:406
  83.8 2.0 %collective-permute-start.3 = (bf16[4,3,48,192]{3,2,1,0:T(8,128)(2,1)}, bf16[4,3,48,192]{3,2,1,0:T(8,128)(2,1)S(1)}, u32[]{:S(2)}, u32[]{:S(2)}) collective-permute-start(bf16[4,3,48,192]{3,2,1,0:T(8,128)(2,1)} %get-tuple-element.80), channel_id=1, source_target_pairs={{0,1},{1,2},{2,3},{3,4},{4,5},{5,6},{6,7},{7,8},{8,9},{9,10},{10,1... | collective-permute-start | bytes 663560 | tf_op jit(solution)/shard_map/ppermute | solution.py:35
  85.7 2.7 %collective-permute-start.4 = (bf16[4,12,8,192]{3,2,1,0:T(8,128)(2,1)}, bf16[4,12,8,192]{3,2,1,0:T(8,128)(2,1)S(1)}, u32[]{:S(2)}, u32[]{:S(2)}) collective-permute-start(bf16[4,12,8,192]{3,2,1,0:T(8,128)(2,1)} %get-tuple-element.81), channel_id=1, source_target_pairs={{0,16},{16,32},{32,48},{48,64},{64,80},{80,96},{96,112},{112,0},{1... | collective-permute-start | bytes 442376 | tf_op jit(solution)/shard_map/ppermute | solution.py:35
  88.5 1.4 %collective-permute-start.5 = (bf16[4,3,8,192]{3,2,1,0:T(8,128)(2,1)}, bf16[4,3,8,192]{3,2,1,0:T(8,128)(2,1)S(1)}, u32[]{:S(2)}, u32[]{:S(2)}) collective-permute-start(bf16[4,3,8,192]{3,2,1,0:T(8,128)(2,1)} %get-tuple-element.82), channel_id=1, source_target_pairs={{0,17},{1,18},{2,19},{3,20},{4,21},{5,22},{6,23},{7,24},{8,25},{9,... | collective-permute-start | bytes 110600 | tf_op jit(solution)/shard_map/ppermute | solution.py:789
  89.8 6.5 %all-to-all-done.1.in_ref = bf16[128,32,128]{2,1,0:T(8,128)(2,1)S(1)} async-done(((bf16[128,32,128]{2,1,0:T(8,128)(2,1)}), bf16[128,32,128]{2,1,0:T(8,128)(2,1)S(1)}, u32[]{:S(2)}, u32[]{:S(2)}) %all-to-all-start.1) | async-done | bytes 1048608 | tf_op jit(solution)/shard_map/all_to_all | solution.py:802
  96.4 1.2 sum_pieces.1
  97.6 1.3 %collective-permute-done.5.corner_ref = bf16[4,3,8,192]{3,2,1,0:T(8,128)(2,1)S(1)} collective-permute-done((bf16[4,3,8,192]{3,2,1,0:T(8,128)(2,1)}, bf16[4,3,8,192]{3,2,1,0:T(8,128)(2,1)S(1)}, u32[]{:S(2)}, u32[]{:S(2)}) %collective-permute-start.5) | collective-permute-done | bytes 36896 | tf_op jit(solution)/shard_map/ppermute | solution.py:789
  98.8 0.0 collective-permute-done.4.lon_ref
  98.8 0.0 collective-permute-done.3.lat_ref
  98.9 7.9 %all-to-all-start.2 = ((bf16[128,32,128]{2,1,0:T(8,128)(2,1)}), bf16[128,32,128]{2,1,0:T(8,128)(2,1)S(1)}, u32[]{:S(2)}, u32[]{:S(2)}) async-start(bf16[128,32,128]{2,1,0:T(8,128)(2,1)} %sum_pieces.1), calls=%async_computation.2 | async-start | bytes 2097152 | tf_op jit(solution)/shard_map/all_to_all | solution.py:808
  106.8 0.0 copy-start
  106.8 0.2 sum_bias.1
  107.0 1.1 copy.23
  108.1 0.0 copy-done
  108.1 1.1 assemble.1
  109.2 16.7 %all-to-all-done.2 = bf16[128,32,128]{2,1,0:T(8,128)(2,1)S(1)} async-done(((bf16[128,32,128]{2,1,0:T(8,128)(2,1)}), bf16[128,32,128]{2,1,0:T(8,128)(2,1)S(1)}, u32[]{:S(2)}, u32[]{:S(2)}) %all-to-all-start.2) | async-done | bytes 1048608 | tf_op jit(solution)/shard_map/all_to_all | solution.py:808
  125.9 1.3 %unpack_sums.1 = (f32[192,576]{1,0:T(8,128)}, f32[192,192]{1,0:T(8,128)}, f32[192,768]{1,0:T(8,128)}, f32[192,768]{1,0:T(8,128)}, f32[2,192]{1,0:T(2,128)}) custom-call(bf16[4096,128]{1,0:T(8,128)(2,1)S(1)} %bitcast.3), custom_call_target="tpu_custom_call" | custom-call | tf_op jit(solution)/shard_map/unpack_sums/pallas_call | solution.py:769
Async XLA Ops:
  3.0 25.7 %collective-permute-start = (bf16[2,4,3,48,192]{4,3,2,1,0:T(8,128)(2,1)}, bf16[2,4,3,48,192]{4,3,2,1,0:T(8,128)(2,1)S(1)}, u32[]{:S(2)}, u32[]{:S(2)}) collective-permute-start(bf16[2,4,3,48,192]{4,3,2,1,0:T(8,128)(2,1)} %get-tuple-element.57), channel_id=1, source_target_pairs={{0,15},{1,0},{2,1},{3,2},{4,3},{5,4},{6,5},{7,6},{8,7},{9,8},{10,9... | collective-permute-start | bytes 1327112 | tf_op jit(solution)/shard_map/ppermute | solution.py:35
  4.4 24.2 %collective-permute-start.2 = (bf16[2,4,3,8,192]{4,3,2,1,0:T(8,128)(2,1)}, bf16[2,4,3,8,192]{4,3,2,1,0:T(8,128)(2,1)S(1)}, u32[]{:S(2)}, u32[]{:S(2)}) collective-permute-start(bf16[2,4,3,8,192]{4,3,2,1,0:T(8,128)(2,1)} %get-tuple-element.59), channel_id=1, source_target_pairs={{0,127},{1,112},{2,113},{3,114},{4,115},{5,116},{6,117},{7,118},{8... | collective-permute-start | bytes 221192 | tf_op jit(solution)/shard_map/ppermute | solution.py:789
  13.7 15.0 %collective-permute-start.1 = (bf16[2,4,12,8,192]{4,3,2,1,0:T(8,128)(2,1)}, bf16[2,4,12,8,192]{4,3,2,1,0:T(8,128)(2,1)S(1)}, u32[]{:S(2)}, u32[]{:S(2)}) collective-permute-start(bf16[2,4,12,8,192]{4,3,2,1,0:T(8,128)(2,1)} %get-tuple-element.58), channel_id=1, source_target_pairs={{0,112},{16,0},{32,16},{48,32},{64,48},{80,64},{96,80},{112,96},{1... | collective-permute-start | bytes 884744 | tf_op jit(solution)/shard_map/ppermute | solution.py:35
  28.6 0.6 copy-start.3
  28.7 0.7 copy-start.2
  28.7 0.9 copy-start.1
  51.3 18.7 %all-to-all-start = ((bf16[8,2,2,128,128]{4,3,2,1,0:T(8,128)(2,1)}), bf16[8,2,2,128,128]{4,3,2,1,0:T(8,128)(2,1)S(1)}, u32[]{:S(2)}, u32[]{:S(2)}) async-start(bf16[8,2,2,128,128]{4,3,2,1,0:T(8,128)(2,1)} %get-tuple-element.78), calls=%async_computation | async-start | bytes 2097152 | tf_op jit(solution)/shard_map/all_to_all | solution.py:798
  70.1 26.3 %all-to-all-start.1 = ((bf16[128,32,128]{2,1,0:T(8,128)(2,1)}), bf16[128,32,128]{2,1,0:T(8,128)(2,1)S(1)}, u32[]{:S(2)}, u32[]{:S(2)}) async-start(bf16[128,32,128]{2,1,0:T(8,128)(2,1)} %get-tuple-element.79), calls=%async_computation.1 | async-start | bytes 2097152 | tf_op jit(solution)/shard_map/all_to_all | solution.py:802
  83.8 15.1 %collective-permute-start.3 = (bf16[4,3,48,192]{3,2,1,0:T(8,128)(2,1)}, bf16[4,3,48,192]{3,2,1,0:T(8,128)(2,1)S(1)}, u32[]{:S(2)}, u32[]{:S(2)}) collective-permute-start(bf16[4,3,48,192]{3,2,1,0:T(8,128)(2,1)} %get-tuple-element.80), channel_id=1, source_target_pairs={{0,1},{1,2},{2,3},{3,4},{4,5},{5,6},{6,7},{7,8},{8,9},{9,10},{10,1... | collective-permute-start | bytes 663560 | tf_op jit(solution)/shard_map/ppermute | solution.py:35
  85.7 13.1 %collective-permute-start.4 = (bf16[4,12,8,192]{3,2,1,0:T(8,128)(2,1)}, bf16[4,12,8,192]{3,2,1,0:T(8,128)(2,1)S(1)}, u32[]{:S(2)}, u32[]{:S(2)}) collective-permute-start(bf16[4,12,8,192]{3,2,1,0:T(8,128)(2,1)} %get-tuple-element.81), channel_id=1, source_target_pairs={{0,16},{16,32},{32,48},{48,64},{64,80},{80,96},{96,112},{112,0},{1... | collective-permute-start | bytes 442376 | tf_op jit(solution)/shard_map/ppermute | solution.py:35
  88.5 10.4 %collective-permute-start.5 = (bf16[4,3,8,192]{3,2,1,0:T(8,128)(2,1)}, bf16[4,3,8,192]{3,2,1,0:T(8,128)(2,1)S(1)}, u32[]{:S(2)}, u32[]{:S(2)}) collective-permute-start(bf16[4,3,8,192]{3,2,1,0:T(8,128)(2,1)} %get-tuple-element.82), channel_id=1, source_target_pairs={{0,17},{1,18},{2,19},{3,20},{4,21},{5,22},{6,23},{7,24},{8,25},{9,... | collective-permute-start | bytes 110600 | tf_op jit(solution)/shard_map/ppermute | solution.py:789
  98.9 27.1 %all-to-all-start.2 = ((bf16[128,32,128]{2,1,0:T(8,128)(2,1)}), bf16[128,32,128]{2,1,0:T(8,128)(2,1)S(1)}, u32[]{:S(2)}, u32[]{:S(2)}) async-start(bf16[128,32,128]{2,1,0:T(8,128)(2,1)} %sum_pieces.1), calls=%async_computation.2 | async-start | bytes 2097152 | tf_op jit(solution)/shard_map/all_to_all | solution.py:808
  106.8 1.3 %copy-start = (bf16[4,12,48,192]{3,2,1,0:T(8,128)(2,1)S(1)}, bf16[4,12,48,192]{3,2,1,0:T(8,128)(2,1)}, u32[]{:S(2)}) copy-start(bf16[4,12,48,192]{3,2,1,0:T(8,128)(2,1)} %get-tuple-element.76.own_ref) | copy-start | bytes 2654212

commit v4 on v3

--- a/solution.py
+++ b/solution.py
@@ -63,19 +63,8 @@
 
 
 def gelu_parts(u):
+    cdf = 0.5 + 0.5 * lax.erf(u * inv_root_two)
     bell = jnp.exp2(u * u * (-0.5 * math.log2(math.e)))
-    under = 1.0 + jnp.abs(u) * (0.3275911 * inv_root_two)
-    t = pl.reciprocal(under, approx=True)
-    tail = t * (
-        0.5 * 0.254829592
-        + t
-        * (
-            0.5 * -0.284496736
-            + t * (0.5 * 1.421413741 + t * (0.5 * -1.453152027 + t * (0.5 * 1.061405429)))
-        )
-    )
-    tail = tail * bell
-    cdf = jnp.where(u >= 0.0, 1.0 - tail, tail)
     return cdf, cdf + u * (bell * inv_root_tau)
 
 
@@ -143,8 +132,24 @@
 HALO_COLS = 8
 
 
+HALO_ROWS = 3 * HALO_COLS
+
+
 class Refs:
     pass
+
+
+def pack(cells):
+    half = cells.shape[0] // 2
+    ends = jnp.concatenate([cells[:half, 128:], cells[half:, 128:]], axis=1)
+    return jnp.concatenate([cells[:, :128], ends], axis=0).astype(BF)
+
+
+def unpack_cells(packed):
+    packed = packed.astype(F32)
+    first = packed.shape[0] * 2 // 3
+    ends = jnp.concatenate([packed[first:, :64], packed[first:, 64:]], axis=0)
+    return jnp.concatenate([packed[:first], ends], axis=1)
 
 
 def named(names, refs):
@@ -206,14 +211,18 @@
                 for i in range(first, stop):
                     row = a * local_rows + i
                     r.own32[at, row * cols : (row + 1) * cols, :] = ref[a, i].astype(F32)
-                    if edge:
-                        r.lon32[at, row] = r.halo_lon[at, a, i].astype(F32)
                 yield None
+            for i in range(first, stop if edge else first):
+                both = unpack_cells(r.halo_lon[at, 0, i - HALF_LAT])
+                for a in range(WLEV):
+                    r.lon32[at, a * local_rows + i] = both[HALO_COLS * a : HALO_COLS * (a + 1)]
             if stop < first + WLAT:
-                r.lat32[at] = r.halo_lat[at].reshape(WLEV * HALF_LAT * cols, C).astype(F32)
-                for a in range(WLEV):
-                    for i in range(HALF_LAT):
-                        r.corner32[at, a * HALF_LAT + i] = r.halo_corner[at, a, i].astype(F32)
+                for i in range(HALF_LAT):
+                    both = unpack_cells(r.halo_corner[at, 0, i])
+                    for a in range(WLEV):
+                        row = a * HALF_LAT + i
+                        r.lat32[at, row * cols : (row + 1) * cols, :] = unpack_cells(r.halo_lat[at, a, i])
+                        r.corner32[at, row] = both[HALO_COLS * a : HALO_COLS * (a + 1)]
                 yield None
 
     def row_id(w, b):
@@ -538,10 +547,18 @@
 
     @pl.when(step == last_step)
     def _():
-        per = r.pack_out.shape[1]
+        per = r.keep_out.shape[1]
+        core = r.core[0]
+
+        def put_rows(half, at, rows):
+            for ref, here in ((r.keep_out, core == half), (r.send_out, core != half)):
+
+                @pl.when(here)
+                def _():
+                    ref[at : at + rows.shape[0]] = rows
 
         def put(i, tile):
-            r.pack_out[C // per * i : C // per * (i + 1)] = tile.astype(BF).reshape(C // per, per, 128)
+            put_rows(i // 9, C // per * (i % 9), tile.astype(BF).reshape(C // per, per, 128))
 
         small = (r.acc[0], r.acc[1], r.acc[2], r.proj[...])
         for i in range(2):
@@ -563,10 +580,11 @@
             [gains[:, :128], jnp.concatenate([gains[:, 128:], jnp.zeros((8, 64), F32)], axis=1)],
             axis=0,
         )
-        r.pack_out[18 * C // per, 0:16, :] = wide.astype(BF)
-
-
-def run_attention(states, sums, weights, devices):
+        wide = jnp.concatenate([wide, jnp.zeros((per - 16, 128), F32)], axis=0)
+        put_rows(0, 9 * C // per, wide.astype(BF)[None])
+
+
+def run_attention(states, sums, weights, core, chips):
     ins, outs = [], []
     blocks = states[0][0].shape[0]
     parts = [state[0].shape[1] for state in states]
@@ -584,13 +602,14 @@
         shape = (blocks, count, M, C)
         for name in ("dq_out", "dk_out"):
             outs.append((name + str(part), shape, BF, by_level(shape, 0)))
-    pack = (devices, 4096 // devices, 128)
-    outs.append(("pack_out", pack, BF, whole(pack)))
+    pack = (chips, 2048 // chips, 128)
+    outs += [("keep_out", pack, BF, whole(pack)), ("send_out", pack, BF, whole(pack))]
+    ins.append(("core", core, pl.BlockSpec(memory_space=pltpu.SMEM)))
     rows = sum(parts) * M
     scratch = [("acc", (3, C, C), F32), ("qbd", (4, LANES, C), BF)]
     scratch += [(name, (rows, C), BF) for name in ("h", "dq", "dk", "dv")]
     got = call(attention_kernel, blocks, ins, outs, scratch, "query_key_grads", 0.3, 60, parts)
-    return [got[0:2], got[2:4]], got[-1]
+    return [got[0:2], got[2:4]], got[4], got[5]
 
 
 def finish_kernel(names, parts, cols, *refs):
@@ -625,12 +644,15 @@
     for at in range(0, len(order), 2):
         in_turn(*[(4, window(at + i, *order[at + i])) for i in range(2)])
     r.gt_out[...] = r.own32[...].astype(BF).reshape(r.gt_out.shape)
-    r.lat_out[...] = r.lat32[...].astype(BF).reshape(r.lat_out.shape)
-    for a in range(WLEV):
-        for i in range(local_rows):
-            r.lon_out[a, i] = r.lon32[a * local_rows + i].astype(BF)
-        for i in range(HALF_LAT):
-            r.corner_out[a, i] = r.corner32[a * HALF_LAT + i].astype(BF)
+    for i in range(HALF_LAT):
+        for a in range(WLEV):
+            row = a * HALF_LAT + i
+            r.lat_out[a, i] = pack(r.lat32[row * cols : (row + 1) * cols, :])
+        r.corner_out[0, i] = pack(jnp.concatenate([r.corner32[a * HALF_LAT + i] for a in range(WLEV)], axis=0))
+    for i in range(HALF_LAT, local_rows):
+        r.lon_out[0, i - HALF_LAT] = pack(
+            jnp.concatenate([r.lon32[a * local_rows + i] for a in range(WLEV)], axis=0)
+        )
 
 
 def run_finish(parts, states, grads, weights, shape):
@@ -647,9 +669,9 @@
     outs = []
     for name, out in (
         ("gt_out", shape),
-        ("lat_out", (levels, HALF_LAT, cols, C)),
-        ("lon_out", (levels, local_rows, HALO_COLS, C)),
-        ("corner_out", (levels, HALF_LAT, HALO_COLS, C)),
+        ("lat_out", (levels, HALF_LAT, cols * 3 // 2, 128)),
+        ("lon_out", (blocks, local_rows - HALF_LAT, HALO_ROWS, 128)),
+        ("corner_out", (blocks, HALF_LAT, HALO_ROWS, 128)),
     ):
         outs.append((name, out, BF, by_level(out, 0)))
     count = sum(len(places) for places in parts)
@@ -665,22 +687,35 @@
 
 
 def cut_kernel(ids_ref, tok_rows, cot_rows, tok_cols, cot_cols, lat_ref, lon_ref, corner_ref):
-    cell = lax.broadcasted_iota(jnp.int32, (16, C), 0)
-    for at, (rows, cols) in enumerate(((tok_rows, tok_cols), (cot_rows, cot_cols))):
-        lat_ref[at] = rows[...]
-        lon_ref[at] = cols[:, :, :HALO_COLS, :]
-        corner_ref[at] = cols[:, :HALF_LAT, :HALO_COLS, :]
-    for a in range(lat_ref.shape[1]):
-        for i in range(HALF_LAT):
-            first = tok_rows[a, i, 0:16, :].astype(F32)
-            lat_ref[0, a, i, 0:16, :] = jnp.where(cell == 0, ids_ref[i].astype(F32), first).astype(BF)
+    levels, half_lat, cols, channels = tok_rows.shape
+    cell = lax.broadcasted_iota(jnp.int32, (cols, C), 0)
+    for at, (rows, columns) in enumerate(((tok_rows, tok_cols), (cot_rows, cot_cols))):
+        for a in range(levels):
+            for i in range(half_lat):
+                row = rows[a, i].astype(F32)
+                if at == 0:
+                    row = jnp.where(cell == 0, ids_ref[i].astype(F32), row)
+                lat_ref[at, a, i] = pack(row)
+        for p in range(levels // WLEV):
+            for i in range(columns.shape[1]):
+                both = [columns[WLEV * p + a, i, :HALO_COLS, :].astype(F32) for a in range(WLEV)]
+                both = pack(jnp.concatenate(both, axis=0))
+                if i < half_lat:
+                    corner_ref[at, p, i] = both
+                else:
+                    lon_ref[at, p, i - half_lat] = both
 
 
 def cut_halos(tokens, cotangent, region_ids):
     levels, local_rows, cols, channels = tokens.shape
     row_spec = pl.BlockSpec((levels, HALF_LAT, cols, C), lambda i: (0, 0, 0, 0))
     col_spec = pl.BlockSpec((levels, local_rows, 16, C), lambda i: (0, 0, 0, 0))
-    shapes = ((2, levels, HALF_LAT, cols, C), (2, levels, local_rows, HALO_COLS, C), (2, levels, HALF_LAT, HALO_COLS, C))
+    blocks = levels // WLEV
+    shapes = (
+        (2, levels, HALF_LAT, cols * 3 // 2, 128),
+        (2, blocks, local_rows - HALF_LAT, HALO_ROWS, 128),
+        (2, blocks, HALF_LAT, HALO_ROWS, 128),
+    )
     return pl.pallas_call(
         cut_kernel,
         grid=(1,),
@@ -696,13 +731,20 @@
     levels, local_rows, cols, channels = out_ref.shape
     keep = lax.broadcasted_iota(jnp.int32, (16, C), 0) >= HALF_LON
     pad = jnp.zeros((16 - HALO_COLS, C), F32)
-    for a in range(levels):
+    for p in range(levels // WLEV):
         for i in range(local_rows):
-            row = own_ref.at[a, i] if i >= HALF_LAT else lat_ref.at[a, i]
-            left = lon_ref[a, i] if i >= HALF_LAT else corner_ref[a, i]
-            left = jnp.concatenate([left.astype(F32), pad], axis=0)
-            out_ref[a, i, 0:16, :] = jnp.where(keep, row[0:16, :].astype(F32), left).astype(BF)
-            out_ref[a, i, 16:, :] = row[16:, :]
+            both = unpack_cells(corner_ref[p, i] if i < HALF_LAT else lon_ref[p, i - HALF_LAT])
+            for a in range(WLEV):
+                level = WLEV * p + a
+                left = jnp.concatenate([both[HALO_COLS * a : HALO_COLS * (a + 1)], pad], axis=0)
+                if i < HALF_LAT:
+                    row = unpack_cells(lat_ref[level, i])
+                    out_ref[level, i, 16:, :] = row[16:].astype(BF)
+                    first = row[:16]
+                else:
+                    out_ref[level, i, 16:, :] = own_ref[level, i, 16:, :]
+                    first = own_ref[level, i, 0:16, :].astype(F32)
+                out_ref[level, i, 0:16, :] = jnp.where(keep, first, left).astype(BF)
 
 
 def assemble(own, *received):
@@ -748,9 +790,13 @@
     )(pieces)
 
 
-def unpack_kernel(scale, in_ref, qkv_ref, proj_ref, up_ref, down_ref, gains_ref):
+def unpack_kernel(scale, core_ref, mine_ref, theirs_ref, qkv_ref, proj_ref, up_ref, down_ref, gains_ref, in_ref):
+    core = core_ref[0]
+    in_ref[core] = mine_ref[...]
+    in_ref[1 - core] = theirs_ref[...]
+
     def tile(i):
-        return in_ref[C * i : C * (i + 1), :].astype(F32) * scale
+        return in_ref[i // 9, C * (i % 9) : C * (i % 9 + 1), :].astype(F32) * scale
 
     half_qk, half_vp = tile(2), tile(5)
     qkv_ref[...] = jnp.concatenate(
@@ -760,18 +806,20 @@
     for i in range(FF // 128):
         up_ref[:, 128 * i : 128 * (i + 1)] = tile(6 + i)
         down_ref[:, 128 * i : 128 * (i + 1)] = tile(12 + i)
-    wide = in_ref[18 * C : 18 * C + 16, :].astype(F32) * scale
+    wide = in_ref[0, 9 * C : 9 * C + 16, :].astype(F32) * scale
     gains_ref[...] = jnp.concatenate([wide[0:2, :], wide[8:10, :64]], axis=1)
 
 
-def unpack(packed, scale):
+def unpack(core, mine, theirs, scale):
     shapes = ((C, 3 * C), (C, C), (C, FF), (C, FF), (2, C))
     return pl.pallas_call(
         functools.partial(unpack_kernel, scale),
         out_shape=[jax.ShapeDtypeStruct(s, F32) for s in shapes],
+        in_specs=[pl.BlockSpec(memory_space=pltpu.SMEM), pl.BlockSpec(memory_space=pltpu.VMEM), pl.BlockSpec(memory_space=pltpu.VMEM)],
+        scratch_shapes=[pltpu.VMEM((2,) + mine.shape, BF)],
         compiler_params=pltpu.CompilerParams(vmem_limit_bytes=32 * 1024 * 1024),
         name="unpack_sums",
-    )(packed)
+    )(core, mine, theirs)
 
 
 def local(tokens, cotangent, region_ids, norm_gains, w_qkv, w_proj, w_up, w_down, earth_bias):
@@ -797,17 +845,27 @@
 
     shares = lax.all_to_all(sums[2], "lon", 0, 0, tiled=True)
     states = (inner, edge)
-    grads, packed = run_attention(states, sums, weights, devices)
-    packed, shares = lax.optimization_barrier((packed, shares))
-    pieces = lax.all_to_all(packed, both, 0, 0, tiled=True)
+    core = lax.rem(lax.axis_index("lat"), 2)[None]
+    cores = [[d for d in range(devices) if d % 2 == c] for c in range(2)]
+
+    def other_core(value):
+        return lax.ppermute(value, "lat", [(i, i ^ 1) for i in range(lats)])
+
+    def exchange(value):
+        return lax.all_to_all(value, both, 0, 0, axis_index_groups=cores, tiled=True)
+
+    grads, keep, send = run_attention(states, sums, weights, core, devices // 2)
+    packed = (keep.astype(F32) + other_core(send).astype(F32)).astype(BF)
     own, *sent = run_finish((INNER, EDGE), states, grads, weights, tokens.shape)
+    packed, shares, own, *sent = lax.optimization_barrier((packed, shares, own, *sent))
+    pieces = exchange(packed)
     lat_in = perm(sent[0], "lat", 1)
     lon_in = perm(sent[1], "lon", 1)
     corner_in = corner_perm(sent[2], 1)
     summed, lat_in, lon_in, corner_in = lax.optimization_barrier((sum_pieces(pieces), lat_in, lon_in, corner_in))
-    packed = lax.all_to_all(summed, both, 0, 0, tiled=True).reshape(-1, 128)
+    mine = exchange(summed).reshape(-1, 128)
     cell_count = levels * nrows * cols * devices
-    weight_grads = unpack(packed, 1.0 / math.sqrt(cell_count))
+    weight_grads = unpack(core, mine, other_core(mine), 1.0 / math.sqrt(cell_count))
     bias_total = sum_bias(shares, earth_bias.shape[:3] + (M // lons, M))
     qkv, proj, up, down, gains = weight_grads
     return (assemble(own, lat_in, lon_in, corner_in), qkv, proj, up, down.T, gains, bias_total)

time: 128 us -> 120 us (0.938)
  blocking collectives: 0 us -> 20.5 us
  waiting for transfers between devices: 29.2 us -> 8.81 us
  starting transfers between devices: 35.8 us -> 30.1 us
  Pallas kernels: 59.4 us -> 57.1 us
    all_to_all x0 -> x1, blocking collectives: none -> 20.5 us  [exchange(): lax.all_to_all(value, both, 0, 0, axis_index_groups=cores, tiled=True)]
    all_to_all x2 -> x1, waiting for transfers between devices: 23.2 us -> 7.48 us  [exchange(): lax.all_to_all(value, both, 0, 0, axis_index_groups=cores, tiled=True)]
    all_to_all x2 -> x1, starting transfers between devices: 14.7 us -> 8.04 us  [exchange(): lax.all_to_all(value, both, 0, 0, axis_index_groups=cores, tiled=True)]
    all_to_all x1, waiting for transfers between devices: 4.7 us -> 0.01 us  [local(): shares = lax.all_to_all(sums[2], 'lon', 0, 0, tiled=True)]
    pallas_call x4, Pallas kernels: 53.2 us -> 51.9 us  [call(): pl.pallas_call(functools.partial(kernel, names, *fixed), grid=(blocks,),...]
  transfers between devices with their start and end apart: 9 -> 10, of which waited for: 4 -> 2; matrix products, arithmetic and copies ran while one was open for 1% -> 2% of each run, Pallas kernels for 27% -> 27%
where the time goes in v4:
time: 120 us
  Pallas kernels  57.1 us (48%)
  starting transfers between devices  30.1 us (25%)
  blocking collectives  20.5 us (17%)
  waiting for transfers between devices  8.81 us (7%)
  local copies, waits for them, and re-layouts  1.94 us (2%)
    pallas_call x4, Pallas kernels, call(): pl.pallas_call(functools.partial(kernel, names, *fixed), grid=(blocks,),...  51.9 us
    all_to_all x1, blocking collectives, exchange(): lax.all_to_all(value, both, 0, 0, axis_index_groups=cores, tiled=True)  20.5 us
    ppermute x2, starting transfers between devices, corner_perm(): return lax.ppermute(value, both, pairs)  10.5 us
    all_to_all x1, starting transfers between devices, exchange(): lax.all_to_all(value, both, 0, 0, axis_index_groups=cores, tiled=True)  8.04 us
    all_to_all x1, waiting for transfers between devices, exchange(): lax.all_to_all(value, both, 0, 0, axis_index_groups=cores, tiled=True)  7.48 us
    ppermute x4, starting transfers between devices, perm(): return lax.ppermute(value, axis, pairs)  6.2 us
    all_to_all x1, starting transfers between devices, local(): shares = lax.all_to_all(sums[2], 'lon', 0, 0, tiled=True)  4.09 us
  transfers between devices with their start and end apart: 10, of which 2 were waited for; matrix products, arithmetic and copies ran while one was open for 2% of the time, Pallas kernels for 27%

profile of v4, /device:TPU:1, one launch (start us, length us, event | category | flops | bytes accessed | tf_op | source)
XLA Modules:
  0.0 120.1 jit_solution(10219687713074894624)
XLA Ops:
  0.6 2.3 %cut_halos.1 = (bf16[2,4,3,72,128]{4,3,2,1,0:T(8,128)(2,1)}, bf16[2,2,9,24,128]{4,3,2,1,0:T(8,128)(2,1)}, bf16[2,2,3,24,128]{4,3,2,1,0:T(8,128)(2,1)}) custom-call(s32[12]{0:T(128)} %refs_3_.3, bf16[4,12,48,192]{3,2,1,0:T(8,128)(2,1)} %refs_0_.3, bf16[4,12,48,192]{3,2,1,0:T(8,128)(2,1)} %refs_1_.3, bf16[4,12,48,192]{3,2,1,0:T(8,128)(2,1)} %refs_0_.3, ...), custom_call_target="tpu_custom_call" | custom-call | tf_op jit(solution)/shard_map/cut_halos/pallas_call | solution.py:719
  2.9 1.4 %collective-permute-start = (bf16[2,4,3,72,128]{4,3,2,1,0:T(8,128)(2,1)}, bf16[2,4,3,72,128]{4,3,2,1,0:T(8,128)(2,1)S(1)}, u32[]{:S(2)}, u32[]{:S(2)}) collective-permute-start(bf16[2,4,3,72,128]{4,3,2,1,0:T(8,128)(2,1)} %get-tuple-element.60), channel_id=1, source_target_pairs={{0,15},{1,0},{2,1},{3,2},{4,3},{5,4},{6,5},{7,6},{8,7},{9,8},{10,9... | collective-permute-start | bytes 1327112 | tf_op jit(solution)/shard_map/ppermute | solution.py:35
  4.4 9.3 %collective-permute-start.2 = (bf16[2,2,3,24,128]{4,3,2,1,0:T(8,128)(2,1)}, bf16[2,2,3,24,128]{4,3,2,1,0:T(8,128)(2,1)S(1)}, u32[]{:S(2)}, u32[]{:S(2)}) collective-permute-start(bf16[2,2,3,24,128]{4,3,2,1,0:T(8,128)(2,1)} %get-tuple-element.62), channel_id=1, source_target_pairs={{0,127},{1,112},{2,113},{3,114},{4,115},{5,116},{6,117},{7,118},{8... | collective-permute-start | bytes 221192 | tf_op jit(solution)/shard_map/ppermute | solution.py:837
  13.6 0.5 collective-permute-start.1
  14.1 13.9 %inner_windows.1 = (bf16[2,3,144,896]{3,2,1,0:T(8,128)(2,1)}, bf16[2,3,144,192]{3,2,1,0:T(8,128)(2,1)}, bf16[2,3,144,192]{3,2,1,0:T(8,128)(2,1)}, bf16[2,3,144,1...) custom-call(bf16[4,12,48,192]{3,2,1,0:T(8,128)(2,1)} %refs_0_.3, ...), custom_call_target="tpu_custom_call" | custom-call | flops 4200000000 | bytes 3000000 | tf_op jit(solution)/shard_map/inner_windows/pallas_call | solution.py:415
  28.1 0.0 collective-permute-done.2.refs_14_
  28.1 0.0 copy-start.6
  28.1 0.0 collective-permute-done.1.refs_13_
  28.1 0.0 copy-start.3
  28.1 0.0 collective-permute-done.refs_12_
  28.1 0.0 copy-start.2
  28.1 0.6 copy-done.6
  28.7 0.1 copy-done.3
  28.8 0.1 copy-done.2
  28.9 20.5 %edge_windows.1 = (bf16[2,5,144,896]{3,2,1,0:T(8,128)(2,1)}, bf16[2,5,144,192]{3,2,1,0:T(8,128)(2,1)}, bf16[2,5,144,192]{3,2,1,0:T(8,128)(2,1)}, bf16[2,5,144,19...) custom-call(bf16[4,12,48,192]{3,2,1,0:T(8,128)(2,1)} %refs_0_.3, ...), custom_call_target="tpu_custom_call" | custom-call | flops 7000000000 | bytes 5000000 | tf_op jit(solution)/shard_map/edge_windows/pallas_call | solution.py:415
  49.4 4.1 %all-to-all-start = ((bf16[8,2,2,128,128]{4,3,2,1,0:T(8,128)(2,1)}), bf16[8,2,2,128,128]{4,3,2,1,0:T(8,128)(2,1)S(1)}, u32[]{:S(2)}, u32[]{:S(2)}) async-start(bf16[8,2,2,128,128]{4,3,2,1,0:T(8,128)(2,1)} %get-tuple-element.75), calls=%async_computation | async-start | bytes 2097152 | tf_op jit(solution)/shard_map/all_to_all | solution.py:846
  53.5 10.4 %query_key_grads.1 = (bf16[2,3,144,192]{3,2,1,0:T(8,128)(2,1)}, bf16[2,3,144,192]{3,2,1,0:T(8,128)(2,1)}, bf16[2,5,144,192]{3,2,1,0:T(8,128)(2,1)}, bf16[2,5,144...) custom-call(bf16[2,3,144,896]{3,2,1,0:T(8,128)(2,1)} %get-tuple-element.55.refs_0_, ...), custom_call_target="tpu_custom_call" | custom-call | flops 4200000000 | bytes 3000000 | tf_op jit(solution)/shard_map/query_key_grads/pallas_call | solution.py:415
  64.0 0.2 collective-permute-start.3
  64.2 0.0 copy-start.1
  64.2 7.1 %token_grads.1 = (bf16[4,12,48,192]{3,2,1,0:T(8,128)(2,1)}, bf16[4,3,72,128]{3,2,1,0:T(8,128)(2,1)}, bf16[2,9,24,128]{3,2,1,0:T(8,128)(2,1)}, bf16[2,3,24,128]{3,2,1,0:T(8,128)(2,1)}) custom-call(bf16[2,3,144,192]{3,2,1,0:T(8,128)(2,1)} %get-tuple-element.59.refs_4_.refs_0_, bf16[2,3,144,192]{3,2,1,0:T(8,128)(2,1)} %get-tuple-element.76.refs_1_, ...), custom_call_target="tpu_custom_call" | custom-call | flops 1400000000 | bytes 1000000 | tf_op jit(solution)/shard_map/token_grads/pallas_call | solution.py:415
  71.3 0.0 collective-permute-done.3
  71.3 0.0 copy-done.1
  71.3 0.0 copy-start.4
  71.3 0.0 copy-start.5
  71.3 0.0 copy-start.7
  71.3 0.9 add_convert_fusion
  72.3 0.0 all-to-all-done.in_ref
  72.3 8.0 %all-to-all-start.1 = ((bf16[64,32,128]{2,1,0:T(8,128)(2,1)}), bf16[64,32,128]{2,1,0:T(8,128)(2,1)S(1)}, u32[]{:S(2)}, u32[]{:S(2)}) async-start(bf16[64,32,128]{2,1,0:T(8,128)(2,1)} %add_convert_fusion), calls=%async_computation.1 | async-start | bytes 1048576 | tf_op jit(solution)/shard_map/all_to_all | solution.py:855
  80.3 0.0 copy-done.4
  80.3 1.6 %collective-permute-start.4 = (bf16[4,3,72,128]{3,2,1,0:T(8,128)(2,1)S(1)}, bf16[4,3,72,128]{3,2,1,0:T(8,128)(2,1)S(1)}, u32[]{:S(2)}, u32[]{:S(2)}) collective-permute-start(bf16[4,3,72,128]{3,2,1,0:T(8,128)(2,1)S(1)} %copy-done.4), channel_id=1, source_target_pairs={{0,1},{1,2},{2,3},{3,4},{4,5},{5,6},{6,7},{7,8},{8,9},{9,10},{10,1... | collective-permute-start | bytes 663560 | tf_op jit(solution)/shard_map/ppermute | solution.py:35
  81.9 0.0 copy-done.5
  81.9 2.7 %collective-permute-start.5 = (bf16[2,9,24,128]{3,2,1,0:T(8,128)(2,1)S(1)}, bf16[2,9,24,128]{3,2,1,0:T(8,128)(2,1)S(1)}, u32[]{:S(2)}, u32[]{:S(2)}) collective-permute-start(bf16[2,9,24,128]{3,2,1,0:T(8,128)(2,1)S(1)} %copy-done.5), channel_id=1, source_target_pairs={{0,16},{16,32},{32,48},{48,64},{64,80},{80,96},{96,112},{112,0},{1... | collective-permute-start | bytes 331784 | tf_op jit(solution)/shard_map/ppermute | solution.py:35
  84.6 0.0 copy-done.7
  84.6 1.3 %collective-permute-start.6 = (bf16[2,3,24,128]{3,2,1,0:T(8,128)(2,1)S(1)}, bf16[2,3,24,128]{3,2,1,0:T(8,128)(2,1)S(1)}, u32[]{:S(2)}, u32[]{:S(2)}) collective-permute-start(bf16[2,3,24,128]{3,2,1,0:T(8,128)(2,1)S(1)} %copy-done.7), channel_id=1, source_target_pairs={{0,17},{1,18},{2,19},{3,20},{4,21},{5,22},{6,23},{7,24},{8,25},{9,... | collective-permute-start | bytes 110600 | tf_op jit(solution)/shard_map/ppermute | solution.py:837
  85.9 7.5 %all-to-all-done.1.in_ref = bf16[64,32,128]{2,1,0:T(8,128)(2,1)S(1)} async-done(((bf16[64,32,128]{2,1,0:T(8,128)(2,1)}), bf16[64,32,128]{2,1,0:T(8,128)(2,1)S(1)}, u32[]{:S(2)}, u32[]{:S(2)}) %all-to-all-start.1) | async-done | bytes 524320 | tf_op jit(solution)/shard_map/all_to_all | solution.py:855
  93.4 0.1 sum_pieces.1
  93.5 1.3 %collective-permute-done.6.corner_ref = bf16[2,3,24,128]{3,2,1,0:T(8,128)(2,1)S(1)} collective-permute-done((bf16[2,3,24,128]{3,2,1,0:T(8,128)(2,1)S(1)}, bf16[2,3,24,128]{3,2,1,0:T(8,128)(2,1)S(1)}, u32[]{:S(2)}, u32[]{:S(2)}) %collective-permute-start.6) | collective-permute-done | bytes 36896 | tf_op jit(solution)/shard_map/ppermute | solution.py:837
  94.8 0.0 collective-permute-done.5.lon_ref
  94.8 0.0 collective-permute-done.4.lat_ref
  94.8 20.5 %all_to_all.15 = bf16[64,32,128]{2,1,0:T(8,128)(2,1)S(1)} all-to-all(bf16[64,32,128]{2,1,0:T(8,128)(2,1)S(1)} %sum_pieces.1), channel_id=1, replica_groups={{0,2,4,6,8,10,12,14,16,18,20,22,24,26,28,30,32,34,36,38,40,42,44,46,48,..., dimensions={0} | all-to-all | bytes 1048576 | tf_op jit(solution)/shard_map/all_to_all | solution.py:855
  115.3 0.0 copy-start
  115.3 1.0 collective-permute-start.7
  116.2 0.2 sum_bias.1
  116.5 1.1 copy.23
  117.6 0.0 copy-done
  117.6 1.1 assemble.1
  118.7 0.0 collective-permute-done.7.theirs_ref
  118.7 1.4 %unpack_sums.1 = (f32[192,576]{1,0:T(8,128)}, f32[192,192]{1,0:T(8,128)}, f32[192,768]{1,0:T(8,128)}, f32[192,768]{1,0:T(8,128)}, f32[2,192]{1,0:T(2,128)}) custom-call(s32[1]{0:T(128)} %bitcast.1.refs_16_.core_ref, bf16[2048,128]{1,0:T(8,128)(2,1)S(1)} %bitcast.5, bf16[2048,128]{1,0:T(8,128)(2,1)S(1)} %collective-permute-done.7.theirs_ref), custom_call_target="tpu_custom_call" | custom-call | tf_op jit(solution)/shard_map/unpack_sums/pallas_call | solution.py:815
Async XLA Ops:
  2.9 25.2 %collective-permute-start = (bf16[2,4,3,72,128]{4,3,2,1,0:T(8,128)(2,1)}, bf16[2,4,3,72,128]{4,3,2,1,0:T(8,128)(2,1)S(1)}, u32[]{:S(2)}, u32[]{:S(2)}) collective-permute-start(bf16[2,4,3,72,128]{4,3,2,1,0:T(8,128)(2,1)} %get-tuple-element.60), channel_id=1, source_target_pairs={{0,15},{1,0},{2,1},{3,2},{4,3},{5,4},{6,5},{7,6},{8,7},{9,8},{10,9... | collective-permute-start | bytes 1327112 | tf_op jit(solution)/shard_map/ppermute | solution.py:35
  4.4 23.7 %collective-permute-start.2 = (bf16[2,2,3,24,128]{4,3,2,1,0:T(8,128)(2,1)}, bf16[2,2,3,24,128]{4,3,2,1,0:T(8,128)(2,1)S(1)}, u32[]{:S(2)}, u32[]{:S(2)}) collective-permute-start(bf16[2,2,3,24,128]{4,3,2,1,0:T(8,128)(2,1)} %get-tuple-element.62), channel_id=1, source_target_pairs={{0,127},{1,112},{2,113},{3,114},{4,115},{5,116},{6,117},{7,118},{8... | collective-permute-start | bytes 221192 | tf_op jit(solution)/shard_map/ppermute | solution.py:837
  13.6 14.5 %collective-permute-start.1 = (bf16[2,2,9,24,128]{4,3,2,1,0:T(8,128)(2,1)}, bf16[2,2,9,24,128]{4,3,2,1,0:T(8,128)(2,1)S(1)}, u32[]{:S(2)}, u32[]{:S(2)}) collective-permute-start(bf16[2,2,9,24,128]{4,3,2,1,0:T(8,128)(2,1)} %get-tuple-element.61), channel_id=1, source_target_pairs={{0,112},{16,0},{32,16},{48,32},{64,48},{80,64},{96,80},{112,96},{1... | collective-permute-start | bytes 663560 | tf_op jit(solution)/shard_map/ppermute | solution.py:35
  28.1 0.6 copy-start.6
  28.1 0.7 copy-start.3
  28.1 0.8 copy-start.2
  49.4 22.8 %all-to-all-start = ((bf16[8,2,2,128,128]{4,3,2,1,0:T(8,128)(2,1)}), bf16[8,2,2,128,128]{4,3,2,1,0:T(8,128)(2,1)S(1)}, u32[]{:S(2)}, u32[]{:S(2)}) async-start(bf16[8,2,2,128,128]{4,3,2,1,0:T(8,128)(2,1)} %get-tuple-element.75), calls=%async_computation | async-start | bytes 2097152 | tf_op jit(solution)/shard_map/all_to_all | solution.py:846
  64.0 7.3 %collective-permute-start.3 = (bf16[64,32,128]{2,1,0:T(8,128)(2,1)}, bf16[64,32,128]{2,1,0:T(8,128)(2,1)S(1)}, u32[]{:S(2)}, u32[]{:S(2)}) collective-permute-start(bf16[64,32,128]{2,1,0:T(8,128)(2,1)} %get-tuple-element.74), channel_id=1, source_target_pairs={{0,1},{1,0},{2,3},{3,2},{4,5},{5,4},{6,7},{7,6},{8,9},{9,8},{10,11... | collective-permute-start | bytes 1572872 | tf_op jit(solution)/shard_map/ppermute | solution.py:852
  64.2 7.1 %copy-start.1 = (bf16[64,32,128]{2,1,0:T(8,128)(2,1)S(1)}, bf16[64,32,128]{2,1,0:T(8,128)(2,1)}, u32[]{:S(2)}) copy-start(bf16[64,32,128]{2,1,0:T(8,128)(2,1)} %get-tuple-element.73) | copy-start | bytes 1572868
  71.3 9.0 %copy-start.4 = (bf16[4,3,72,128]{3,2,1,0:T(8,128)(2,1)S(1)}, bf16[4,3,72,128]{3,2,1,0:T(8,128)(2,1)}, u32[]{:S(2)}) copy-start(bf16[4,3,72,128]{3,2,1,0:T(8,128)(2,1)} %get-tuple-element.90) | copy-start | bytes 663556
  71.3 10.6 %copy-start.5 = (bf16[2,9,24,128]{3,2,1,0:T(8,128)(2,1)S(1)}, bf16[2,9,24,128]{3,2,1,0:T(8,128)(2,1)}, u32[]{:S(2)}) copy-start(bf16[2,9,24,128]{3,2,1,0:T(8,128)(2,1)} %get-tuple-element.91) | copy-start | bytes 331780
  71.3 13.3 %copy-start.7 = (bf16[2,3,24,128]{3,2,1,0:T(8,128)(2,1)S(1)}, bf16[2,3,24,128]{3,2,1,0:T(8,128)(2,1)}, u32[]{:S(2)}) copy-start(bf16[2,3,24,128]{3,2,1,0:T(8,128)(2,1)} %get-tuple-element.92) | copy-start | bytes 110596
  72.3 21.1 %all-to-all-start.1 = ((bf16[64,32,128]{2,1,0:T(8,128)(2,1)}), bf16[64,32,128]{2,1,0:T(8,128)(2,1)S(1)}, u32[]{:S(2)}, u32[]{:S(2)}) async-start(bf16[64,32,128]{2,1,0:T(8,128)(2,1)} %add_convert_fusion), calls=%async_computation.1 | async-start | bytes 1048576 | tf_op jit(solution)/shard_map/all_to_all | solution.py:855
  80.3 14.5 %collective-permute-start.4 = (bf16[4,3,72,128]{3,2,1,0:T(8,128)(2,1)S(1)}, bf16[4,3,72,128]{3,2,1,0:T(8,128)(2,1)S(1)}, u32[]{:S(2)}, u32[]{:S(2)}) collective-permute-start(bf16[4,3,72,128]{3,2,1,0:T(8,128)(2,1)S(1)} %copy-done.4), channel_id=1, source_target_pairs={{0,1},{1,2},{2,3},{3,4},{4,5},{5,6},{6,7},{7,8},{8,9},{9,10},{10,1... | collective-permute-start | bytes 663560 | tf_op jit(solution)/shard_map/ppermute | solution.py:35
  81.9 12.9 %collective-permute-start.5 = (bf16[2,9,24,128]{3,2,1,0:T(8,128)(2,1)S(1)}, bf16[2,9,24,128]{3,2,1,0:T(8,128)(2,1)S(1)}, u32[]{:S(2)}, u32[]{:S(2)}) collective-permute-start(bf16[2,9,24,128]{3,2,1,0:T(8,128)(2,1)S(1)} %copy-done.5), channel_id=1, source_target_pairs={{0,16},{16,32},{32,48},{48,64},{64,80},{80,96},{96,112},{112,0},{1... | collective-permute-start | bytes 331784 | tf_op jit(solution)/shard_map/ppermute | solution.py:35
  84.6 10.2 %collective-permute-start.6 = (bf16[2,3,24,128]{3,2,1,0:T(8,128)(2,1)S(1)}, bf16[2,3,24,128]{3,2,1,0:T(8,128)(2,1)S(1)}, u32[]{:S(2)}, u32[]{:S(2)}) collective-permute-start(bf16[2,3,24,128]{3,2,1,0:T(8,128)(2,1)S(1)} %copy-done.7), channel_id=1, source_target_pairs={{0,17},{1,18},{2,19},{3,20},{4,21},{5,22},{6,23},{7,24},{8,25},{9,... | collective-permute-start | bytes 110600 | tf_op jit(solution)/shard_map/ppermute | solution.py:837
  115.3 2.3 %copy-start = (bf16[4,12,48,192]{3,2,1,0:T(8,128)(2,1)S(1)}, bf16[4,12,48,192]{3,2,1,0:T(8,128)(2,1)}, u32[]{:S(2)}) copy-start(bf16[4,12,48,192]{3,2,1,0:T(8,128)(2,1)} %get-tuple-element.88.own_ref) | copy-start | bytes 2654212
  115.3 3.5 %collective-permute-start.7 = (bf16[2048,128]{1,0:T(8,128)(2,1)S(1)}, bf16[2048,128]{1,0:T(8,128)(2,1)S(1)}, u32[]{:S(2)}, u32[]{:S(2)}) collective-permute-start(bf16[2048,128]{1,0:T(8,128)(2,1)S(1)} %bitcast.4), channel_id=1, source_target_pairs={{0,1},{1,0},{2,3},{3,2},{4,5},{5,4},{6,7},{7,6},{8,9},{9,8},{10,11... | collective-permute-start | bytes 1572872 | tf_op jit(solution)/shard_map/ppermute | solution.py:852

commit v5 on v4

--- a/solution.py
+++ b/solution.py
@@ -123,7 +123,6 @@
         tick += 1
 
 
-STAGGER = 3
 INNER = ((0, 0), (0, 1), (0, 2))
 EDGE = ((0, 3), (1, 0), (1, 1), (1, 2), (1, 3))
 STATE = ("ds", "q", "k", "h", "dv", "xb", "dy")
@@ -187,12 +186,9 @@
     @pl.when(step == 0)
     def _():
         if edge:
-            r.acc[...] = r.acc_in[...]
-            r.proj[...] = r.proj_in[...]
             r.share32[...] = jnp.zeros_like(r.share32)
-        else:
-            r.acc[...] = jnp.zeros_like(r.acc)
-            r.proj[...] = jnp.zeros_like(r.proj)
+        r.acc[...] = jnp.zeros_like(r.acc)
+        r.proj[...] = jnp.zeros_like(r.proj)
         r.wq[...] = r.wqkv[:, 0:C]
         r.wk[...] = r.wqkv[:, C : 2 * C]
         r.wv[...] = r.wqkv[:, 2 * C : 3 * C]
@@ -379,7 +375,7 @@
     events = [(0, 2, widen(bands[0])), (0, 3, bias_rows(0, bands[0]))]
     events += [(1, 2, widen(w)) for w in bands[1:]]
     events += [(2, 2, bias_rows(at, bands[at])) for at in range(1, len(bands))]
-    start = [3 + STAGGER * t for t in range(count)]
+    start = [3 + (3 if edge else 2) * t for t in range(count)]
     for t in range(count):
         events.append((start[t], 1, chain(front(t), middle(t), back(t))))
         events.append((start[t] + 22, 1, sums(t)))
@@ -488,8 +484,7 @@
     if edge:
         for name, value in zip(("halo_lat", "halo_lon", "halo_corner"), halos):
             ins.append((name, value, by_level(value.shape, 1)))
-        for name, value in zip(("acc_in", "proj_in", "gbt_in"), before):
-            ins.append((name, value, by_level(value.shape, 0) if name == "gbt_in" else whole(value.shape)))
+        ins.append(("gbt_in", before, by_level(before.shape, 0)))
         share = (lons, blocks, bands, 128, 128)
         outs.append(("share_out", share, BF, by_level(share, 1)))
         scratch += [
@@ -560,20 +555,20 @@
         def put(i, tile):
             put_rows(i // 9, C // per * (i % 9), tile.astype(BF).reshape(C // per, per, 128))
 
-        small = (r.acc[0], r.acc[1], r.acc[2], r.proj[...])
+        small = (r.acc[0], r.acc[1], r.acc[2], r.proj0[...] + r.proj1[...])
         for i in range(2):
             one, two = small[2 * i], small[2 * i + 1]
             put(3 * i, one[:, :128])
             put(3 * i + 1, two[:, :128])
             put(3 * i + 2, jnp.concatenate([one[:, 128:], two[:, 128:]], axis=1))
         for i in range(12):
-            put(6 + i, r.dense[i])
+            put(6 + i, r.dense0[i] + r.dense1[i])
         first = jnp.zeros((C, C), F32)
         for i in range(3):
             first = first + r.acc[i] * r.wqkv[:, C * i : C * (i + 1)].astype(F32)
         second = jnp.zeros((C, 128), F32)
         for i in range(6):
-            second = second + r.dense[i] * r.wup[:, 128 * i : 128 * (i + 1)].astype(F32)
+            second = second + (r.dense0[i] + r.dense1[i]) * r.wup[:, 128 * i : 128 * (i + 1)].astype(F32)
         sums = [jnp.sum(part.T, axis=0, keepdims=True) for part in (first, second)]
         gains = jnp.concatenate([sums[0] / r.gains[0:1, :], sums[1] / r.gains[1:2, :], jnp.zeros((6, C), F32)], axis=0)
         wide = jnp.concatenate(
@@ -594,10 +589,12 @@
                 ins.append((name + str(part), value, by_level(value.shape, 0)))
     mask = head_mask()
     ins += [
-        ("dense", sums[0], whole(sums[0].shape)),
-        ("proj", sums[1], whole(sums[1].shape)),
-        ("mask", mask, whole(mask.shape)),
-    ] + [(name, weights[name], whole(weights[name].shape)) for name in ("wqkv", "wup", "gains")]
+        (name + str(part), value, whole(value.shape))
+        for part, both in enumerate(sums)
+        for name, value in zip(("dense", "proj"), both)
+    ]
+    ins += [("mask", mask, whole(mask.shape))]
+    ins += [(name, weights[name], whole(weights[name].shape)) for name in ("wqkv", "wup", "gains")]
     for part, count in enumerate(parts):
         shape = (blocks, count, M, C)
         for name in ("dq_out", "dk_out"):
@@ -771,14 +768,14 @@
 
 
 def sum_bias_kernel(in_ref, out_ref):
-    blocks, bands, heads, share, cells = out_ref.shape
+    blocks, heads, share, bands, cells = out_ref.shape
     for p in range(blocks):
         for w in range(bands):
             total = jnp.sum(in_ref[:, p, w].astype(F32), axis=0)
             far = total[share * heads : share * (heads + 1)]
             for e in range(heads):
                 near = total[share * e : share * (e + 1)]
-                out_ref[p, w, e] = jnp.concatenate([near, far[:, REST * e : REST * (e + 1)]], axis=1)
+                out_ref[p, e, :, w, :] = jnp.concatenate([near, far[:, REST * e : REST * (e + 1)]], axis=1)
 
 
 def sum_bias(pieces, shape):
@@ -840,8 +837,8 @@
     halos = (perm(lat_cut, "lat", -1), perm(lon_cut, "lon", -1), corner_perm(corner_cut, -1))
 
     weights = {"wqkv": w_qkv, "wp": w_proj, "wup": w_up, "wdt": w_down.T, "gains": norm_gains}
-    inner, sums = run_forward(INNER, tokens, cotangent, earth_bias, region_ids, weights)
-    edge, sums = run_forward(EDGE, tokens, cotangent, earth_bias, region_ids, weights, halos, sums, lons)
+    inner, inner_sums = run_forward(INNER, tokens, cotangent, earth_bias, region_ids, weights)
+    edge, sums = run_forward(EDGE, tokens, cotangent, earth_bias, region_ids, weights, halos, inner_sums[2], lons)
 
     shares = lax.all_to_all(sums[2], "lon", 0, 0, tiled=True)
     states = (inner, edge)
@@ -854,7 +851,7 @@
     def exchange(value):
         return lax.all_to_all(value, both, 0, 0, axis_index_groups=cores, tiled=True)
 
-    grads, keep, send = run_attention(states, sums, weights, core, devices // 2)
+    grads, keep, send = run_attention(states, (inner_sums[:2], sums[:2]), weights, core, devices // 2)
     packed = (keep.astype(F32) + other_core(send).astype(F32)).astype(BF)
     own, *sent = run_finish((INNER, EDGE), states, grads, weights, tokens.shape)
     packed, shares, own, *sent = lax.optimization_barrier((packed, shares, own, *sent))
@@ -862,13 +859,15 @@
     lat_in = perm(sent[0], "lat", 1)
     lon_in = perm(sent[1], "lon", 1)
     corner_in = corner_perm(sent[2], 1)
-    summed, lat_in, lon_in, corner_in = lax.optimization_barrier((sum_pieces(pieces), lat_in, lon_in, corner_in))
-    mine = exchange(summed).reshape(-1, 128)
+    mine = exchange(sum_pieces(pieces)).reshape(-1, 128)
+    grad_tokens = assemble(own, lat_in, lon_in, corner_in)
+    mine, grad_tokens = lax.optimization_barrier((mine, grad_tokens))
     cell_count = levels * nrows * cols * devices
     weight_grads = unpack(core, mine, other_core(mine), 1.0 / math.sqrt(cell_count))
-    bias_total = sum_bias(shares, earth_bias.shape[:3] + (M // lons, M))
+    blocks, bands = earth_bias.shape[:2]
+    bias_total = sum_bias(shares, (blocks, HEADS, M // lons, bands, M)).transpose(0, 3, 1, 2, 4)
     qkv, proj, up, down, gains = weight_grads
-    return (assemble(own, lat_in, lon_in, corner_in), qkv, proj, up, down.T, gains, bias_total)
+    return (grad_tokens, qkv, proj, up, down.T, gains, bias_total)
 
 
 def solution(mesh):

time: 120 us -> 117 us (0.975)
  starting transfers between devices: 30.1 us -> 27 us
    all_to_all x1, waiting for transfers between devices: 7.48 us -> 0.01 us  [exchange(): lax.all_to_all(value, both, 0, 0, axis_index_groups=cores, tiled=True)]
    ppermute x2, waiting for transfers between devices: 1.31 us -> 7.79 us  [corner_perm(): return lax.ppermute(value, both, pairs)]
    all_to_all x1, starting transfers between devices: 8.04 us -> 4.69 us  [exchange(): lax.all_to_all(value, both, 0, 0, axis_index_groups=cores, tiled=True)]
    ppermute x4, starting transfers between devices: 6.2 us -> 7.61 us  [perm(): return lax.ppermute(value, axis, pairs)]
  transfers between devices with their start and end apart: 10 -> 10, of which waited for: 2 -> 2; matrix products, arithmetic and copies ran while one was open for 2% -> 0% of each run, Pallas kernels for 27% -> 29%
where the time goes in v5:
time: 117 us; the launch traced here: 116 us
  Pallas kernels  58.3 us (50%)
  starting transfers between devices  27 us (23%)
  blocking collectives  20.5 us (18%)
  waiting for transfers between devices  8.7 us (7%)
    pallas_call x4, Pallas kernels, call(): pl.pallas_call(functools.partial(kernel, names, *fixed), grid=(blocks,),...  51.5 us
    all_to_all x1, blocking collectives, exchange(): lax.all_to_all(value, both, 0, 0, axis_index_groups=cores, tiled=True)  20.5 us
    ppermute x2, starting transfers between devices, corner_perm(): return lax.ppermute(value, both, pairs)  10.5 us
    ppermute x2, waiting for transfers between devices, corner_perm(): return lax.ppermute(value, both, pairs)  7.79 us
    ppermute x4, starting transfers between devices, perm(): return lax.ppermute(value, axis, pairs)  7.61 us
    all_to_all x1, starting transfers between devices, exchange(): lax.all_to_all(value, both, 0, 0, axis_index_groups=cores, tiled=True)  4.69 us
    all_to_all x1, starting transfers between devices, local(): shares = lax.all_to_all(sums[2], 'lon', 0, 0, tiled=True)  3.92 us
  transfers between devices with their start and end apart: 10, of which 2 were waited for; matrix products, arithmetic and copies ran while one was open for 0% of the time, Pallas kernels for 29%

profile of v5, /device:TPU:1, one launch (start us, length us, event | category | flops | bytes accessed | tf_op | source)
XLA Modules:
  0.0 116.2 jit_solution(15348131278521937682)
XLA Ops:
  0.6 2.3 %cut_halos.1 = (bf16[2,4,3,72,128]{4,3,2,1,0:T(8,128)(2,1)}, bf16[2,2,9,24,128]{4,3,2,1,0:T(8,128)(2,1)}, bf16[2,2,3,24,128]{4,3,2,1,0:T(8,128)(2,1)}) custom-call(s32[12]{0:T(128)} %refs_3_.3, bf16[4,12,48,192]{3,2,1,0:T(8,128)(2,1)} %refs_0_.3, bf16[4,12,48,192]{3,2,1,0:T(8,128)(2,1)} %refs_1_.3, bf16[4,12,48,192]{3,2,1,0:T(8,128)(2,1)} %refs_0_.3, ...), custom_call_target="tpu_custom_call" | custom-call | tf_op jit(solution)/shard_map/cut_halos/pallas_call | solution.py:716
  2.9 1.4 %collective-permute-start = (bf16[2,4,3,72,128]{4,3,2,1,0:T(8,128)(2,1)}, bf16[2,4,3,72,128]{4,3,2,1,0:T(8,128)(2,1)S(1)}, u32[]{:S(2)}, u32[]{:S(2)}) collective-permute-start(bf16[2,4,3,72,128]{4,3,2,1,0:T(8,128)(2,1)} %get-tuple-element.58), channel_id=1, source_target_pairs={{0,15},{1,0},{2,1},{3,2},{4,3},{5,4},{6,5},{7,6},{8,7},{9,8},{10,9... | collective-permute-start | bytes 1327112 | tf_op jit(solution)/shard_map/ppermute | solution.py:35
  4.4 9.3 %collective-permute-start.2 = (bf16[2,2,3,24,128]{4,3,2,1,0:T(8,128)(2,1)}, bf16[2,2,3,24,128]{4,3,2,1,0:T(8,128)(2,1)S(1)}, u32[]{:S(2)}, u32[]{:S(2)}) collective-permute-start(bf16[2,2,3,24,128]{4,3,2,1,0:T(8,128)(2,1)} %get-tuple-element.60), channel_id=1, source_target_pairs={{0,127},{1,112},{2,113},{3,114},{4,115},{5,116},{6,117},{7,118},{8... | collective-permute-start | bytes 221192 | tf_op jit(solution)/shard_map/ppermute | solution.py:834
  13.6 0.5 collective-permute-start.1
  14.1 13.4 %inner_windows.1 = (bf16[2,3,144,896]{3,2,1,0:T(8,128)(2,1)}, bf16[2,3,144,192]{3,2,1,0:T(8,128)(2,1)}, bf16[2,3,144,192]{3,2,1,0:T(8,128)(2,1)}, bf16[2,3,144,1...) custom-call(bf16[4,12,48,192]{3,2,1,0:T(8,128)(2,1)} %refs_0_.3, ...), custom_call_target="tpu_custom_call" | custom-call | flops 4200000000 | bytes 3000000 | tf_op jit(solution)/shard_map/inner_windows/pallas_call | solution.py:411
  27.5 0.0 collective-permute-done.2.refs_14_
  27.5 0.0 copy-start.6
  27.6 0.0 collective-permute-done.1.refs_13_
  27.6 0.0 copy-start.3
  27.6 0.0 collective-permute-done.refs_12_
  27.6 0.0 copy-start.2
  27.6 0.6 copy-done.6
  28.2 0.1 copy-done.3
  28.3 0.1 copy-done.2
  28.4 20.1 %edge_windows.1 = (bf16[2,5,144,896]{3,2,1,0:T(8,128)(2,1)}, bf16[2,5,144,192]{3,2,1,0:T(8,128)(2,1)}, bf16[2,5,144,192]{3,2,1,0:T(8,128)(2,1)}, bf16[2,5,144,19...) custom-call(bf16[4,12,48,192]{3,2,1,0:T(8,128)(2,1)} %refs_0_.3, ...), custom_call_target="tpu_custom_call" | custom-call | flops 7000000000 | bytes 5000000 | tf_op jit(solution)/shard_map/edge_windows/pallas_call | solution.py:411
  48.5 3.9 %all-to-all-start = ((bf16[8,2,2,128,128]{4,3,2,1,0:T(8,128)(2,1)}), bf16[8,2,2,128,128]{4,3,2,1,0:T(8,128)(2,1)S(1)}, u32[]{:S(2)}, u32[]{:S(2)}) async-start(bf16[8,2,2,128,128]{4,3,2,1,0:T(8,128)(2,1)} %get-tuple-element.73), calls=%async_computation | async-start | bytes 2097152 | tf_op jit(solution)/shard_map/all_to_all | solution.py:843
  52.5 10.9 %query_key_grads.1 = (bf16[2,3,144,192]{3,2,1,0:T(8,128)(2,1)}, bf16[2,3,144,192]{3,2,1,0:T(8,128)(2,1)}, bf16[2,5,144,192]{3,2,1,0:T(8,128)(2,1)}, bf16[2,5,144...) custom-call(bf16[2,3,144,896]{3,2,1,0:T(8,128)(2,1)} %get-tuple-element.53.refs_0_, ...), custom_call_target="tpu_custom_call" | custom-call | flops 4200000000 | bytes 3000000 | tf_op jit(solution)/shard_map/query_key_grads/pallas_call | solution.py:411
  63.4 0.2 collective-permute-start.3
  63.6 0.0 copy-start.1
  63.6 7.1 %token_grads.1 = (bf16[4,12,48,192]{3,2,1,0:T(8,128)(2,1)}, bf16[4,3,72,128]{3,2,1,0:T(8,128)(2,1)}, bf16[2,9,24,128]{3,2,1,0:T(8,128)(2,1)}, bf16[2,3,24,128]{3,2,1,0:T(8,128)(2,1)}) custom-call(bf16[2,3,144,192]{3,2,1,0:T(8,128)(2,1)} %get-tuple-element.57.refs_4_.refs_0_, bf16[2,3,144,192]{3,2,1,0:T(8,128)(2,1)} %get-tuple-element.74.refs_1_, ...), custom_call_target="tpu_custom_call" | custom-call | flops 1400000000 | bytes 1000000 | tf_op jit(solution)/shard_map/token_grads/pallas_call | solution.py:411
  70.7 0.0 collective-permute-done.3
  70.7 0.0 copy-done.1
  70.7 0.1 add_convert_fusion
  70.9 0.0 all-to-all-done.in_ref
  70.9 20.5 %all_to_all.15.in_ref = bf16[64,32,128]{2,1,0:T(8,128)(2,1)S(1)} all-to-all(bf16[64,32,128]{2,1,0:T(8,128)(2,1)S(1)} %add_convert_fusion), channel_id=1, replica_groups={{0,2,4,6,8,10,12,14,16,18,20,22,24,26,28,30,32,34,36,38,40,42,44,46,48,..., dimensions={0} | all-to-all | bytes 1048576 | tf_op jit(solution)/shard_map/all_to_all | solution.py:852
  91.3 0.0 copy-start.4
  91.3 0.0 copy-start.5
  91.3 0.0 copy-start.7
  91.3 0.0 copy-start
  91.3 0.9 sum_pieces.1
  92.3 4.7 %all-to-all-start.2 = ((bf16[64,32,128]{2,1,0:T(8,128)(2,1)}), bf16[64,32,128]{2,1,0:T(8,128)(2,1)S(1)}, u32[]{:S(2)}, u32[]{:S(2)}) async-start(bf16[64,32,128]{2,1,0:T(8,128)(2,1)} %sum_pieces.1), calls=%async_computation.2 | async-start | bytes 1048576 | tf_op jit(solution)/shard_map/all_to_all | solution.py:852
  96.9 0.0 copy-done.4
  97.0 3.0 %collective-permute-start.4 = (bf16[4,3,72,128]{3,2,1,0:T(8,128)(2,1)S(1)}, bf16[4,3,72,128]{3,2,1,0:T(8,128)(2,1)S(1)}, u32[]{:S(2)}, u32[]{:S(2)}) collective-permute-start(bf16[4,3,72,128]{3,2,1,0:T(8,128)(2,1)S(1)} %copy-done.4), channel_id=1, source_target_pairs={{0,1},{1,2},{2,3},{3,4},{4,5},{5,6},{6,7},{7,8},{8,9},{9,10},{10,1... | collective-permute-start | bytes 663560 | tf_op jit(solution)/shard_map/ppermute | solution.py:35
  99.9 0.0 copy-done.5
  99.9 2.7 %collective-permute-start.5 = (bf16[2,9,24,128]{3,2,1,0:T(8,128)(2,1)S(1)}, bf16[2,9,24,128]{3,2,1,0:T(8,128)(2,1)S(1)}, u32[]{:S(2)}, u32[]{:S(2)}) collective-permute-start(bf16[2,9,24,128]{3,2,1,0:T(8,128)(2,1)S(1)} %copy-done.5), channel_id=1, source_target_pairs={{0,16},{16,32},{32,48},{48,64},{64,80},{80,96},{96,112},{112,0},{1... | collective-permute-start | bytes 331784 | tf_op jit(solution)/shard_map/ppermute | solution.py:35
  102.6 0.0 copy-done.7
  102.6 1.3 %collective-permute-start.6 = (bf16[2,3,24,128]{3,2,1,0:T(8,128)(2,1)S(1)}, bf16[2,3,24,128]{3,2,1,0:T(8,128)(2,1)S(1)}, u32[]{:S(2)}, u32[]{:S(2)}) collective-permute-start(bf16[2,3,24,128]{3,2,1,0:T(8,128)(2,1)S(1)} %copy-done.7), channel_id=1, source_target_pairs={{0,17},{1,18},{2,19},{3,20},{4,21},{5,22},{6,23},{7,24},{8,25},{9,... | collective-permute-start | bytes 110600 | tf_op jit(solution)/shard_map/ppermute | solution.py:834
  103.9 7.8 %collective-permute-done.6.corner_ref = bf16[2,3,24,128]{3,2,1,0:T(8,128)(2,1)S(1)} collective-permute-done((bf16[2,3,24,128]{3,2,1,0:T(8,128)(2,1)S(1)}, bf16[2,3,24,128]{3,2,1,0:T(8,128)(2,1)S(1)}, u32[]{:S(2)}, u32[]{:S(2)}) %collective-permute-start.6) | collective-permute-done | bytes 36896 | tf_op jit(solution)/shard_map/ppermute | solution.py:834
  111.7 0.0 collective-permute-done.5.lon_ref
  111.7 0.0 collective-permute-done.4.lat_ref
  111.7 0.0 copy-done
  111.7 1.1 assemble.1
  112.9 0.0 all-to-all-done.2
  112.9 0.0 collective-permute-start.7
  112.9 1.0 sum_bias.1
  113.9 0.9 collective-permute-done.7.theirs_ref
  114.8 1.4 %unpack_sums.1 = (f32[192,576]{1,0:T(8,128)}, f32[192,192]{1,0:T(8,128)}, f32[192,768]{1,0:T(8,128)}, f32[192,768]{1,0:T(8,128)}, f32[2,192]{1,0:T(2,128)}) custom-call(s32[1]{0:T(128)} %bitcast.1.refs_18_.core_ref, bf16[2048,128]{1,0:T(8,128)(2,1)S(1)} %bitcast.6, bf16[2048,128]{1,0:T(8,128)(2,1)S(1)} %collective-permute-done.7.theirs_ref), custom_call_target="tpu_custom_call" | custom-call | tf_op jit(solution)/shard_map/unpack_sums/pallas_call | solution.py:812
Async XLA Ops:
  2.9 24.6 %collective-permute-start = (bf16[2,4,3,72,128]{4,3,2,1,0:T(8,128)(2,1)}, bf16[2,4,3,72,128]{4,3,2,1,0:T(8,128)(2,1)S(1)}, u32[]{:S(2)}, u32[]{:S(2)}) collective-permute-start(bf16[2,4,3,72,128]{4,3,2,1,0:T(8,128)(2,1)} %get-tuple-element.58), channel_id=1, source_target_pairs={{0,15},{1,0},{2,1},{3,2},{4,3},{5,4},{6,5},{7,6},{8,7},{9,8},{10,9... | collective-permute-start | bytes 1327112 | tf_op jit(solution)/shard_map/ppermute | solution.py:35
  4.4 23.2 %collective-permute-start.2 = (bf16[2,2,3,24,128]{4,3,2,1,0:T(8,128)(2,1)}, bf16[2,2,3,24,128]{4,3,2,1,0:T(8,128)(2,1)S(1)}, u32[]{:S(2)}, u32[]{:S(2)}) collective-permute-start(bf16[2,2,3,24,128]{4,3,2,1,0:T(8,128)(2,1)} %get-tuple-element.60), channel_id=1, source_target_pairs={{0,127},{1,112},{2,113},{3,114},{4,115},{5,116},{6,117},{7,118},{8... | collective-permute-start | bytes 221192 | tf_op jit(solution)/shard_map/ppermute | solution.py:834
  13.6 13.9 %collective-permute-start.1 = (bf16[2,2,9,24,128]{4,3,2,1,0:T(8,128)(2,1)}, bf16[2,2,9,24,128]{4,3,2,1,0:T(8,128)(2,1)S(1)}, u32[]{:S(2)}, u32[]{:S(2)}) collective-permute-start(bf16[2,2,9,24,128]{4,3,2,1,0:T(8,128)(2,1)} %get-tuple-element.59), channel_id=1, source_target_pairs={{0,112},{16,0},{32,16},{48,32},{64,48},{80,64},{96,80},{112,96},{1... | collective-permute-start | bytes 663560 | tf_op jit(solution)/shard_map/ppermute | solution.py:35
  27.5 0.6 copy-start.6
  27.6 0.7 copy-start.3
  27.6 0.8 copy-start.2
  48.5 22.3 %all-to-all-start = ((bf16[8,2,2,128,128]{4,3,2,1,0:T(8,128)(2,1)}), bf16[8,2,2,128,128]{4,3,2,1,0:T(8,128)(2,1)S(1)}, u32[]{:S(2)}, u32[]{:S(2)}) async-start(bf16[8,2,2,128,128]{4,3,2,1,0:T(8,128)(2,1)} %get-tuple-element.73), calls=%async_computation | async-start | bytes 2097152 | tf_op jit(solution)/shard_map/all_to_all | solution.py:843
  63.4 7.3 %collective-permute-start.3 = (bf16[64,32,128]{2,1,0:T(8,128)(2,1)}, bf16[64,32,128]{2,1,0:T(8,128)(2,1)S(1)}, u32[]{:S(2)}, u32[]{:S(2)}) collective-permute-start(bf16[64,32,128]{2,1,0:T(8,128)(2,1)} %get-tuple-element.72), channel_id=1, source_target_pairs={{0,1},{1,0},{2,3},{3,2},{4,5},{5,4},{6,7},{7,6},{8,9},{9,8},{10,11... | collective-permute-start | bytes 1572872 | tf_op jit(solution)/shard_map/ppermute | solution.py:849
  63.6 7.1 %copy-start.1 = (bf16[64,32,128]{2,1,0:T(8,128)(2,1)S(1)}, bf16[64,32,128]{2,1,0:T(8,128)(2,1)}, u32[]{:S(2)}) copy-start(bf16[64,32,128]{2,1,0:T(8,128)(2,1)} %get-tuple-element.71) | copy-start | bytes 1572868
  91.3 5.6 %copy-start.4 = (bf16[4,3,72,128]{3,2,1,0:T(8,128)(2,1)S(1)}, bf16[4,3,72,128]{3,2,1,0:T(8,128)(2,1)}, u32[]{:S(2)}) copy-start(bf16[4,3,72,128]{3,2,1,0:T(8,128)(2,1)} %get-tuple-element.88) | copy-start | bytes 663556
  91.3 8.6 %copy-start.5 = (bf16[2,9,24,128]{3,2,1,0:T(8,128)(2,1)S(1)}, bf16[2,9,24,128]{3,2,1,0:T(8,128)(2,1)}, u32[]{:S(2)}) copy-start(bf16[2,9,24,128]{3,2,1,0:T(8,128)(2,1)} %get-tuple-element.89) | copy-start | bytes 331780
  91.3 11.3 %copy-start.7 = (bf16[2,3,24,128]{3,2,1,0:T(8,128)(2,1)S(1)}, bf16[2,3,24,128]{3,2,1,0:T(8,128)(2,1)}, u32[]{:S(2)}) copy-start(bf16[2,3,24,128]{3,2,1,0:T(8,128)(2,1)} %get-tuple-element.90) | copy-start | bytes 110596
  91.3 20.4 %copy-start = (bf16[4,12,48,192]{3,2,1,0:T(8,128)(2,1)S(1)}, bf16[4,12,48,192]{3,2,1,0:T(8,128)(2,1)}, u32[]{:S(2)}) copy-start(bf16[4,12,48,192]{3,2,1,0:T(8,128)(2,1)} %get-tuple-element.87.own_ref) | copy-start | bytes 2654212
  92.3 20.6 %all-to-all-start.2 = ((bf16[64,32,128]{2,1,0:T(8,128)(2,1)}), bf16[64,32,128]{2,1,0:T(8,128)(2,1)S(1)}, u32[]{:S(2)}, u32[]{:S(2)}) async-start(bf16[64,32,128]{2,1,0:T(8,128)(2,1)} %sum_pieces.1), calls=%async_computation.2 | async-start | bytes 1048576 | tf_op jit(solution)/shard_map/all_to_all | solution.py:852
  97.0 14.7 %collective-permute-start.4 = (bf16[4,3,72,128]{3,2,1,0:T(8,128)(2,1)S(1)}, bf16[4,3,72,128]{3,2,1,0:T(8,128)(2,1)S(1)}, u32[]{:S(2)}, u32[]{:S(2)}) collective-permute-start(bf16[4,3,72,128]{3,2,1,0:T(8,128)(2,1)S(1)} %copy-done.4), channel_id=1, source_target_pairs={{0,1},{1,2},{2,3},{3,4},{4,5},{5,6},{6,7},{7,8},{8,9},{9,10},{10,1... | collective-permute-start | bytes 663560 | tf_op jit(solution)/shard_map/ppermute | solution.py:35
  99.9 11.8 %collective-permute-start.5 = (bf16[2,9,24,128]{3,2,1,0:T(8,128)(2,1)S(1)}, bf16[2,9,24,128]{3,2,1,0:T(8,128)(2,1)S(1)}, u32[]{:S(2)}, u32[]{:S(2)}) collective-permute-start(bf16[2,9,24,128]{3,2,1,0:T(8,128)(2,1)S(1)} %copy-done.5), channel_id=1, source_target_pairs={{0,16},{16,32},{32,48},{48,64},{64,80},{80,96},{96,112},{112,0},{1... | collective-permute-start | bytes 331784 | tf_op jit(solution)/shard_map/ppermute | solution.py:35
  102.6 9.1 %collective-permute-start.6 = (bf16[2,3,24,128]{3,2,1,0:T(8,128)(2,1)S(1)}, bf16[2,3,24,128]{3,2,1,0:T(8,128)(2,1)S(1)}, u32[]{:S(2)}, u32[]{:S(2)}) collective-permute-start(bf16[2,3,24,128]{3,2,1,0:T(8,128)(2,1)S(1)} %copy-done.7), channel_id=1, source_target_pairs={{0,17},{1,18},{2,19},{3,20},{4,21},{5,22},{6,23},{7,24},{8,25},{9,... | collective-permute-start | bytes 110600 | tf_op jit(solution)/shard_map/ppermute | solution.py:834
  112.9 1.9 %collective-permute-start.7 = (bf16[2048,128]{1,0:T(8,128)(2,1)S(1)}, bf16[2048,128]{1,0:T(8,128)(2,1)S(1)}, u32[]{:S(2)}, u32[]{:S(2)}) collective-permute-start(bf16[2048,128]{1,0:T(8,128)(2,1)S(1)} %bitcast.5), channel_id=1, source_target_pairs={{0,1},{1,0},{2,3},{3,2},{4,5},{5,4},{6,7},{7,6},{8,9},{9,8},{10,11... | collective-permute-start | bytes 1572872 | tf_op jit(solution)/shard_map/ppermute | solution.py:849

commit v6 on v5

--- a/solution.py
+++ b/solution.py
@@ -854,12 +854,13 @@
     grads, keep, send = run_attention(states, (inner_sums[:2], sums[:2]), weights, core, devices // 2)
     packed = (keep.astype(F32) + other_core(send).astype(F32)).astype(BF)
     own, *sent = run_finish((INNER, EDGE), states, grads, weights, tokens.shape)
-    packed, shares, own, *sent = lax.optimization_barrier((packed, shares, own, *sent))
+    packed, shares = lax.optimization_barrier((packed, shares))
     pieces = exchange(packed)
     lat_in = perm(sent[0], "lat", 1)
     lon_in = perm(sent[1], "lon", 1)
     corner_in = corner_perm(sent[2], 1)
-    mine = exchange(sum_pieces(pieces)).reshape(-1, 128)
+    summed, own = lax.optimization_barrier((sum_pieces(pieces), own))
+    mine = exchange(summed).reshape(-1, 128)
     grad_tokens = assemble(own, lat_in, lon_in, corner_in)
     mine, grad_tokens = lax.optimization_barrier((mine, grad_tokens))
     cell_count = levels * nrows * cols * devices

time: 117 us -> 113 us (0.966)
  blocking collectives: 20.5 us -> 0 us
  waiting for transfers between devices: 8.7 us -> 17.5 us
  starting transfers between devices: 27 us -> 33.1 us
  other arithmetic: 0.14 us -> 1.97 us
    all_to_all x1 -> x0, blocking collectives: 20.5 us -> none  [exchange(): lax.all_to_all(value, both, 0, 0, axis_index_groups=cores, tiled=True)]
    all_to_all x1 -> x2, starting transfers between devices: 4.69 us -> 10.4 us  [exchange(): lax.all_to_all(value, both, 0, 0, axis_index_groups=cores, tiled=True)]
    all_to_all x1 -> x2, waiting for transfers between devices: 0.01 us -> 5.15 us  [exchange(): lax.all_to_all(value, both, 0, 0, axis_index_groups=cores, tiled=True)]
    all_to_all x1, waiting for transfers between devices: 0.01 us -> 2.09 us  [local(): shares = lax.all_to_all(sums[2], 'lon', 0, 0, tiled=True)]
    ppermute x2, waiting for transfers between devices: 0.89 us -> 2.85 us  [other_core(): return lax.ppermute(value, 'lat', [(i, i ^ 1) for i in range(lats)])]
    convert_element_type x1, other arithmetic: 0.14 us -> 1.97 us  [local(): packed = (keep.astype(F32) + other_core(send).astype(F32)).astype(BF)]
  transfers between devices with their start and end apart: 10 -> 11, of which waited for: 2 -> 5; matrix products, arithmetic and copies ran while one was open for 0% -> 2% of each run, Pallas kernels for 29% -> 30%
where the time goes in v6:
time: 113 us; the launch traced here: 112 us
  Pallas kernels  58.2 us (52%)
  starting transfers between devices  33.1 us (29%)
  waiting for transfers between devices  17.5 us (15%)
  other arithmetic  1.97 us (2%)
    pallas_call x4, Pallas kernels, call(): pl.pallas_call(functools.partial(kernel, names, *fixed), grid=(blocks,),...  51.4 us
    ppermute x2, starting transfers between devices, corner_perm(): return lax.ppermute(value, both, pairs)  10.5 us
    all_to_all x2, starting transfers between devices, exchange(): lax.all_to_all(value, both, 0, 0, axis_index_groups=cores, tiled=True)  10.4 us
    ppermute x4, starting transfers between devices, perm(): return lax.ppermute(value, axis, pairs)  8 us
    ppermute x2, waiting for transfers between devices, corner_perm(): return lax.ppermute(value, both, pairs)  7.41 us
    all_to_all x2, waiting for transfers between devices, exchange(): lax.all_to_all(value, both, 0, 0, axis_index_groups=cores, tiled=True)  5.15 us
    all_to_all x1, starting transfers between devices, local(): shares = lax.all_to_all(sums[2], 'lon', 0, 0, tiled=True)  3.92 us
    ppermute x2, waiting for transfers between devices, other_core(): return lax.ppermute(value, 'lat', [(i, i ^ 1) for i in range(lats)])  2.85 us
  transfers between devices with their start and end apart: 11, of which 5 were waited for; matrix products, arithmetic and copies ran while one was open for 2% of the time, Pallas kernels for 30%

profile of v6, /device:TPU:1, one launch (start us, length us, event | category | flops | bytes accessed | tf_op | source)
XLA Modules:
  0.0 112.5 jit_solution(7581141096023935145)
XLA Ops:
  0.6 2.3 %cut_halos.1 = (bf16[2,4,3,72,128]{4,3,2,1,0:T(8,128)(2,1)}, bf16[2,2,9,24,128]{4,3,2,1,0:T(8,128)(2,1)}, bf16[2,2,3,24,128]{4,3,2,1,0:T(8,128)(2,1)}) custom-call(s32[12]{0:T(128)} %refs_3_.3, bf16[4,12,48,192]{3,2,1,0:T(8,128)(2,1)} %refs_0_.3, bf16[4,12,48,192]{3,2,1,0:T(8,128)(2,1)} %refs_1_.3, bf16[4,12,48,192]{3,2,1,0:T(8,128)(2,1)} %refs_0_.3, ...), custom_call_target="tpu_custom_call" | custom-call | tf_op jit(solution)/shard_map/cut_halos/pallas_call | solution.py:716
  2.9 1.4 %collective-permute-start = (bf16[2,4,3,72,128]{4,3,2,1,0:T(8,128)(2,1)}, bf16[2,4,3,72,128]{4,3,2,1,0:T(8,128)(2,1)S(1)}, u32[]{:S(2)}, u32[]{:S(2)}) collective-permute-start(bf16[2,4,3,72,128]{4,3,2,1,0:T(8,128)(2,1)} %get-tuple-element.56), channel_id=1, source_target_pairs={{0,15},{1,0},{2,1},{3,2},{4,3},{5,4},{6,5},{7,6},{8,7},{9,8},{10,9... | collective-permute-start | bytes 1327112 | tf_op jit(solution)/shard_map/ppermute | solution.py:35
  4.4 9.3 %collective-permute-start.2 = (bf16[2,2,3,24,128]{4,3,2,1,0:T(8,128)(2,1)}, bf16[2,2,3,24,128]{4,3,2,1,0:T(8,128)(2,1)S(1)}, u32[]{:S(2)}, u32[]{:S(2)}) collective-permute-start(bf16[2,2,3,24,128]{4,3,2,1,0:T(8,128)(2,1)} %get-tuple-element.58), channel_id=1, source_target_pairs={{0,127},{1,112},{2,113},{3,114},{4,115},{5,116},{6,117},{7,118},{8... | collective-permute-start | bytes 221192 | tf_op jit(solution)/shard_map/ppermute | solution.py:834
  13.6 0.5 collective-permute-start.1
  14.2 13.4 %inner_windows.1 = (bf16[2,3,144,896]{3,2,1,0:T(8,128)(2,1)}, bf16[2,3,144,192]{3,2,1,0:T(8,128)(2,1)}, bf16[2,3,144,192]{3,2,1,0:T(8,128)(2,1)}, bf16[2,3,144,1...) custom-call(bf16[4,12,48,192]{3,2,1,0:T(8,128)(2,1)} %refs_0_.3, ...), custom_call_target="tpu_custom_call" | custom-call | flops 4200000000 | bytes 3000000 | tf_op jit(solution)/shard_map/inner_windows/pallas_call | solution.py:411
  27.6 0.0 collective-permute-done.2.refs_14_
  27.6 0.0 copy-start.5
  27.6 0.0 collective-permute-done.1.refs_13_
  27.6 0.0 copy-start.2
  27.6 0.0 collective-permute-done.refs_12_
  27.6 0.0 copy-start.1
  27.6 0.6 copy-done.5
  28.2 0.1 copy-done.2
  28.3 0.1 copy-done.1
  28.4 20.1 %edge_windows.1 = (bf16[2,5,144,896]{3,2,1,0:T(8,128)(2,1)}, bf16[2,5,144,192]{3,2,1,0:T(8,128)(2,1)}, bf16[2,5,144,192]{3,2,1,0:T(8,128)(2,1)}, bf16[2,5,144,19...) custom-call(bf16[4,12,48,192]{3,2,1,0:T(8,128)(2,1)} %refs_0_.3, ...), custom_call_target="tpu_custom_call" | custom-call | flops 7000000000 | bytes 5000000 | tf_op jit(solution)/shard_map/edge_windows/pallas_call | solution.py:411
  48.5 3.9 %all-to-all-start = ((bf16[8,2,2,128,128]{4,3,2,1,0:T(8,128)(2,1)}), bf16[8,2,2,128,128]{4,3,2,1,0:T(8,128)(2,1)S(1)}, u32[]{:S(2)}, u32[]{:S(2)}) async-start(bf16[8,2,2,128,128]{4,3,2,1,0:T(8,128)(2,1)} %get-tuple-element.71), calls=%async_computation | async-start | bytes 2097152 | tf_op jit(solution)/shard_map/all_to_all | solution.py:843
  52.4 10.9 %query_key_grads.1 = (bf16[2,3,144,192]{3,2,1,0:T(8,128)(2,1)}, bf16[2,3,144,192]{3,2,1,0:T(8,128)(2,1)}, bf16[2,5,144,192]{3,2,1,0:T(8,128)(2,1)}, bf16[2,5,144...) custom-call(bf16[2,3,144,896]{3,2,1,0:T(8,128)(2,1)} %get-tuple-element.51.refs_0_, ...), custom_call_target="tpu_custom_call" | custom-call | flops 4200000000 | bytes 3000000 | tf_op jit(solution)/shard_map/query_key_grads/pallas_call | solution.py:411
  63.4 0.2 collective-permute-start.3
  63.6 2.0 %collective-permute-done.3 = bf16[64,32,128]{2,1,0:T(8,128)(2,1)S(1)} collective-permute-done((bf16[64,32,128]{2,1,0:T(8,128)(2,1)}, bf16[64,32,128]{2,1,0:T(8,128)(2,1)S(1)}, u32[]{:S(2)}, u32[]{:S(2)}) %collective-permute-start.3) | collective-permute-done | bytes 524320 | tf_op jit(solution)/shard_map/ppermute | solution.py:849
  65.6 2.0 %add_convert_fusion = bf16[64,32,128]{2,1,0:T(8,128)(2,1)} fusion(bf16[64,32,128]{2,1,0:T(8,128)(2,1)S(1)} %collective-permute-done.3, bf16[64,32,128]{2,1,0:T(8,128)(2,1)} %get-tuple-element.69), kind=kLoop, calls=%fused_computation | loop fusion | flops 1048576 | bytes 1572864 | tf_op jit(solution)/shard_map/convert_element_type | solution.py:855
  67.5 2.1 %all-to-all-done.in_ref = bf16[8,2,2,128,128]{4,3,2,1,0:T(8,128)(2,1)S(1)} async-done(((bf16[8,2,2,128,128]{4,3,2,1,0:T(8,128)(2,1)}), bf16[8,2,2,128,128]{4,3,2,1,0:T(8,128)(2,1)S(1)}, u32[]{:S(2)}, u32[]{:S(2)}) %all-to-all-start) | async-done | bytes 1048608 | tf_op jit(solution)/shard_map/all_to_all | solution.py:843
  69.6 5.7 %all-to-all-start.1 = ((bf16[64,32,128]{2,1,0:T(8,128)(2,1)}), bf16[64,32,128]{2,1,0:T(8,128)(2,1)S(1)}, u32[]{:S(2)}, u32[]{:S(2)}) async-start(bf16[64,32,128]{2,1,0:T(8,128)(2,1)} %add_convert_fusion), calls=%async_computation.1 | async-start | bytes 1048576 | tf_op jit(solution)/shard_map/all_to_all | solution.py:852
  75.4 7.0 %token_grads.1 = (bf16[4,12,48,192]{3,2,1,0:T(8,128)(2,1)}, bf16[4,3,72,128]{3,2,1,0:T(8,128)(2,1)}, bf16[2,9,24,128]{3,2,1,0:T(8,128)(2,1)}, bf16[2,3,24,128]{3,2,1,0:T(8,128)(2,1)}) custom-call(bf16[2,3,144,192]{3,2,1,0:T(8,128)(2,1)} %get-tuple-element.55.refs_4_.refs_0_, bf16[2,3,144,192]{3,2,1,0:T(8,128)(2,1)} %get-tuple-element.73.refs_1_, ...), custom_call_target="tpu_custom_call" | custom-call | flops 1400000000 | bytes 1000000 | tf_op jit(solution)/shard_map/token_grads/pallas_call | solution.py:411
  82.4 0.0 copy-start.3
  82.4 0.0 copy-start.4
  82.4 0.0 copy-start.6
  82.5 0.0 copy-start
  82.5 5.1 %all-to-all-done.1.in_ref = bf16[64,32,128]{2,1,0:T(8,128)(2,1)S(1)} async-done(((bf16[64,32,128]{2,1,0:T(8,128)(2,1)}), bf16[64,32,128]{2,1,0:T(8,128)(2,1)S(1)}, u32[]{:S(2)}, u32[]{:S(2)}) %all-to-all-start.1) | async-done | bytes 524320 | tf_op jit(solution)/shard_map/all_to_all | solution.py:852
  87.6 0.9 sum_pieces.1
  88.5 4.7 %all-to-all-start.2 = ((bf16[64,32,128]{2,1,0:T(8,128)(2,1)}), bf16[64,32,128]{2,1,0:T(8,128)(2,1)S(1)}, u32[]{:S(2)}, u32[]{:S(2)}) async-start(bf16[64,32,128]{2,1,0:T(8,128)(2,1)} %sum_pieces.1), calls=%async_computation.2 | async-start | bytes 1048576 | tf_op jit(solution)/shard_map/all_to_all | solution.py:852
  93.2 0.0 copy-done.3
  93.2 3.4 %collective-permute-start.4 = (bf16[4,3,72,128]{3,2,1,0:T(8,128)(2,1)S(1)}, bf16[4,3,72,128]{3,2,1,0:T(8,128)(2,1)S(1)}, u32[]{:S(2)}, u32[]{:S(2)}) collective-permute-start(bf16[4,3,72,128]{3,2,1,0:T(8,128)(2,1)S(1)} %copy-done.3), channel_id=1, source_target_pairs={{0,1},{1,2},{2,3},{3,4},{4,5},{5,6},{6,7},{7,8},{8,9},{9,10},{10,1... | collective-permute-start | bytes 663560 | tf_op jit(solution)/shard_map/ppermute | solution.py:35
  96.6 0.0 copy-done.4
  96.6 2.7 %collective-permute-start.5 = (bf16[2,9,24,128]{3,2,1,0:T(8,128)(2,1)S(1)}, bf16[2,9,24,128]{3,2,1,0:T(8,128)(2,1)S(1)}, u32[]{:S(2)}, u32[]{:S(2)}) collective-permute-start(bf16[2,9,24,128]{3,2,1,0:T(8,128)(2,1)S(1)} %copy-done.4), channel_id=1, source_target_pairs={{0,16},{16,32},{32,48},{48,64},{64,80},{80,96},{96,112},{112,0},{1... | collective-permute-start | bytes 331784 | tf_op jit(solution)/shard_map/ppermute | solution.py:35
  99.3 0.0 copy-done.6
  99.3 1.3 %collective-permute-start.6 = (bf16[2,3,24,128]{3,2,1,0:T(8,128)(2,1)S(1)}, bf16[2,3,24,128]{3,2,1,0:T(8,128)(2,1)S(1)}, u32[]{:S(2)}, u32[]{:S(2)}) collective-permute-start(bf16[2,3,24,128]{3,2,1,0:T(8,128)(2,1)S(1)} %copy-done.6), channel_id=1, source_target_pairs={{0,17},{1,18},{2,19},{3,20},{4,21},{5,22},{6,23},{7,24},{8,25},{9,... | collective-permute-start | bytes 110600 | tf_op jit(solution)/shard_map/ppermute | solution.py:834
  100.6 7.4 %collective-permute-done.6.corner_ref = bf16[2,3,24,128]{3,2,1,0:T(8,128)(2,1)S(1)} collective-permute-done((bf16[2,3,24,128]{3,2,1,0:T(8,128)(2,1)S(1)}, bf16[2,3,24,128]{3,2,1,0:T(8,128)(2,1)S(1)}, u32[]{:S(2)}, u32[]{:S(2)}) %collective-permute-start.6) | collective-permute-done | bytes 36896 | tf_op jit(solution)/shard_map/ppermute | solution.py:834
  108.0 0.0 collective-permute-done.5.lon_ref
  108.0 0.0 collective-permute-done.4.lat_ref
  108.0 0.0 copy-done
  108.0 1.1 %assemble.1 = bf16[4,12,48,192]{3,2,1,0:T(8,128)(2,1)} custom-call(bf16[4,12,48,192]{3,2,1,0:T(8,128)(2,1)S(1)} %copy-done, bf16[4,3,72,128]{3,2,1,0:T(8,128)(2,1)S(1)} %collective-permute-done.4.lat_ref, bf16[2,9,24,128]{3,2,1,0:T(8,128)(2,1)S(1)} %collective-permute-done.5.lon_ref, bf16[2,3,24,128]{3,2,1,0:T(8,128)(2,1)S(1)} %collective-permute-done.6.corner_ref), custom_call_target="tpu_custom_call" | custom-call | tf_op jit(solution)/shard_map/assemble/pallas_call | solution.py:748
  109.1 0.0 all-to-all-done.2
  109.1 0.0 collective-permute-start.7
  109.1 1.0 sum_bias.1
  110.2 0.9 collective-permute-done.7.theirs_ref
  111.0 1.4 %unpack_sums.1 = (f32[192,576]{1,0:T(8,128)}, f32[192,192]{1,0:T(8,128)}, f32[192,768]{1,0:T(8,128)}, f32[192,768]{1,0:T(8,128)}, f32[2,192]{1,0:T(2,128)}) custom-call(s32[1]{0:T(128)} %bitcast.1.refs_18_.core_ref, bf16[2048,128]{1,0:T(8,128)(2,1)S(1)} %bitcast.6, bf16[2048,128]{1,0:T(8,128)(2,1)S(1)} %collective-permute-done.7.theirs_ref), custom_call_target="tpu_custom_call" | custom-call | tf_op jit(solution)/shard_map/unpack_sums/pallas_call | solution.py:812
Async XLA Ops:
  2.9 24.7 %collective-permute-start = (bf16[2,4,3,72,128]{4,3,2,1,0:T(8,128)(2,1)}, bf16[2,4,3,72,128]{4,3,2,1,0:T(8,128)(2,1)S(1)}, u32[]{:S(2)}, u32[]{:S(2)}) collective-permute-start(bf16[2,4,3,72,128]{4,3,2,1,0:T(8,128)(2,1)} %get-tuple-element.56), channel_id=1, source_target_pairs={{0,15},{1,0},{2,1},{3,2},{4,3},{5,4},{6,5},{7,6},{8,7},{9,8},{10,9... | collective-permute-start | bytes 1327112 | tf_op jit(solution)/shard_map/ppermute | solution.py:35
  4.4 23.2 %collective-permute-start.2 = (bf16[2,2,3,24,128]{4,3,2,1,0:T(8,128)(2,1)}, bf16[2,2,3,24,128]{4,3,2,1,0:T(8,128)(2,1)S(1)}, u32[]{:S(2)}, u32[]{:S(2)}) collective-permute-start(bf16[2,2,3,24,128]{4,3,2,1,0:T(8,128)(2,1)} %get-tuple-element.58), channel_id=1, source_target_pairs={{0,127},{1,112},{2,113},{3,114},{4,115},{5,116},{6,117},{7,118},{8... | collective-permute-start | bytes 221192 | tf_op jit(solution)/shard_map/ppermute | solution.py:834
  13.6 13.9 %collective-permute-start.1 = (bf16[2,2,9,24,128]{4,3,2,1,0:T(8,128)(2,1)}, bf16[2,2,9,24,128]{4,3,2,1,0:T(8,128)(2,1)S(1)}, u32[]{:S(2)}, u32[]{:S(2)}) collective-permute-start(bf16[2,2,9,24,128]{4,3,2,1,0:T(8,128)(2,1)} %get-tuple-element.57), channel_id=1, source_target_pairs={{0,112},{16,0},{32,16},{48,32},{64,48},{80,64},{96,80},{112,96},{1... | collective-permute-start | bytes 663560 | tf_op jit(solution)/shard_map/ppermute | solution.py:35
  27.6 0.6 copy-start.5
  27.6 0.7 copy-start.2
  27.6 0.8 copy-start.1
  48.5 21.1 %all-to-all-start = ((bf16[8,2,2,128,128]{4,3,2,1,0:T(8,128)(2,1)}), bf16[8,2,2,128,128]{4,3,2,1,0:T(8,128)(2,1)S(1)}, u32[]{:S(2)}, u32[]{:S(2)}) async-start(bf16[8,2,2,128,128]{4,3,2,1,0:T(8,128)(2,1)} %get-tuple-element.71), calls=%async_computation | async-start | bytes 2097152 | tf_op jit(solution)/shard_map/all_to_all | solution.py:843
  63.4 2.2 %collective-permute-start.3 = (bf16[64,32,128]{2,1,0:T(8,128)(2,1)}, bf16[64,32,128]{2,1,0:T(8,128)(2,1)S(1)}, u32[]{:S(2)}, u32[]{:S(2)}) collective-permute-start(bf16[64,32,128]{2,1,0:T(8,128)(2,1)} %get-tuple-element.70), channel_id=1, source_target_pairs={{0,1},{1,0},{2,3},{3,2},{4,5},{5,4},{6,7},{7,6},{8,9},{9,8},{10,11... | collective-permute-start | bytes 1572872 | tf_op jit(solution)/shard_map/ppermute | solution.py:849
  69.6 18.0 %all-to-all-start.1 = ((bf16[64,32,128]{2,1,0:T(8,128)(2,1)}), bf16[64,32,128]{2,1,0:T(8,128)(2,1)S(1)}, u32[]{:S(2)}, u32[]{:S(2)}) async-start(bf16[64,32,128]{2,1,0:T(8,128)(2,1)} %add_convert_fusion), calls=%async_computation.1 | async-start | bytes 1048576 | tf_op jit(solution)/shard_map/all_to_all | solution.py:852
  82.4 10.8 %copy-start.3 = (bf16[4,3,72,128]{3,2,1,0:T(8,128)(2,1)S(1)}, bf16[4,3,72,128]{3,2,1,0:T(8,128)(2,1)}, u32[]{:S(2)}) copy-start(bf16[4,3,72,128]{3,2,1,0:T(8,128)(2,1)} %get-tuple-element.84) | copy-start | bytes 663556
  82.4 14.2 %copy-start.4 = (bf16[2,9,24,128]{3,2,1,0:T(8,128)(2,1)S(1)}, bf16[2,9,24,128]{3,2,1,0:T(8,128)(2,1)}, u32[]{:S(2)}) copy-start(bf16[2,9,24,128]{3,2,1,0:T(8,128)(2,1)} %get-tuple-element.85) | copy-start | bytes 331780
  82.4 16.8 %copy-start.6 = (bf16[2,3,24,128]{3,2,1,0:T(8,128)(2,1)S(1)}, bf16[2,3,24,128]{3,2,1,0:T(8,128)(2,1)}, u32[]{:S(2)}) copy-start(bf16[2,3,24,128]{3,2,1,0:T(8,128)(2,1)} %get-tuple-element.86) | copy-start | bytes 110596
  82.5 25.5 %copy-start = (bf16[4,12,48,192]{3,2,1,0:T(8,128)(2,1)S(1)}, bf16[4,12,48,192]{3,2,1,0:T(8,128)(2,1)}, u32[]{:S(2)}) copy-start(bf16[4,12,48,192]{3,2,1,0:T(8,128)(2,1)} %get-tuple-element.83.own_ref) | copy-start | bytes 2654212
  88.5 20.6 %all-to-all-start.2 = ((bf16[64,32,128]{2,1,0:T(8,128)(2,1)}), bf16[64,32,128]{2,1,0:T(8,128)(2,1)S(1)}, u32[]{:S(2)}, u32[]{:S(2)}) async-start(bf16[64,32,128]{2,1,0:T(8,128)(2,1)} %sum_pieces.1), calls=%async_computation.2 | async-start | bytes 1048576 | tf_op jit(solution)/shard_map/all_to_all | solution.py:852
  93.2 14.7 %collective-permute-start.4 = (bf16[4,3,72,128]{3,2,1,0:T(8,128)(2,1)S(1)}, bf16[4,3,72,128]{3,2,1,0:T(8,128)(2,1)S(1)}, u32[]{:S(2)}, u32[]{:S(2)}) collective-permute-start(bf16[4,3,72,128]{3,2,1,0:T(8,128)(2,1)S(1)} %copy-done.3), channel_id=1, source_target_pairs={{0,1},{1,2},{2,3},{3,4},{4,5},{5,6},{6,7},{7,8},{8,9},{9,10},{10,1... | collective-permute-start | bytes 663560 | tf_op jit(solution)/shard_map/ppermute | solution.py:35
  96.6 11.4 %collective-permute-start.5 = (bf16[2,9,24,128]{3,2,1,0:T(8,128)(2,1)S(1)}, bf16[2,9,24,128]{3,2,1,0:T(8,128)(2,1)S(1)}, u32[]{:S(2)}, u32[]{:S(2)}) collective-permute-start(bf16[2,9,24,128]{3,2,1,0:T(8,128)(2,1)S(1)} %copy-done.4), channel_id=1, source_target_pairs={{0,16},{16,32},{32,48},{48,64},{64,80},{80,96},{96,112},{112,0},{1... | collective-permute-start | bytes 331784 | tf_op jit(solution)/shard_map/ppermute | solution.py:35
  99.3 8.7 %collective-permute-start.6 = (bf16[2,3,24,128]{3,2,1,0:T(8,128)(2,1)S(1)}, bf16[2,3,24,128]{3,2,1,0:T(8,128)(2,1)S(1)}, u32[]{:S(2)}, u32[]{:S(2)}) collective-permute-start(bf16[2,3,24,128]{3,2,1,0:T(8,128)(2,1)S(1)} %copy-done.6), channel_id=1, source_target_pairs={{0,17},{1,18},{2,19},{3,20},{4,21},{5,22},{6,23},{7,24},{8,25},{9,... | collective-permute-start | bytes 110600 | tf_op jit(solution)/shard_map/ppermute | solution.py:834
  109.1 1.9 %collective-permute-start.7 = (bf16[2048,128]{1,0:T(8,128)(2,1)S(1)}, bf16[2048,128]{1,0:T(8,128)(2,1)S(1)}, u32[]{:S(2)}, u32[]{:S(2)}) collective-permute-start(bf16[2048,128]{1,0:T(8,128)(2,1)S(1)} %bitcast.5), channel_id=1, source_target_pairs={{0,1},{1,0},{2,3},{3,2},{4,5},{5,4},{6,7},{7,6},{8,9},{9,8},{10,11... | collective-permute-start | bytes 1572872 | tf_op jit(solution)/shard_map/ppermute | solution.py:849

commit v7 on v6

--- a/solution.py
+++ b/solution.py
@@ -753,6 +753,19 @@
     )(own, *received)
 
 
+def add_kernel(one_ref, two_ref, out_ref):
+    out_ref[...] = (one_ref[...].astype(F32) + two_ref[...].astype(F32)).astype(BF)
+
+
+def add_halves(one, two):
+    return pl.pallas_call(
+        add_kernel,
+        out_shape=jax.ShapeDtypeStruct(one.shape, BF),
+        compiler_params=pltpu.CompilerParams(vmem_limit_bytes=32 * 1024 * 1024),
+        name="add_halves",
+    )(one, two)
+
+
 def sum_kernel(in_ref, out_ref):
     total = jnp.sum(in_ref[...].astype(F32), axis=0, keepdims=True).astype(BF)
     out_ref[...] = jnp.broadcast_to(total, out_ref.shape)
@@ -852,7 +865,7 @@
         return lax.all_to_all(value, both, 0, 0, axis_index_groups=cores, tiled=True)
 
     grads, keep, send = run_attention(states, (inner_sums[:2], sums[:2]), weights, core, devices // 2)
-    packed = (keep.astype(F32) + other_core(send).astype(F32)).astype(BF)
+    packed = add_halves(keep, other_core(send))
     own, *sent = run_finish((INNER, EDGE), states, grads, weights, tokens.shape)
     packed, shares = lax.optimization_barrier((packed, shares))
     pieces = exchange(packed)

time: 113 us -> 113 us (level)
  other arithmetic: 1.97 us -> 0 us
    convert_element_type x1 -> x0, other arithmetic: 1.97 us -> none  [local(): packed = (keep.astype(F32) + other_core(send).astype(F32)).astype(BF)]
  transfers between devices with their start and end apart: 11 -> 11, of which waited for: 5 -> 5; matrix products, arithmetic and copies ran while one was open for 2% -> 0% of each run, Pallas kernels for 30% -> 31%
where the time goes in v7:
time: 113 us; the launch traced here: 112 us
  Pallas kernels  59.1 us (52%)
  starting transfers between devices  33.1 us (29%)
  waiting for transfers between devices  17.5 us (15%)
  local copies, waits for them, and re-layouts  1.88 us (2%)
    pallas_call x4, Pallas kernels, call(): pl.pallas_call(functools.partial(kernel, names, *fixed), grid=(blocks,),...  51.4 us
    ppermute x2, starting transfers between devices, corner_perm(): return lax.ppermute(value, both, pairs)  10.5 us
    all_to_all x2, starting transfers between devices, exchange(): lax.all_to_all(value, both, 0, 0, axis_index_groups=cores, tiled=True)  10.4 us
    ppermute x4, starting transfers between devices, perm(): return lax.ppermute(value, axis, pairs)  8 us
    ppermute x2, waiting for transfers between devices, corner_perm(): return lax.ppermute(value, both, pairs)  7.41 us
    all_to_all x2, waiting for transfers between devices, exchange(): lax.all_to_all(value, both, 0, 0, axis_index_groups=cores, tiled=True)  5.15 us
    all_to_all x1, starting transfers between devices, local(): shares = lax.all_to_all(sums[2], 'lon', 0, 0, tiled=True)  3.91 us
    ppermute x2, waiting for transfers between devices, other_core(): return lax.ppermute(value, 'lat', [(i, i ^ 1) for i in range(lats)])  2.85 us
  transfers between devices with their start and end apart: 11, of which 5 were waited for; matrix products, arithmetic and copies ran while one was open for 0% of the time, Pallas kernels for 31%

profile of v7, /device:TPU:1, one launch (start us, length us, event | category | flops | bytes accessed | tf_op | source)
XLA Modules:
  0.0 112.5 jit_solution(186541127321593072)
XLA Ops:
  0.6 2.3 %cut_halos.1 = (bf16[2,4,3,72,128]{4,3,2,1,0:T(8,128)(2,1)}, bf16[2,2,9,24,128]{4,3,2,1,0:T(8,128)(2,1)}, bf16[2,2,3,24,128]{4,3,2,1,0:T(8,128)(2,1)}) custom-call(s32[12]{0:T(128)} %refs_3_.3, bf16[4,12,48,192]{3,2,1,0:T(8,128)(2,1)} %refs_0_.3, bf16[4,12,48,192]{3,2,1,0:T(8,128)(2,1)} %refs_1_.3, bf16[4,12,48,192]{3,2,1,0:T(8,128)(2,1)} %refs_0_.3, ...), custom_call_target="tpu_custom_call" | custom-call | tf_op jit(solution)/shard_map/cut_halos/pallas_call | solution.py:716
  2.9 1.4 %collective-permute-start = (bf16[2,4,3,72,128]{4,3,2,1,0:T(8,128)(2,1)}, bf16[2,4,3,72,128]{4,3,2,1,0:T(8,128)(2,1)S(1)}, u32[]{:S(2)}, u32[]{:S(2)}) collective-permute-start(bf16[2,4,3,72,128]{4,3,2,1,0:T(8,128)(2,1)} %get-tuple-element.56), channel_id=1, source_target_pairs={{0,15},{1,0},{2,1},{3,2},{4,3},{5,4},{6,5},{7,6},{8,7},{9,8},{10,9... | collective-permute-start | bytes 1327112 | tf_op jit(solution)/shard_map/ppermute | solution.py:35
  4.4 9.3 %collective-permute-start.2 = (bf16[2,2,3,24,128]{4,3,2,1,0:T(8,128)(2,1)}, bf16[2,2,3,24,128]{4,3,2,1,0:T(8,128)(2,1)S(1)}, u32[]{:S(2)}, u32[]{:S(2)}) collective-permute-start(bf16[2,2,3,24,128]{4,3,2,1,0:T(8,128)(2,1)} %get-tuple-element.58), channel_id=1, source_target_pairs={{0,127},{1,112},{2,113},{3,114},{4,115},{5,116},{6,117},{7,118},{8... | collective-permute-start | bytes 221192 | tf_op jit(solution)/shard_map/ppermute | solution.py:847
  13.6 0.5 collective-permute-start.1
  14.1 13.4 %inner_windows.1 = (bf16[2,3,144,896]{3,2,1,0:T(8,128)(2,1)}, bf16[2,3,144,192]{3,2,1,0:T(8,128)(2,1)}, bf16[2,3,144,192]{3,2,1,0:T(8,128)(2,1)}, bf16[2,3,144,1...) custom-call(bf16[4,12,48,192]{3,2,1,0:T(8,128)(2,1)} %refs_0_.3, ...), custom_call_target="tpu_custom_call" | custom-call | flops 4200000000 | bytes 3000000 | tf_op jit(solution)/shard_map/inner_windows/pallas_call | solution.py:411
  27.5 0.0 collective-permute-done.2.refs_14_
  27.5 0.0 copy-start.6
  27.6 0.0 collective-permute-done.1.refs_13_
  27.6 0.0 copy-start.3
  27.6 0.0 collective-permute-done.refs_12_
  27.6 0.0 copy-start.2
  27.6 0.6 copy-done.6
  28.2 0.1 copy-done.3
  28.3 0.1 copy-done.2
  28.4 20.1 %edge_windows.1 = (bf16[2,5,144,896]{3,2,1,0:T(8,128)(2,1)}, bf16[2,5,144,192]{3,2,1,0:T(8,128)(2,1)}, bf16[2,5,144,192]{3,2,1,0:T(8,128)(2,1)}, bf16[2,5,144,19...) custom-call(bf16[4,12,48,192]{3,2,1,0:T(8,128)(2,1)} %refs_0_.3, ...), custom_call_target="tpu_custom_call" | custom-call | flops 7000000000 | bytes 5000000 | tf_op jit(solution)/shard_map/edge_windows/pallas_call | solution.py:411
  48.5 3.9 %all-to-all-start = ((bf16[8,2,2,128,128]{4,3,2,1,0:T(8,128)(2,1)}), bf16[8,2,2,128,128]{4,3,2,1,0:T(8,128)(2,1)S(1)}, u32[]{:S(2)}, u32[]{:S(2)}) async-start(bf16[8,2,2,128,128]{4,3,2,1,0:T(8,128)(2,1)} %get-tuple-element.71), calls=%async_computation | async-start | bytes 2097152 | tf_op jit(solution)/shard_map/all_to_all | solution.py:856
  52.4 10.9 %query_key_grads.1 = (bf16[2,3,144,192]{3,2,1,0:T(8,128)(2,1)}, bf16[2,3,144,192]{3,2,1,0:T(8,128)(2,1)}, bf16[2,5,144,192]{3,2,1,0:T(8,128)(2,1)}, bf16[2,5,144...) custom-call(bf16[2,3,144,896]{3,2,1,0:T(8,128)(2,1)} %get-tuple-element.51.refs_0_, ...), custom_call_target="tpu_custom_call" | custom-call | flops 4200000000 | bytes 3000000 | tf_op jit(solution)/shard_map/query_key_grads/pallas_call | solution.py:411
  63.4 0.2 collective-permute-start.3
  63.6 2.0 %collective-permute-done.3.two_ref = bf16[64,32,128]{2,1,0:T(8,128)(2,1)S(1)} collective-permute-done((bf16[64,32,128]{2,1,0:T(8,128)(2,1)}, bf16[64,32,128]{2,1,0:T(8,128)(2,1)S(1)}, u32[]{:S(2)}, u32[]{:S(2)}) %collective-permute-start.3) | collective-permute-done | bytes 524320 | tf_op jit(solution)/shard_map/ppermute | solution.py:862
  65.6 0.0 copy-start.1
  65.6 1.0 copy-done.1
  66.6 0.9 add_halves.1
  67.5 2.1 %all-to-all-done.in_ref = bf16[8,2,2,128,128]{4,3,2,1,0:T(8,128)(2,1)S(1)} async-done(((bf16[8,2,2,128,128]{4,3,2,1,0:T(8,128)(2,1)}), bf16[8,2,2,128,128]{4,3,2,1,0:T(8,128)(2,1)S(1)}, u32[]{:S(2)}, u32[]{:S(2)}) %all-to-all-start) | async-done | bytes 1048608 | tf_op jit(solution)/shard_map/all_to_all | solution.py:856
  69.6 5.7 %all-to-all-start.1 = ((bf16[64,32,128]{2,1,0:T(8,128)(2,1)}), bf16[64,32,128]{2,1,0:T(8,128)(2,1)S(1)}, u32[]{:S(2)}, u32[]{:S(2)}) async-start(bf16[64,32,128]{2,1,0:T(8,128)(2,1)} %add_halves.1), calls=%async_computation.1 | async-start | bytes 1048576 | tf_op jit(solution)/shard_map/all_to_all | solution.py:865
  75.4 7.0 %token_grads.1 = (bf16[4,12,48,192]{3,2,1,0:T(8,128)(2,1)}, bf16[4,3,72,128]{3,2,1,0:T(8,128)(2,1)}, bf16[2,9,24,128]{3,2,1,0:T(8,128)(2,1)}, bf16[2,3,24,128]{3,2,1,0:T(8,128)(2,1)}) custom-call(bf16[2,3,144,192]{3,2,1,0:T(8,128)(2,1)} %get-tuple-element.55.refs_4_.refs_0_, bf16[2,3,144,192]{3,2,1,0:T(8,128)(2,1)} %get-tuple-element.73.refs_1_, ...), custom_call_target="tpu_custom_call" | custom-call | flops 1400000000 | bytes 1000000 | tf_op jit(solution)/shard_map/token_grads/pallas_call | solution.py:411
  82.4 0.0 copy-start.4
  82.4 0.0 copy-start.5
  82.4 0.0 copy-start.7
  82.4 0.0 copy-start
  82.5 5.1 %all-to-all-done.1.in_ref = bf16[64,32,128]{2,1,0:T(8,128)(2,1)S(1)} async-done(((bf16[64,32,128]{2,1,0:T(8,128)(2,1)}), bf16[64,32,128]{2,1,0:T(8,128)(2,1)S(1)}, u32[]{:S(2)}, u32[]{:S(2)}) %all-to-all-start.1) | async-done | bytes 524320 | tf_op jit(solution)/shard_map/all_to_all | solution.py:865
  87.6 0.9 sum_pieces.1
  88.5 4.7 %all-to-all-start.2 = ((bf16[64,32,128]{2,1,0:T(8,128)(2,1)}), bf16[64,32,128]{2,1,0:T(8,128)(2,1)S(1)}, u32[]{:S(2)}, u32[]{:S(2)}) async-start(bf16[64,32,128]{2,1,0:T(8,128)(2,1)} %sum_pieces.1), calls=%async_computation.2 | async-start | bytes 1048576 | tf_op jit(solution)/shard_map/all_to_all | solution.py:865
  93.2 0.0 copy-done.4
  93.2 3.4 %collective-permute-start.4 = (bf16[4,3,72,128]{3,2,1,0:T(8,128)(2,1)S(1)}, bf16[4,3,72,128]{3,2,1,0:T(8,128)(2,1)S(1)}, u32[]{:S(2)}, u32[]{:S(2)}) collective-permute-start(bf16[4,3,72,128]{3,2,1,0:T(8,128)(2,1)S(1)} %copy-done.4), channel_id=1, source_target_pairs={{0,1},{1,2},{2,3},{3,4},{4,5},{5,6},{6,7},{7,8},{8,9},{9,10},{10,1... | collective-permute-start | bytes 663560 | tf_op jit(solution)/shard_map/ppermute | solution.py:35
  96.6 0.0 copy-done.5
  96.6 2.7 %collective-permute-start.5 = (bf16[2,9,24,128]{3,2,1,0:T(8,128)(2,1)S(1)}, bf16[2,9,24,128]{3,2,1,0:T(8,128)(2,1)S(1)}, u32[]{:S(2)}, u32[]{:S(2)}) collective-permute-start(bf16[2,9,24,128]{3,2,1,0:T(8,128)(2,1)S(1)} %copy-done.5), channel_id=1, source_target_pairs={{0,16},{16,32},{32,48},{48,64},{64,80},{80,96},{96,112},{112,0},{1... | collective-permute-start | bytes 331784 | tf_op jit(solution)/shard_map/ppermute | solution.py:35
  99.3 0.0 copy-done.7
  99.3 1.3 %collective-permute-start.6 = (bf16[2,3,24,128]{3,2,1,0:T(8,128)(2,1)S(1)}, bf16[2,3,24,128]{3,2,1,0:T(8,128)(2,1)S(1)}, u32[]{:S(2)}, u32[]{:S(2)}) collective-permute-start(bf16[2,3,24,128]{3,2,1,0:T(8,128)(2,1)S(1)} %copy-done.7), channel_id=1, source_target_pairs={{0,17},{1,18},{2,19},{3,20},{4,21},{5,22},{6,23},{7,24},{8,25},{9,... | collective-permute-start | bytes 110600 | tf_op jit(solution)/shard_map/ppermute | solution.py:847
  100.6 7.4 %collective-permute-done.6.corner_ref = bf16[2,3,24,128]{3,2,1,0:T(8,128)(2,1)S(1)} collective-permute-done((bf16[2,3,24,128]{3,2,1,0:T(8,128)(2,1)S(1)}, bf16[2,3,24,128]{3,2,1,0:T(8,128)(2,1)S(1)}, u32[]{:S(2)}, u32[]{:S(2)}) %collective-permute-start.6) | collective-permute-done | bytes 36896 | tf_op jit(solution)/shard_map/ppermute | solution.py:847
  108.0 0.0 collective-permute-done.5.lon_ref
  108.0 0.0 collective-permute-done.4.lat_ref
  108.0 0.0 copy-done
  108.0 1.1 %assemble.1 = bf16[4,12,48,192]{3,2,1,0:T(8,128)(2,1)} custom-call(bf16[4,12,48,192]{3,2,1,0:T(8,128)(2,1)S(1)} %copy-done, bf16[4,3,72,128]{3,2,1,0:T(8,128)(2,1)S(1)} %collective-permute-done.4.lat_ref, bf16[2,9,24,128]{3,2,1,0:T(8,128)(2,1)S(1)} %collective-permute-done.5.lon_ref, bf16[2,3,24,128]{3,2,1,0:T(8,128)(2,1)S(1)} %collective-permute-done.6.corner_ref), custom_call_target="tpu_custom_call" | custom-call | tf_op jit(solution)/shard_map/assemble/pallas_call | solution.py:748
  109.1 0.0 all-to-all-done.2
  109.1 0.0 collective-permute-start.7
  109.1 1.0 sum_bias.1
  110.1 0.9 collective-permute-done.7.theirs_ref
  111.0 1.4 %unpack_sums.1 = (f32[192,576]{1,0:T(8,128)}, f32[192,192]{1,0:T(8,128)}, f32[192,768]{1,0:T(8,128)}, f32[192,768]{1,0:T(8,128)}, f32[2,192]{1,0:T(2,128)}) custom-call(s32[1]{0:T(128)} %bitcast.1.refs_18_.core_ref, bf16[2048,128]{1,0:T(8,128)(2,1)S(1)} %bitcast.6, bf16[2048,128]{1,0:T(8,128)(2,1)S(1)} %collective-permute-done.7.theirs_ref), custom_call_target="tpu_custom_call" | custom-call | tf_op jit(solution)/shard_map/unpack_sums/pallas_call | solution.py:825
Async XLA Ops:
  2.9 24.7 %collective-permute-start = (bf16[2,4,3,72,128]{4,3,2,1,0:T(8,128)(2,1)}, bf16[2,4,3,72,128]{4,3,2,1,0:T(8,128)(2,1)S(1)}, u32[]{:S(2)}, u32[]{:S(2)}) collective-permute-start(bf16[2,4,3,72,128]{4,3,2,1,0:T(8,128)(2,1)} %get-tuple-element.56), channel_id=1, source_target_pairs={{0,15},{1,0},{2,1},{3,2},{4,3},{5,4},{6,5},{7,6},{8,7},{9,8},{10,9... | collective-permute-start | bytes 1327112 | tf_op jit(solution)/shard_map/ppermute | solution.py:35
  4.4 23.2 %collective-permute-start.2 = (bf16[2,2,3,24,128]{4,3,2,1,0:T(8,128)(2,1)}, bf16[2,2,3,24,128]{4,3,2,1,0:T(8,128)(2,1)S(1)}, u32[]{:S(2)}, u32[]{:S(2)}) collective-permute-start(bf16[2,2,3,24,128]{4,3,2,1,0:T(8,128)(2,1)} %get-tuple-element.58), channel_id=1, source_target_pairs={{0,127},{1,112},{2,113},{3,114},{4,115},{5,116},{6,117},{7,118},{8... | collective-permute-start | bytes 221192 | tf_op jit(solution)/shard_map/ppermute | solution.py:847
  13.6 13.9 %collective-permute-start.1 = (bf16[2,2,9,24,128]{4,3,2,1,0:T(8,128)(2,1)}, bf16[2,2,9,24,128]{4,3,2,1,0:T(8,128)(2,1)S(1)}, u32[]{:S(2)}, u32[]{:S(2)}) collective-permute-start(bf16[2,2,9,24,128]{4,3,2,1,0:T(8,128)(2,1)} %get-tuple-element.57), channel_id=1, source_target_pairs={{0,112},{16,0},{32,16},{48,32},{64,48},{80,64},{96,80},{112,96},{1... | collective-permute-start | bytes 663560 | tf_op jit(solution)/shard_map/ppermute | solution.py:35
  27.5 0.6 copy-start.6
  27.6 0.7 copy-start.3
  27.6 0.8 copy-start.2
  48.5 21.1 %all-to-all-start = ((bf16[8,2,2,128,128]{4,3,2,1,0:T(8,128)(2,1)}), bf16[8,2,2,128,128]{4,3,2,1,0:T(8,128)(2,1)S(1)}, u32[]{:S(2)}, u32[]{:S(2)}) async-start(bf16[8,2,2,128,128]{4,3,2,1,0:T(8,128)(2,1)} %get-tuple-element.71), calls=%async_computation | async-start | bytes 2097152 | tf_op jit(solution)/shard_map/all_to_all | solution.py:856
  63.4 2.2 %collective-permute-start.3 = (bf16[64,32,128]{2,1,0:T(8,128)(2,1)}, bf16[64,32,128]{2,1,0:T(8,128)(2,1)S(1)}, u32[]{:S(2)}, u32[]{:S(2)}) collective-permute-start(bf16[64,32,128]{2,1,0:T(8,128)(2,1)} %get-tuple-element.70), channel_id=1, source_target_pairs={{0,1},{1,0},{2,3},{3,2},{4,5},{5,4},{6,7},{7,6},{8,9},{9,8},{10,11... | collective-permute-start | bytes 1572872 | tf_op jit(solution)/shard_map/ppermute | solution.py:862
  65.6 1.0 copy-start.1
  69.6 18.0 %all-to-all-start.1 = ((bf16[64,32,128]{2,1,0:T(8,128)(2,1)}), bf16[64,32,128]{2,1,0:T(8,128)(2,1)S(1)}, u32[]{:S(2)}, u32[]{:S(2)}) async-start(bf16[64,32,128]{2,1,0:T(8,128)(2,1)} %add_halves.1), calls=%async_computation.1 | async-start | bytes 1048576 | tf_op jit(solution)/shard_map/all_to_all | solution.py:865
  82.4 10.8 %copy-start.4 = (bf16[4,3,72,128]{3,2,1,0:T(8,128)(2,1)S(1)}, bf16[4,3,72,128]{3,2,1,0:T(8,128)(2,1)}, u32[]{:S(2)}) copy-start(bf16[4,3,72,128]{3,2,1,0:T(8,128)(2,1)} %get-tuple-element.84) | copy-start | bytes 663556
  82.4 14.2 %copy-start.5 = (bf16[2,9,24,128]{3,2,1,0:T(8,128)(2,1)S(1)}, bf16[2,9,24,128]{3,2,1,0:T(8,128)(2,1)}, u32[]{:S(2)}) copy-start(bf16[2,9,24,128]{3,2,1,0:T(8,128)(2,1)} %get-tuple-element.85) | copy-start | bytes 331780
  82.4 16.8 %copy-start.7 = (bf16[2,3,24,128]{3,2,1,0:T(8,128)(2,1)S(1)}, bf16[2,3,24,128]{3,2,1,0:T(8,128)(2,1)}, u32[]{:S(2)}) copy-start(bf16[2,3,24,128]{3,2,1,0:T(8,128)(2,1)} %get-tuple-element.86) | copy-start | bytes 110596
  82.4 25.5 %copy-start = (bf16[4,12,48,192]{3,2,1,0:T(8,128)(2,1)S(1)}, bf16[4,12,48,192]{3,2,1,0:T(8,128)(2,1)}, u32[]{:S(2)}) copy-start(bf16[4,12,48,192]{3,2,1,0:T(8,128)(2,1)} %get-tuple-element.83.own_ref) | copy-start | bytes 2654212
  88.5 20.6 %all-to-all-start.2 = ((bf16[64,32,128]{2,1,0:T(8,128)(2,1)}), bf16[64,32,128]{2,1,0:T(8,128)(2,1)S(1)}, u32[]{:S(2)}, u32[]{:S(2)}) async-start(bf16[64,32,128]{2,1,0:T(8,128)(2,1)} %sum_pieces.1), calls=%async_computation.2 | async-start | bytes 1048576 | tf_op jit(solution)/shard_map/all_to_all | solution.py:865
  93.2 14.7 %collective-permute-start.4 = (bf16[4,3,72,128]{3,2,1,0:T(8,128)(2,1)S(1)}, bf16[4,3,72,128]{3,2,1,0:T(8,128)(2,1)S(1)}, u32[]{:S(2)}, u32[]{:S(2)}) collective-permute-start(bf16[4,3,72,128]{3,2,1,0:T(8,128)(2,1)S(1)} %copy-done.4), channel_id=1, source_target_pairs={{0,1},{1,2},{2,3},{3,4},{4,5},{5,6},{6,7},{7,8},{8,9},{9,10},{10,1... | collective-permute-start | bytes 663560 | tf_op jit(solution)/shard_map/ppermute | solution.py:35
  96.6 11.4 %collective-permute-start.5 = (bf16[2,9,24,128]{3,2,1,0:T(8,128)(2,1)S(1)}, bf16[2,9,24,128]{3,2,1,0:T(8,128)(2,1)S(1)}, u32[]{:S(2)}, u32[]{:S(2)}) collective-permute-start(bf16[2,9,24,128]{3,2,1,0:T(8,128)(2,1)S(1)} %copy-done.5), channel_id=1, source_target_pairs={{0,16},{16,32},{32,48},{48,64},{64,80},{80,96},{96,112},{112,0},{1... | collective-permute-start | bytes 331784 | tf_op jit(solution)/shard_map/ppermute | solution.py:35
  99.3 8.7 %collective-permute-start.6 = (bf16[2,3,24,128]{3,2,1,0:T(8,128)(2,1)S(1)}, bf16[2,3,24,128]{3,2,1,0:T(8,128)(2,1)S(1)}, u32[]{:S(2)}, u32[]{:S(2)}) collective-permute-start(bf16[2,3,24,128]{3,2,1,0:T(8,128)(2,1)S(1)} %copy-done.7), channel_id=1, source_target_pairs={{0,17},{1,18},{2,19},{3,20},{4,21},{5,22},{6,23},{7,24},{8,25},{9,... | collective-permute-start | bytes 110600 | tf_op jit(solution)/shard_map/ppermute | solution.py:847
  109.1 1.9 %collective-permute-start.7 = (bf16[2048,128]{1,0:T(8,128)(2,1)S(1)}, bf16[2048,128]{1,0:T(8,128)(2,1)S(1)}, u32[]{:S(2)}, u32[]{:S(2)}) collective-permute-start(bf16[2048,128]{1,0:T(8,128)(2,1)S(1)} %bitcast.5), channel_id=1, source_target_pairs={{0,1},{1,0},{2,3},{3,2},{4,5},{5,4},{6,7},{7,6},{8,9},{9,8},{10,11... | collective-permute-start | bytes 1572872 | tf_op jit(solution)/shard_map/ppermute | solution.py:862

commit v8 on v6

--- a/solution.py
+++ b/solution.py
@@ -706,7 +706,7 @@
 def cut_halos(tokens, cotangent, region_ids):
     levels, local_rows, cols, channels = tokens.shape
     row_spec = pl.BlockSpec((levels, HALF_LAT, cols, C), lambda i: (0, 0, 0, 0))
-    col_spec = pl.BlockSpec((levels, local_rows, 16, C), lambda i: (0, 0, 0, 0))
+    col_spec = pl.BlockSpec((levels, local_rows, HALO_COLS, C), lambda i: (0, 0, 0, 0))
     blocks = levels // WLEV
     shapes = (
         (2, levels, HALF_LAT, cols * 3 // 2, 128),

time: 113 us -> 113 us (level)
  no operation moved by 1% of the time
where the time goes in v8:
time: 113 us; the launch traced here: 112 us
  Pallas kernels  58.1 us (51%)
  starting transfers between devices  33.1 us (29%)
  waiting for transfers between devices  17.5 us (15%)
  other arithmetic  1.97 us (2%)
    pallas_call x4, Pallas kernels, call(): pl.pallas_call(functools.partial(kernel, names, *fixed), grid=(blocks,),...  51.4 us
    ppermute x2, starting transfers between devices, corner_perm(): return lax.ppermute(value, both, pairs)  10.5 us
    all_to_all x2, starting transfers between devices, exchange(): lax.all_to_all(value, both, 0, 0, axis_index_groups=cores, tiled=True)  10.4 us
    ppermute x4, starting transfers between devices, perm(): return lax.ppermute(value, axis, pairs)  8 us
    ppermute x2, waiting for transfers between devices, corner_perm(): return lax.ppermute(value, both, pairs)  7.41 us
    all_to_all x2, waiting for transfers between devices, exchange(): lax.all_to_all(value, both, 0, 0, axis_index_groups=cores, tiled=True)  5.15 us
    all_to_all x1, starting transfers between devices, local(): shares = lax.all_to_all(sums[2], 'lon', 0, 0, tiled=True)  3.91 us
    ppermute x2, waiting for transfers between devices, other_core(): return lax.ppermute(value, 'lat', [(i, i ^ 1) for i in range(lats)])  2.85 us
  transfers between devices with their start and end apart: 11, of which 5 were waited for; matrix products, arithmetic and copies ran while one was open for 2% of the time, Pallas kernels for 30%

profile of v8, /device:TPU:1, one launch (start us, length us, event | category | flops | bytes accessed | tf_op | source)
XLA Modules:
  0.0 112.3 jit_solution(17671990681025495156)
XLA Ops:
  0.6 2.2 %cut_halos.1 = (bf16[2,4,3,72,128]{4,3,2,1,0:T(8,128)(2,1)}, bf16[2,2,9,24,128]{4,3,2,1,0:T(8,128)(2,1)}, bf16[2,2,3,24,128]{4,3,2,1,0:T(8,128)(2,1)}) custom-call(s32[12]{0:T(128)} %refs_3_.3, bf16[4,12,48,192]{3,2,1,0:T(8,128)(2,1)} %refs_0_.3, bf16[4,12,48,192]{3,2,1,0:T(8,128)(2,1)} %refs_1_.3, bf16[4,12,48,192]{3,2,1,0:T(8,128)(2,1)} %refs_0_.3, ...), custom_call_target="tpu_custom_call" | custom-call | tf_op jit(solution)/shard_map/cut_halos/pallas_call | solution.py:716
  2.8 1.4 %collective-permute-start = (bf16[2,4,3,72,128]{4,3,2,1,0:T(8,128)(2,1)}, bf16[2,4,3,72,128]{4,3,2,1,0:T(8,128)(2,1)S(1)}, u32[]{:S(2)}, u32[]{:S(2)}) collective-permute-start(bf16[2,4,3,72,128]{4,3,2,1,0:T(8,128)(2,1)} %get-tuple-element.56), channel_id=1, source_target_pairs={{0,15},{1,0},{2,1},{3,2},{4,3},{5,4},{6,5},{7,6},{8,7},{9,8},{10,9... | collective-permute-start | bytes 1327112 | tf_op jit(solution)/shard_map/ppermute | solution.py:35
  4.2 9.3 %collective-permute-start.2 = (bf16[2,2,3,24,128]{4,3,2,1,0:T(8,128)(2,1)}, bf16[2,2,3,24,128]{4,3,2,1,0:T(8,128)(2,1)S(1)}, u32[]{:S(2)}, u32[]{:S(2)}) collective-permute-start(bf16[2,2,3,24,128]{4,3,2,1,0:T(8,128)(2,1)} %get-tuple-element.58), channel_id=1, source_target_pairs={{0,127},{1,112},{2,113},{3,114},{4,115},{5,116},{6,117},{7,118},{8... | collective-permute-start | bytes 221192 | tf_op jit(solution)/shard_map/ppermute | solution.py:834
  13.5 0.5 collective-permute-start.1
  14.0 13.4 %inner_windows.1 = (bf16[2,3,144,896]{3,2,1,0:T(8,128)(2,1)}, bf16[2,3,144,192]{3,2,1,0:T(8,128)(2,1)}, bf16[2,3,144,192]{3,2,1,0:T(8,128)(2,1)}, bf16[2,3,144,1...) custom-call(bf16[4,12,48,192]{3,2,1,0:T(8,128)(2,1)} %refs_0_.3, ...), custom_call_target="tpu_custom_call" | custom-call | flops 4200000000 | bytes 3000000 | tf_op jit(solution)/shard_map/inner_windows/pallas_call | solution.py:411
  27.4 0.0 collective-permute-done.2.refs_14_
  27.4 0.0 copy-start.5
  27.4 0.0 collective-permute-done.1.refs_13_
  27.4 0.0 copy-start.2
  27.5 0.0 collective-permute-done.refs_12_
  27.5 0.0 copy-start.1
  27.5 0.6 copy-done.5
  28.0 0.1 copy-done.2
  28.1 0.1 copy-done.1
  28.3 20.1 %edge_windows.1 = (bf16[2,5,144,896]{3,2,1,0:T(8,128)(2,1)}, bf16[2,5,144,192]{3,2,1,0:T(8,128)(2,1)}, bf16[2,5,144,192]{3,2,1,0:T(8,128)(2,1)}, bf16[2,5,144,19...) custom-call(bf16[4,12,48,192]{3,2,1,0:T(8,128)(2,1)} %refs_0_.3, ...), custom_call_target="tpu_custom_call" | custom-call | flops 7000000000 | bytes 5000000 | tf_op jit(solution)/shard_map/edge_windows/pallas_call | solution.py:411
  48.4 3.9 %all-to-all-start = ((bf16[8,2,2,128,128]{4,3,2,1,0:T(8,128)(2,1)}), bf16[8,2,2,128,128]{4,3,2,1,0:T(8,128)(2,1)S(1)}, u32[]{:S(2)}, u32[]{:S(2)}) async-start(bf16[8,2,2,128,128]{4,3,2,1,0:T(8,128)(2,1)} %get-tuple-element.71), calls=%async_computation | async-start | bytes 2097152 | tf_op jit(solution)/shard_map/all_to_all | solution.py:843
  52.3 10.9 %query_key_grads.1 = (bf16[2,3,144,192]{3,2,1,0:T(8,128)(2,1)}, bf16[2,3,144,192]{3,2,1,0:T(8,128)(2,1)}, bf16[2,5,144,192]{3,2,1,0:T(8,128)(2,1)}, bf16[2,5,144...) custom-call(bf16[2,3,144,896]{3,2,1,0:T(8,128)(2,1)} %get-tuple-element.51.refs_0_, ...), custom_call_target="tpu_custom_call" | custom-call | flops 4200000000 | bytes 3000000 | tf_op jit(solution)/shard_map/query_key_grads/pallas_call | solution.py:411
  63.2 0.2 collective-permute-start.3
  63.5 2.0 %collective-permute-done.3 = bf16[64,32,128]{2,1,0:T(8,128)(2,1)S(1)} collective-permute-done((bf16[64,32,128]{2,1,0:T(8,128)(2,1)}, bf16[64,32,128]{2,1,0:T(8,128)(2,1)S(1)}, u32[]{:S(2)}, u32[]{:S(2)}) %collective-permute-start.3) | collective-permute-done | bytes 524320 | tf_op jit(solution)/shard_map/ppermute | solution.py:849
  65.4 2.0 %add_convert_fusion = bf16[64,32,128]{2,1,0:T(8,128)(2,1)} fusion(bf16[64,32,128]{2,1,0:T(8,128)(2,1)S(1)} %collective-permute-done.3, bf16[64,32,128]{2,1,0:T(8,128)(2,1)} %get-tuple-element.69), kind=kLoop, calls=%fused_computation | loop fusion | flops 1048576 | bytes 1572864 | tf_op jit(solution)/shard_map/convert_element_type | solution.py:855
  67.4 2.1 %all-to-all-done.in_ref = bf16[8,2,2,128,128]{4,3,2,1,0:T(8,128)(2,1)S(1)} async-done(((bf16[8,2,2,128,128]{4,3,2,1,0:T(8,128)(2,1)}), bf16[8,2,2,128,128]{4,3,2,1,0:T(8,128)(2,1)S(1)}, u32[]{:S(2)}, u32[]{:S(2)}) %all-to-all-start) | async-done | bytes 1048608 | tf_op jit(solution)/shard_map/all_to_all | solution.py:843
  69.5 5.7 %all-to-all-start.1 = ((bf16[64,32,128]{2,1,0:T(8,128)(2,1)}), bf16[64,32,128]{2,1,0:T(8,128)(2,1)S(1)}, u32[]{:S(2)}, u32[]{:S(2)}) async-start(bf16[64,32,128]{2,1,0:T(8,128)(2,1)} %add_convert_fusion), calls=%async_computation.1 | async-start | bytes 1048576 | tf_op jit(solution)/shard_map/all_to_all | solution.py:852
  75.2 7.0 %token_grads.1 = (bf16[4,12,48,192]{3,2,1,0:T(8,128)(2,1)}, bf16[4,3,72,128]{3,2,1,0:T(8,128)(2,1)}, bf16[2,9,24,128]{3,2,1,0:T(8,128)(2,1)}, bf16[2,3,24,128]{3,2,1,0:T(8,128)(2,1)}) custom-call(bf16[2,3,144,192]{3,2,1,0:T(8,128)(2,1)} %get-tuple-element.55.refs_4_.refs_0_, bf16[2,3,144,192]{3,2,1,0:T(8,128)(2,1)} %get-tuple-element.73.refs_1_, ...), custom_call_target="tpu_custom_call" | custom-call | flops 1400000000 | bytes 1000000 | tf_op jit(solution)/shard_map/token_grads/pallas_call | solution.py:411
  82.3 0.0 copy-start.3
  82.3 0.0 copy-start.4
  82.3 0.0 copy-start.6
  82.3 0.0 copy-start
  82.3 5.1 %all-to-all-done.1.in_ref = bf16[64,32,128]{2,1,0:T(8,128)(2,1)S(1)} async-done(((bf16[64,32,128]{2,1,0:T(8,128)(2,1)}), bf16[64,32,128]{2,1,0:T(8,128)(2,1)S(1)}, u32[]{:S(2)}, u32[]{:S(2)}) %all-to-all-start.1) | async-done | bytes 524320 | tf_op jit(solution)/shard_map/all_to_all | solution.py:852
  87.5 0.9 sum_pieces.1
  88.4 4.7 %all-to-all-start.2 = ((bf16[64,32,128]{2,1,0:T(8,128)(2,1)}), bf16[64,32,128]{2,1,0:T(8,128)(2,1)S(1)}, u32[]{:S(2)}, u32[]{:S(2)}) async-start(bf16[64,32,128]{2,1,0:T(8,128)(2,1)} %sum_pieces.1), calls=%async_computation.2 | async-start | bytes 1048576 | tf_op jit(solution)/shard_map/all_to_all | solution.py:852
  93.1 0.0 copy-done.3
  93.1 3.4 %collective-permute-start.4 = (bf16[4,3,72,128]{3,2,1,0:T(8,128)(2,1)S(1)}, bf16[4,3,72,128]{3,2,1,0:T(8,128)(2,1)S(1)}, u32[]{:S(2)}, u32[]{:S(2)}) collective-permute-start(bf16[4,3,72,128]{3,2,1,0:T(8,128)(2,1)S(1)} %copy-done.3), channel_id=1, source_target_pairs={{0,1},{1,2},{2,3},{3,4},{4,5},{5,6},{6,7},{7,8},{8,9},{9,10},{10,1... | collective-permute-start | bytes 663560 | tf_op jit(solution)/shard_map/ppermute | solution.py:35
  96.5 0.0 copy-done.4
  96.5 2.7 %collective-permute-start.5 = (bf16[2,9,24,128]{3,2,1,0:T(8,128)(2,1)S(1)}, bf16[2,9,24,128]{3,2,1,0:T(8,128)(2,1)S(1)}, u32[]{:S(2)}, u32[]{:S(2)}) collective-permute-start(bf16[2,9,24,128]{3,2,1,0:T(8,128)(2,1)S(1)} %copy-done.4), channel_id=1, source_target_pairs={{0,16},{16,32},{32,48},{48,64},{64,80},{80,96},{96,112},{112,0},{1... | collective-permute-start | bytes 331784 | tf_op jit(solution)/shard_map/ppermute | solution.py:35
  99.1 0.0 copy-done.6
  99.1 1.3 %collective-permute-start.6 = (bf16[2,3,24,128]{3,2,1,0:T(8,128)(2,1)S(1)}, bf16[2,3,24,128]{3,2,1,0:T(8,128)(2,1)S(1)}, u32[]{:S(2)}, u32[]{:S(2)}) collective-permute-start(bf16[2,3,24,128]{3,2,1,0:T(8,128)(2,1)S(1)} %copy-done.6), channel_id=1, source_target_pairs={{0,17},{1,18},{2,19},{3,20},{4,21},{5,22},{6,23},{7,24},{8,25},{9,... | collective-permute-start | bytes 110600 | tf_op jit(solution)/shard_map/ppermute | solution.py:834
  100.4 7.4 %collective-permute-done.6.corner_ref = bf16[2,3,24,128]{3,2,1,0:T(8,128)(2,1)S(1)} collective-permute-done((bf16[2,3,24,128]{3,2,1,0:T(8,128)(2,1)S(1)}, bf16[2,3,24,128]{3,2,1,0:T(8,128)(2,1)S(1)}, u32[]{:S(2)}, u32[]{:S(2)}) %collective-permute-start.6) | collective-permute-done | bytes 36896 | tf_op jit(solution)/shard_map/ppermute | solution.py:834
  107.8 0.0 collective-permute-done.5.lon_ref
  107.8 0.0 collective-permute-done.4.lat_ref
  107.8 0.0 copy-done
  107.8 1.1 %assemble.1 = bf16[4,12,48,192]{3,2,1,0:T(8,128)(2,1)} custom-call(bf16[4,12,48,192]{3,2,1,0:T(8,128)(2,1)S(1)} %copy-done, bf16[4,3,72,128]{3,2,1,0:T(8,128)(2,1)S(1)} %collective-permute-done.4.lat_ref, bf16[2,9,24,128]{3,2,1,0:T(8,128)(2,1)S(1)} %collective-permute-done.5.lon_ref, bf16[2,3,24,128]{3,2,1,0:T(8,128)(2,1)S(1)} %collective-permute-done.6.corner_ref), custom_call_target="tpu_custom_call" | custom-call | tf_op jit(solution)/shard_map/assemble/pallas_call | solution.py:748
  109.0 0.0 all-to-all-done.2
  109.0 0.0 collective-permute-start.7
  109.0 1.0 sum_bias.1
  110.0 0.9 collective-permute-done.7.theirs_ref
  110.9 1.4 %unpack_sums.1 = (f32[192,576]{1,0:T(8,128)}, f32[192,192]{1,0:T(8,128)}, f32[192,768]{1,0:T(8,128)}, f32[192,768]{1,0:T(8,128)}, f32[2,192]{1,0:T(2,128)}) custom-call(s32[1]{0:T(128)} %bitcast.1.refs_18_.core_ref, bf16[2048,128]{1,0:T(8,128)(2,1)S(1)} %bitcast.6, bf16[2048,128]{1,0:T(8,128)(2,1)S(1)} %collective-permute-done.7.theirs_ref), custom_call_target="tpu_custom_call" | custom-call | tf_op jit(solution)/shard_map/unpack_sums/pallas_call | solution.py:812
Async XLA Ops:
  2.8 24.7 %collective-permute-start = (bf16[2,4,3,72,128]{4,3,2,1,0:T(8,128)(2,1)}, bf16[2,4,3,72,128]{4,3,2,1,0:T(8,128)(2,1)S(1)}, u32[]{:S(2)}, u32[]{:S(2)}) collective-permute-start(bf16[2,4,3,72,128]{4,3,2,1,0:T(8,128)(2,1)} %get-tuple-element.56), channel_id=1, source_target_pairs={{0,15},{1,0},{2,1},{3,2},{4,3},{5,4},{6,5},{7,6},{8,7},{9,8},{10,9... | collective-permute-start | bytes 1327112 | tf_op jit(solution)/shard_map/ppermute | solution.py:35
  4.2 23.2 %collective-permute-start.2 = (bf16[2,2,3,24,128]{4,3,2,1,0:T(8,128)(2,1)}, bf16[2,2,3,24,128]{4,3,2,1,0:T(8,128)(2,1)S(1)}, u32[]{:S(2)}, u32[]{:S(2)}) collective-permute-start(bf16[2,2,3,24,128]{4,3,2,1,0:T(8,128)(2,1)} %get-tuple-element.58), channel_id=1, source_target_pairs={{0,127},{1,112},{2,113},{3,114},{4,115},{5,116},{6,117},{7,118},{8... | collective-permute-start | bytes 221192 | tf_op jit(solution)/shard_map/ppermute | solution.py:834
  13.5 13.9 %collective-permute-start.1 = (bf16[2,2,9,24,128]{4,3,2,1,0:T(8,128)(2,1)}, bf16[2,2,9,24,128]{4,3,2,1,0:T(8,128)(2,1)S(1)}, u32[]{:S(2)}, u32[]{:S(2)}) collective-permute-start(bf16[2,2,9,24,128]{4,3,2,1,0:T(8,128)(2,1)} %get-tuple-element.57), channel_id=1, source_target_pairs={{0,112},{16,0},{32,16},{48,32},{64,48},{80,64},{96,80},{112,96},{1... | collective-permute-start | bytes 663560 | tf_op jit(solution)/shard_map/ppermute | solution.py:35
  27.4 0.6 copy-start.5
  27.4 0.7 copy-start.2
  27.5 0.8 copy-start.1
  48.4 21.1 %all-to-all-start = ((bf16[8,2,2,128,128]{4,3,2,1,0:T(8,128)(2,1)}), bf16[8,2,2,128,128]{4,3,2,1,0:T(8,128)(2,1)S(1)}, u32[]{:S(2)}, u32[]{:S(2)}) async-start(bf16[8,2,2,128,128]{4,3,2,1,0:T(8,128)(2,1)} %get-tuple-element.71), calls=%async_computation | async-start | bytes 2097152 | tf_op jit(solution)/shard_map/all_to_all | solution.py:843
  63.2 2.2 %collective-permute-start.3 = (bf16[64,32,128]{2,1,0:T(8,128)(2,1)}, bf16[64,32,128]{2,1,0:T(8,128)(2,1)S(1)}, u32[]{:S(2)}, u32[]{:S(2)}) collective-permute-start(bf16[64,32,128]{2,1,0:T(8,128)(2,1)} %get-tuple-element.70), channel_id=1, source_target_pairs={{0,1},{1,0},{2,3},{3,2},{4,5},{5,4},{6,7},{7,6},{8,9},{9,8},{10,11... | collective-permute-start | bytes 1572872 | tf_op jit(solution)/shard_map/ppermute | solution.py:849
  69.5 18.0 %all-to-all-start.1 = ((bf16[64,32,128]{2,1,0:T(8,128)(2,1)}), bf16[64,32,128]{2,1,0:T(8,128)(2,1)S(1)}, u32[]{:S(2)}, u32[]{:S(2)}) async-start(bf16[64,32,128]{2,1,0:T(8,128)(2,1)} %add_convert_fusion), calls=%async_computation.1 | async-start | bytes 1048576 | tf_op jit(solution)/shard_map/all_to_all | solution.py:852
  82.3 10.8 %copy-start.3 = (bf16[4,3,72,128]{3,2,1,0:T(8,128)(2,1)S(1)}, bf16[4,3,72,128]{3,2,1,0:T(8,128)(2,1)}, u32[]{:S(2)}) copy-start(bf16[4,3,72,128]{3,2,1,0:T(8,128)(2,1)} %get-tuple-element.84) | copy-start | bytes 663556
  82.3 14.2 %copy-start.4 = (bf16[2,9,24,128]{3,2,1,0:T(8,128)(2,1)S(1)}, bf16[2,9,24,128]{3,2,1,0:T(8,128)(2,1)}, u32[]{:S(2)}) copy-start(bf16[2,9,24,128]{3,2,1,0:T(8,128)(2,1)} %get-tuple-element.85) | copy-start | bytes 331780
  82.3 16.8 %copy-start.6 = (bf16[2,3,24,128]{3,2,1,0:T(8,128)(2,1)S(1)}, bf16[2,3,24,128]{3,2,1,0:T(8,128)(2,1)}, u32[]{:S(2)}) copy-start(bf16[2,3,24,128]{3,2,1,0:T(8,128)(2,1)} %get-tuple-element.86) | copy-start | bytes 110596
  82.3 25.5 %copy-start = (bf16[4,12,48,192]{3,2,1,0:T(8,128)(2,1)S(1)}, bf16[4,12,48,192]{3,2,1,0:T(8,128)(2,1)}, u32[]{:S(2)}) copy-start(bf16[4,12,48,192]{3,2,1,0:T(8,128)(2,1)} %get-tuple-element.83.own_ref) | copy-start | bytes 2654212
  88.4 20.6 %all-to-all-start.2 = ((bf16[64,32,128]{2,1,0:T(8,128)(2,1)}), bf16[64,32,128]{2,1,0:T(8,128)(2,1)S(1)}, u32[]{:S(2)}, u32[]{:S(2)}) async-start(bf16[64,32,128]{2,1,0:T(8,128)(2,1)} %sum_pieces.1), calls=%async_computation.2 | async-start | bytes 1048576 | tf_op jit(solution)/shard_map/all_to_all | solution.py:852
  93.1 14.7 %collective-permute-start.4 = (bf16[4,3,72,128]{3,2,1,0:T(8,128)(2,1)S(1)}, bf16[4,3,72,128]{3,2,1,0:T(8,128)(2,1)S(1)}, u32[]{:S(2)}, u32[]{:S(2)}) collective-permute-start(bf16[4,3,72,128]{3,2,1,0:T(8,128)(2,1)S(1)} %copy-done.3), channel_id=1, source_target_pairs={{0,1},{1,2},{2,3},{3,4},{4,5},{5,6},{6,7},{7,8},{8,9},{9,10},{10,1... | collective-permute-start | bytes 663560 | tf_op jit(solution)/shard_map/ppermute | solution.py:35
  96.5 11.4 %collective-permute-start.5 = (bf16[2,9,24,128]{3,2,1,0:T(8,128)(2,1)S(1)}, bf16[2,9,24,128]{3,2,1,0:T(8,128)(2,1)S(1)}, u32[]{:S(2)}, u32[]{:S(2)}) collective-permute-start(bf16[2,9,24,128]{3,2,1,0:T(8,128)(2,1)S(1)} %copy-done.4), channel_id=1, source_target_pairs={{0,16},{16,32},{32,48},{48,64},{64,80},{80,96},{96,112},{112,0},{1... | collective-permute-start | bytes 331784 | tf_op jit(solution)/shard_map/ppermute | solution.py:35
  99.1 8.7 %collective-permute-start.6 = (bf16[2,3,24,128]{3,2,1,0:T(8,128)(2,1)S(1)}, bf16[2,3,24,128]{3,2,1,0:T(8,128)(2,1)S(1)}, u32[]{:S(2)}, u32[]{:S(2)}) collective-permute-start(bf16[2,3,24,128]{3,2,1,0:T(8,128)(2,1)S(1)} %copy-done.6), channel_id=1, source_target_pairs={{0,17},{1,18},{2,19},{3,20},{4,21},{5,22},{6,23},{7,24},{8,25},{9,... | collective-permute-start | bytes 110600 | tf_op jit(solution)/shard_map/ppermute | solution.py:834
  109.0 1.9 %collective-permute-start.7 = (bf16[2048,128]{1,0:T(8,128)(2,1)S(1)}, bf16[2048,128]{1,0:T(8,128)(2,1)S(1)}, u32[]{:S(2)}, u32[]{:S(2)}) collective-permute-start(bf16[2048,128]{1,0:T(8,128)(2,1)S(1)} %bitcast.5), channel_id=1, source_target_pairs={{0,1},{1,0},{2,3},{3,2},{4,5},{5,4},{6,7},{7,6},{8,9},{9,8},{10,11... | collective-permute-start | bytes 1572872 | tf_op jit(solution)/shard_map/ppermute | solution.py:849
